TPU v7x, 32 devices: a whole 2x2x4 slice. The times are simulated.
32 devices in a mesh: test: 4 (over y, core), src: 8 (over z, x).
Axes of the slice: x: 2, y: 2, z: 4, core: 2. Of those that a mesh axis runs over, the one named last changes fastest.
Arguments:
- test_points: float32 [8, 3, 1024], P('test'), may hold values from 0 to 1
- test_basis: bfloat16 [8, 1024, 384], P('test'), may hold values from -0.1875 to 0.1875
- test_counts: int32 [8], P('test'), may hold values from 128 to 384, as said below
- source_points: float32 [64, 3, 1024], P('src'), may hold values from 0 to 1
- source_basis: bfloat16 [64, 1024, 384], P('src', 'test'), may hold values from -0.1875 to 0.1875
- source_counts: int32 [64], P('src'), may hold values from 128 to 384, as said below
- coefficients: bfloat16 [64, 384, 512], P('src'), may hold values from -0.0546875 to 0.0546875
Outputs:
- reduced: bfloat16 [8, 384, 64, 384], P('test', 'src')
- projected: bfloat16 [8, 384, 512], P('test', 'src')
Inputs may be any that keep to these rules, and one draw needn't show every extreme that they name: `test_counts`: number of leading basis columns of a test block that are used; the rest are ignored. Some test block uses all 384 in every draw. `source_counts`: number of leading basis columns of a source block that are used; the rest are ignored. Some source block uses all 384 in every draw.
All inputs are finite; a program needn't handle non-finite values.
Results may differ from a plain program's by a relative error of at most 0.015.
Values may be sent and summed in bfloat16 or wider, within the bound.
No kernel may reach another device: no remote copies, remote signals or barrier semaphores. Data moves between devices by JAX's collectives and lax.ppermute only.
A program may use at most 128 MiB of HBM per device.

v0:
```python
import functools

import jax
import jax.numpy as jnp
from jax import lax
from jax.experimental import pallas as pl
from jax.experimental.pallas import tpu as pltpu
from jax.sharding import PartitionSpec as P

softening = 0.0025
QBLOCK = 256
LANES = 128
VMEM_LIMIT = 60 * 1024 * 1024


def exchange(x, axis, flip):
    size = lax.axis_size(axis)
    return lax.ppermute(x, axis, [(a, a ^ flip) for a in range(size)])


def bits_down(size):
    bit = size // 2
    while bit >= 1:
        yield bit
        bit //= 2


def sum_rows(total, axis):
    size = lax.axis_size(axis)
    me = lax.axis_index(axis)
    held, bit = total, 1
    while held.shape[0] > 4:
        pairs = held.reshape((held.shape[0] // 2, 2) + held.shape[1:])
        mine = (me // bit) % 2
        keep = lax.dynamic_index_in_dim(pairs, mine, 1, keepdims=False)
        give = lax.dynamic_index_in_dim(pairs, 1 - mine, 1, keepdims=False)
        got = exchange(give, axis, bit)
        held = (keep.astype(jnp.float32) + got.astype(jnp.float32)).astype(held.dtype)
        bit *= 2
    mine = me // bit
    result = lax.dynamic_index_in_dim(held, mine, 0, keepdims=False).astype(jnp.float32)
    for flip in range(1, held.shape[0]):
        give = lax.dynamic_index_in_dim(held, mine ^ flip, 0, keepdims=False)
        result = result + exchange(give, axis, flip * bit).astype(jnp.float32)
    return result.astype(total.dtype)


def rank_blocks(counts, cut):
    ranks = []
    for j, mine in enumerate(counts):
        rank = jnp.int32(0)
        for k, other in enumerate(counts):
            if k != j:
                ahead = other >= mine if k < j else other > mine
                rank += ahead.astype(jnp.int32)
        ranks.append(rank)
    offsets = []
    for j in range(len(counts)):
        offset = jnp.int32(0)
        for k, other in enumerate(counts):
            if k != j:
                offset += jnp.where((ranks[k] >= cut) & (ranks[k] < ranks[j]), other, 0)
        offsets.append(offset)
    return ranks, offsets


def pick_kernel(cut, counts_ref, basis_ref, order_ref, offsets_ref, first_ref, rest_ref):
    nblock = basis_ref.shape[0]
    ranks, offsets = rank_blocks([counts_ref[j] for j in range(nblock)], cut)
    for j in range(nblock):
        order_ref[ranks[j]] = jnp.int32(j)
        offsets_ref[j] = offsets[j]
    for place in range(nblock):
        block = basis_ref[order_ref[place]]
        if place < cut:
            first_ref[place] = block
        else:
            rest_ref[place - cut] = block


def pick(cut, counts, basis):
    nblock = basis.shape[0]
    smem, vmem = pl.BlockSpec(memory_space=pltpu.SMEM), pl.BlockSpec(memory_space=pltpu.VMEM)
    return pl.pallas_call(
        functools.partial(pick_kernel, cut),
        out_shape=(
            jax.ShapeDtypeStruct((nblock,), jnp.int32),
            jax.ShapeDtypeStruct((nblock,), jnp.int32),
            jax.ShapeDtypeStruct((cut,) + basis.shape[1:], basis.dtype),
            jax.ShapeDtypeStruct((nblock - cut,) + basis.shape[1:], basis.dtype),
        ),
        in_specs=[smem, vmem],
        out_specs=(smem, smem, vmem, vmem),
        compiler_params=pltpu.CompilerParams(vmem_limit_bytes=VMEM_LIMIT),
    )(counts, basis)


def tables_kernel(cut, nblock, widths, me_ref, *refs):
    *group_refs, counts_ref, order_ref, offsets_ref, branch_ref, joined_ref = refs
    group = group_refs[0].shape[0]
    for place, group_ref in enumerate(group_refs):
        for k in range(group):
            joined_ref[place * group + k] = group_ref[k]

    def step(source, need):
        base = source * nblock
        theirs = (source ^ me_ref[0]) * nblock
        counts = [joined_ref[theirs + j] for j in range(nblock)]
        ranks, offsets = rank_blocks(counts, cut)
        used = jnp.int32(0)
        for j in range(nblock):
            counts_ref[base + j] = counts[j]
            order_ref[base + ranks[j]] = jnp.int32(j)
            offsets_ref[base + j] = offsets[j]
            used += jnp.where(ranks[j] >= cut, counts[j], 0)
        return jnp.maximum(need, used)

    need = lax.fori_loop(0, counts_ref.shape[0] // nblock, step, jnp.int32(0))
    branch = jnp.int32(0)
    for width in widths[:-1]:
        branch += (need > width).astype(jnp.int32)
    branch_ref[0] = branch


def all_tables(cut, nblock, widths, me, groups):
    smem = pl.BlockSpec(memory_space=pltpu.SMEM)
    total = sum(group.shape[0] for group in groups)
    table = jax.ShapeDtypeStruct((total,), jnp.int32)
    return pl.pallas_call(
        functools.partial(tables_kernel, cut, nblock, widths),
        out_shape=(table, table, table, jax.ShapeDtypeStruct((1,), jnp.int32)),
        in_specs=[smem] * (1 + len(groups)),
        out_specs=(smem,) * 4,
        scratch_shapes=[pltpu.SMEM((total,), jnp.int32)],
    )(me, *groups)


def features_kernel(nshard, me_ref, test_ref, source_ref, basis_ref, *refs):
    *counts_refs, test_out_ref, source_out_ref, basis_out_ref, joined_ref, rows_ref = refs
    part = source_ref.shape[2] // nshard
    nblock = counts_refs[0].shape[0]
    for place, counts_ref in enumerate(counts_refs):
        for j in range(nblock):
            joined_ref[place * nblock + j] = counts_ref[j]

    def three_terms(x):
        high = x.astype(jnp.bfloat16).astype(jnp.float32)
        middle = (x - high).astype(jnp.bfloat16).astype(jnp.float32)
        return high, middle, x - high - middle

    def fill(centred, is_test):
        norm = jnp.sum(centred * centred, axis=0, keepdims=True)
        terms = three_terms(centred)
        norms = three_terms(norm + softening if is_test else norm)
        for a in range(3):
            for b in range(3):
                place = 3 * (3 * a + b)
                rows_ref[place : place + 3, :] = -2.0 * terms[a] if is_test else terms[b]
        for a in range(3):
            rows_ref[27 + a : 28 + a, :] = norms[a] if is_test else jnp.ones_like(norm)
            rows_ref[30 + a : 31 + a, :] = jnp.ones_like(norm) if is_test else norms[a]
        return rows_ref[...]

    rows_ref[...] = jnp.zeros_like(rows_ref)
    for i in range(test_ref.shape[1]):
        rows = fill(test_ref[:, i, :] - 0.5, True)
        test_out_ref[i] = rows.T.astype(jnp.bfloat16)
        basis_out_ref[i] = basis_ref[i].T
    for j in range(source_ref.shape[1]):
        pieces = []
        for offset in range(nshard):
            start = pl.multiple_of((me_ref[0] ^ offset) * part, part)
            pieces.append(source_ref[:, j, pl.ds(start, part)])
        rows = fill(jnp.concatenate(pieces, axis=1) - 0.5, False)
        source_out_ref[j] = rows.astype(jnp.bfloat16)


NFEATURE = 128


def distance_features(nshard, me, test_points, source_points, test_basis, counts):
    ntest, _, npoint = test_points.shape
    nsource, _, nq = source_points.shape
    kmax = test_basis.shape[2]
    smem, vmem = pl.BlockSpec(memory_space=pltpu.SMEM), pl.BlockSpec(memory_space=pltpu.VMEM)
    return pl.pallas_call(
        functools.partial(features_kernel, nshard),
        out_shape=(
            jax.ShapeDtypeStruct((ntest, npoint, NFEATURE), jnp.bfloat16),
            jax.ShapeDtypeStruct((nsource, NFEATURE, nq), jnp.bfloat16),
            jax.ShapeDtypeStruct((ntest, kmax, npoint), jnp.bfloat16),
            jax.ShapeDtypeStruct((len(counts) * nsource,), jnp.int32),
        ),
        in_specs=[smem, vmem, vmem, vmem] + [smem] * len(counts),
        out_specs=(vmem, vmem, vmem, smem),
        scratch_shapes=[pltpu.VMEM((NFEATURE, max(npoint, nq)), jnp.float32)],
        compiler_params=pltpu.CompilerParams(vmem_limit_bytes=VMEM_LIMIT),
    )(me, test_points.transpose(1, 0, 2), source_points.transpose(1, 0, 2), test_basis, *counts)


def left_kernel(order_ref, test_ref, source_ref, basis_ref, out_ref):
    nq = source_ref.shape[2]
    block = min(QBLOCK, nq)
    steps = [(i, start) for i in range(test_ref.shape[0]) for start in range(0, nq, block)]

    def kernel_block(i, start):
        squared = jnp.dot(
            test_ref[i], source_ref[0, :, start : start + block], preferred_element_type=jnp.float32
        )
        return lax.rsqrt(squared.astype(jnp.bfloat16))

    ready = kernel_block(*steps[0])
    for place, (i, start) in enumerate(steps):
        now = ready
        if place + 1 < len(steps):
            ready = kernel_block(*steps[place + 1])
        out_ref[i, 0, :, start : start + block] = jnp.dot(
            basis_ref[i], now, preferred_element_type=jnp.float32
        ).astype(jnp.bfloat16)


def left_products(order, test_features, source_features, basis_rows, first, last):
    ntest, npoint, nfeature = test_features.shape
    nq = source_features.shape[2]
    kmax = basis_rows.shape[1]
    nsource = last - first
    return pl.pallas_call(
        left_kernel,
        grid_spec=pltpu.PrefetchScalarGridSpec(
            num_scalar_prefetch=1,
            grid=(nsource,),
            in_specs=[
                pl.BlockSpec((ntest, npoint, nfeature), lambda j, order: (0, 0, 0)),
                pl.BlockSpec((1, nfeature, nq), lambda j, order: (order[first + j], 0, 0)),
                pl.BlockSpec((ntest, kmax, npoint), lambda j, order: (0, 0, 0)),
            ],
            out_specs=pl.BlockSpec((ntest, 1, kmax, nq), lambda j, order: (0, j, 0, 0)),
        ),
        out_shape=jax.ShapeDtypeStruct((ntest, nsource, kmax, nq), jnp.bfloat16),
        compiler_params=pltpu.CompilerParams(vmem_limit_bytes=VMEM_LIMIT),
        cost_estimate=pl.CostEstimate(
            flops=2 * ntest * nsource * npoint * nq * kmax,
            bytes_accessed=2 * ntest * nsource * kmax * nq,
            transcendentals=ntest * nsource * npoint * nq,
        ),
    )(order, test_features, source_features, basis_rows)


def tile_kernel(nshard, first, packed, *refs):
    order_ref, source_counts_ref, offsets_ref, test_counts_ref, left_ref = refs[:5]
    shard_refs = refs[5 : 5 + nshard]
    if packed:
        tile_ref, main_ref, over_ref, pack_ref = refs[5 + nshard :]
    else:
        (tile_ref,) = refs[5 + nshard :]
    j = pl.program_id(0)
    ntest, _, kmax, _ = left_ref.shape
    ndest, _, _, rows, width = tile_ref.shape
    count = source_counts_ref[order_ref[first + j]]

    def work(wide):
        side = jnp.concatenate([shard_ref[0, :, :wide] for shard_ref in shard_refs], axis=0)
        row_ids = lax.broadcasted_iota(jnp.int32, (kmax, wide), 0)
        column_ids = lax.broadcasted_iota(jnp.int32, (kmax, wide), 1)
        products = [
            jnp.dot(left_ref[i, 0], side, preferred_element_type=jnp.float32) for i in range(ntest)
        ]
        if packed:
            offset = offsets_ref[order_ref[first + j]]
            shift = offset % LANES
            base = offset - shift
            low = lax.broadcasted_iota(jnp.int32, (kmax, LANES), 1) < shift
        for i in range(ntest):
            used = (row_ids < test_counts_ref[i]) & (column_ids < count)
            tile = jnp.where(used, products[i], 0.0)
            for dest in range(ndest):
                tile_ref[dest, i, 0, :, :wide] = tile[dest * rows : (dest + 1) * rows].astype(jnp.bfloat16)
                if wide < width:
                    tile_ref[dest, i, 0, :, wide:] = jnp.zeros((rows, width - wide), jnp.bfloat16)
            if not packed:
                continue
            rolled = [
                pltpu.roll(tile[:, start : start + LANES], shift, axis=1) for start in range(0, wide, LANES)
            ]
            for place in range(len(rolled) + 1):
                here = pl.ds(pl.multiple_of(base + place * LANES, LANES), LANES)
                if place == 0:
                    before = jnp.concatenate(
                        [pack_ref[dest, i, :, here].astype(jnp.float32) for dest in range(ndest)], axis=0
                    )
                else:
                    before = rolled[place - 1]
                after = rolled[place] if place < len(rolled) else jnp.zeros_like(before)
                window = jnp.where(low, before, after)
                for dest in range(ndest):
                    pack_ref[dest, i, :, here] = window[dest * rows : (dest + 1) * rows].astype(jnp.bfloat16)

    narrow = width - LANES
    if narrow > 0:
        pl.when(count <= narrow)(lambda: work(narrow))
        pl.when(count > narrow)(lambda: work(width))
    else:
        work(width)

    if packed:

        @pl.when(j == pl.num_programs(0) - 1)
        def _():
            main = main_ref.shape[3]
            main_ref[...] = pack_ref[:, :, :, :main]
            over_ref[...] = pack_ref[:, :, :, main : main + over_ref.shape[3]]


def tiles(ndest, first, tables, test_counts, left, shards, main):
    ntest, nsource, kmax, nq = left.shape
    nshard = len(shards)
    part, width = shards[0].shape[1:]
    rows = kmax // ndest
    packed = main is not None
    shapes = [jax.ShapeDtypeStruct((ndest, ntest, nsource, rows, width), jnp.bfloat16)]
    specs = [pl.BlockSpec((ndest, ntest, 1, rows, width), lambda j, *_: (0, 0, j, 0, 0))]
    scratch = []
    if packed:
        for columns in (main, nsource * width - main):
            shape = (ndest, ntest, rows, columns)
            shapes.append(jax.ShapeDtypeStruct(shape, jnp.bfloat16))
            specs.append(pl.BlockSpec(shape, lambda j, *_: (0, 0, 0, 0)))
        scratch.append(pltpu.VMEM((ndest, ntest, rows, nsource * width + LANES), jnp.bfloat16))
    return pl.pallas_call(
        functools.partial(tile_kernel, nshard, first, packed),
        grid_spec=pltpu.PrefetchScalarGridSpec(
            num_scalar_prefetch=4,
            grid=(nsource,),
            in_specs=[pl.BlockSpec((ntest, 1, kmax, nq), lambda j, *_: (0, j, 0, 0))]
            + [pl.BlockSpec((1, part, width), lambda j, *_: (j, 0, 0))] * nshard,
            out_specs=specs,
            scratch_shapes=scratch,
        ),
        out_shape=shapes,
        compiler_params=pltpu.CompilerParams(vmem_limit_bytes=VMEM_LIMIT),
        cost_estimate=pl.CostEstimate(
            flops=2 * ntest * nsource * kmax * width * nq,
            bytes_accessed=2 * ntest * nsource * kmax * (nq + width),
            transcendentals=0,
        ),
    )(*tables, test_counts, left, *shards)


def project_kernel(cut, order_ref, first_ref, rest_ref, coeff_ref, sum_ref, total_ref):
    j = pl.program_id(0)
    ndest, ntest, _, rows, width = first_ref.shape

    def add(tile_ref, fresh):
        whole = [tile_ref[dest, i, 0] for i in range(ntest) for dest in range(ndest)]
        term = jnp.dot(jnp.concatenate(whole, axis=0), coeff_ref[0], preferred_element_type=jnp.float32)
        total_ref[...] = term if fresh else total_ref[...] + term

    pl.when(j == 0)(lambda: add(first_ref, True))
    pl.when((j > 0) & (j < cut))(lambda: add(first_ref, False))
    pl.when(j >= cut)(lambda: add(rest_ref, False))

    @pl.when(j == pl.num_programs(0) - 1)
    def _():
        for i in range(ntest):
            for dest in range(ndest):
                top = (i * ndest + dest) * rows
                sum_ref[dest, i] = total_ref[top : top + rows, :].astype(sum_ref.dtype)


def project(order, first, rest, coefficients):
    ndest, ntest, cut, rows, width = first.shape
    nsource, _, ncol = coefficients.shape
    block = (ndest, ntest, 1, rows, width)
    return pl.pallas_call(
        functools.partial(project_kernel, cut),
        grid_spec=pltpu.PrefetchScalarGridSpec(
            num_scalar_prefetch=1,
            grid=(nsource,),
            in_specs=[
                pl.BlockSpec(block, lambda j, order: (0, 0, jnp.minimum(j, cut - 1), 0, 0)),
                pl.BlockSpec(block, lambda j, order: (0, 0, jnp.maximum(j - cut, 0), 0, 0)),
                pl.BlockSpec((1, width, ncol), lambda j, order: (order[j], 0, 0)),
            ],
            out_specs=pl.BlockSpec((ndest, ntest, rows, ncol), lambda j, order: (0, 0, 0, 0)),
            scratch_shapes=[pltpu.VMEM((ndest * ntest * rows, ncol), jnp.float32)],
        ),
        out_shape=jax.ShapeDtypeStruct((ndest, ntest, rows, ncol), jnp.bfloat16),
        compiler_params=pltpu.CompilerParams(vmem_limit_bytes=VMEM_LIMIT),
        cost_estimate=pl.CostEstimate(
            flops=2 * ndest * ntest * rows * width * ncol * nsource,
            bytes_accessed=2 * ndest * ntest * rows * width * nsource,
            transcendentals=0,
        ),
    )(order, first, rest, coefficients)


def unpack_kernel(cut, order_ref, counts_ref, offsets_ref, whole_ref, packed_ref, out_ref, rows_ref):
    nsrc, _, _, rows, width = whole_ref.shape
    packed_width = packed_ref.shape[3]
    nall = out_ref.shape[2]
    nblock = nall // nsrc
    ntile = width // LANES
    step = 16 if rows % 16 == 0 else rows
    lanes = lax.broadcasted_iota(jnp.int32, (rows, LANES), 1)

    @pl.loop(0, nsrc)
    def _(source):
        for place in range(nblock):
            block = order_ref[source * nblock + place]
            target = source * nblock + block
            if place < cut:
                rows_ref[target] = whole_ref[source, 0, place].astype(jnp.float32)
                continue
            count = counts_ref[target]
            offset = offsets_ref[target]
            shift = offset % LANES
            base = offset - shift
            back = (LANES - shift) % LANES
            low = lanes < LANES - shift
            rolled = []
            for tile in range(ntile + 1):
                start = pl.multiple_of(jnp.minimum(base + tile * LANES, packed_width - LANES), LANES)
                piece = packed_ref[source, 0, :, pl.ds(start, LANES)].astype(jnp.float32)
                rolled.append(pltpu.roll(piece, back, axis=1))
            for tile in range(ntile):
                value = jnp.where(low, rolled[tile], rolled[tile + 1])
                value = jnp.where(lanes < count - tile * LANES, value, 0.0)
                rows_ref[target, :, tile * LANES : (tile + 1) * LANES] = value

    @pl.loop(0, nall // 16)
    def _(group):
        here = pl.ds(pl.multiple_of(group * 16, 16), 16)
        for top in range(0, rows, step):
            turned = jnp.transpose(rows_ref[here, top : top + step, :], (1, 0, 2))
            out_ref[0, top : top + step, here, :] = turned.astype(out_ref.dtype)


def unpack(cut, tables, whole, packed):
    nsrc, ntest, _, rows, width = whole.shape
    packed_width = packed.shape[3]
    nall = tables[0].shape[0]
    return pl.pallas_call(
        functools.partial(unpack_kernel, cut),
        grid_spec=pltpu.PrefetchScalarGridSpec(
            num_scalar_prefetch=3,
            grid=(ntest,),
            in_specs=[
                pl.BlockSpec((nsrc, 1, cut, rows, width), lambda i, *_: (0, i, 0, 0, 0)),
                pl.BlockSpec((nsrc, 1, rows, packed_width), lambda i, *_: (0, i, 0, 0)),
            ],
            out_specs=pl.BlockSpec((1, rows, nall, width), lambda i, *_: (i, 0, 0, 0)),
            scratch_shapes=[pltpu.VMEM((nall, rows, width), jnp.float32)],
        ),
        out_shape=jax.ShapeDtypeStruct((ntest, rows, nall, width), jnp.bfloat16),
        compiler_params=pltpu.CompilerParams(vmem_limit_bytes=VMEM_LIMIT),
    )(*tables, whole, packed)


def body(
    test_points, test_basis, test_counts, source_points, source_basis, source_counts, coefficients
):
    nsource, part, kmax = source_basis.shape
    ntest = test_points.shape[0]
    nsrc = lax.axis_size("src")
    ntest_axis = lax.axis_size("test")
    me_test = lax.axis_index("test")
    cut = max(1, nsource * 3 // 8)
    held = {}

    def gather(name, shard, left):
        got = {0: shard}
        bits = list(bits_down(ntest_axis))
        for bit in bits:
            if bit == bits[-1]:
                names = [o for o in got if o != 0]
                tied = lax.optimization_barrier(tuple(got[o] for o in names) + (left,))
                got.update(zip(names, tied[:-1]))
                left = tied[-1]
            for offset in list(got):
                got[offset ^ bit] = exchange(got[offset], "test", bit)
            if bit == bits[0]:
                held[name] = got[bit]
        return [got[offset] for offset in sorted(got)], left

    most = (nsource - cut) * kmax
    main = min(most, -(-most * 18 // (25 * LANES)) * LANES)
    widths = [main, min(most, main + 2 * LANES), most]

    order, offsets, basis_a, basis_b = pick(cut, source_counts, source_basis)
    tables = (order, source_counts, offsets)
    inner = max(1, nsrc // 4)
    near = [source_counts] + [exchange(source_counts, "src", flip) for flip in range(1, inner)]
    test_features, source_features, basis_rows, joined = distance_features(
        ntest_axis, jnp.reshape(me_test, (1,)), test_points, source_points, test_basis, near
    )
    groups = [joined] + [exchange(joined, "src", flip) for flip in range(inner, nsrc, inner)]

    left_a = left_products(order, test_features, source_features, basis_rows, 0, cut)
    shards_a, left_a = gather("a", basis_a, left_a)
    (tiles_a,) = tiles(nsrc, 0, tables, test_counts, left_a, shards_a, None)
    moved_a = lax.all_to_all(tiles_a, "src", split_axis=0, concat_axis=0, tiled=True)

    rest, _ = lax.optimization_barrier((basis_b, held["a"]))
    features_b, _ = lax.optimization_barrier((source_features, tiles_a))
    left_b = left_products(order, test_features, features_b, basis_rows, cut, nsource)
    shards_b, left_b = gather("b", rest, left_b)
    tiles_b, packed, beyond = tiles(nsrc, cut, tables, test_counts, left_b, shards_b, main)
    moved_b = lax.all_to_all(packed, "src", split_axis=0, concat_axis=0, tiled=True)

    projected = sum_rows(project(order, tiles_a, tiles_b, coefficients), "src")
    me_src, _ = lax.optimization_barrier((jnp.reshape(lax.axis_index("src"), (1,)), packed))
    all_counts, all_order, all_offsets, branch = all_tables(cut, nsource, widths, me_src, groups)
    spread = (all_order, all_counts, all_offsets)

    def finish(width, beyond, moved_a, moved_b, spread):
        if width > main:
            more = lax.all_to_all(
                beyond[..., : width - main], "src", split_axis=0, concat_axis=0, tiled=True
            )
            moved_b = jnp.concatenate([moved_b, more], axis=3)
        return unpack(cut, spread, moved_a, moved_b)

    reduced = lax.switch(
        branch[0],
        [functools.partial(finish, width) for width in widths],
        beyond,
        moved_a,
        moved_b,
        spread,
    )
    return (reduced, projected)


def solution(mesh):
    return jax.shard_map(
        body,
        mesh=mesh,
        in_specs=(
            P("test", None, None),
            P("test", None, None),
            P("test"),
            P("src", None, None),
            P("src", "test", None),
            P("src"),
            P("src", None, None),
        ),
        out_specs=(P("test", "src", None, None), P("test", "src", None)),
        check_vma=False,
    )
```

profile of v0, /device:TPU:0, one launch (start us, length us, event | category | flops | bytes accessed | tf_op | source)
XLA Modules:
  0.0 161.7 jit_solution(2373691421209063461)
XLA Ops:
  0.6 2.8 %shard_map.86 = (s32[8]{0:T(128)}, s32[8]{0:T(128)}, bf16[3,256,384]{2,1,0:T(8,128)(2,1)}, bf16[5,256,384]{2,1,0:T(8,128)(2,1)}) custom-call(s32[8]{0:T(128)} %refs_1_.3, bf16[8,256,384]{2,1,0:T(8,128)(2,1)} %basis_ref.2), custom_call_target="tpu_custom_call" | custom-call | tf_op jit(solution)/shard_map/pallas_call | solution.py:84
  3.4 3.0 %collective-permute-start = (bf16[3,256,384]{2,1,0:T(8,128)(2,1)}, bf16[3,256,384]{2,1,0:T(8,128)(2,1)S(1)}, u32[]{:S(2)}, u32[]{:S(2)}) collective-permute-start(bf16[3,256,384]{2,1,0:T(8,128)(2,1)} %get-tuple-element.82.refs_5_), channel_id=1, source_target_pairs={{0,16},{8,24},{16,0},{24,8},{1,17},{9,25},{17,1},{25,9},{2,18},{10... | collective-permute-start | bytes 1769480 | tf_op jit(solution)/shard_map/ppermute | solution.py:18
  6.5 1.5 collective-permute-start.2
  7.9 0.0 collective-permute-start.3
  7.9 2.2 %collective-permute-done.2.refs_1_ = s32[8]{0:T(128)S(1)} collective-permute-done((s32[8]{0:T(128)}, s32[8]{0:T(128)S(1)}, u32[]{:S(2)}, u32[]{:S(2)}) %collective-permute-start.2) | collective-permute-done | bytes 64 | tf_op jit(solution)/shard_map/ppermute | solution.py:18
  10.1 0.5 copy-done.7
  10.6 4.8 %shard_map.87 = (bf16[2,1024,128]{2,1,0:T(8,128)(2,1)}, bf16[8,128,1024]{2,1,0:T(8,128)(2,1)}, bf16[2,384,1024]{2,1,0:T(8,128)(2,1)}, s32[16]{0:T(128)}) custom-call(s32[1]{0:T(128)} %bitcast.1.me_ref, f32[3,2,1024]{2,1,0:T(2,128)} %bitcast.25, f32[3,8,1024]{2,1,0:T(8,128)} %bitcast.24, bf16[2,1024,384]{2,1,0:T(8,128)(2,1)} %basis_ref.3, s32[8]{0:T(128)} %refs_1_.3, ...), custom_call_target="tpu_custom_call" | custom-call | tf_op jit(solution)/shard_map/pallas_call | solution.py:186
  15.4 12.7 %shard_map.88.refs_4_ = bf16[2,3,384,1024]{3,2,1,0:T(8,128)(2,1)} custom-call(s32[8]{0:T(128)} %get-tuple-element.79.order_ref.refs_0_, bf16[2,1024,128]{2,1,0:T(8,128)(2,1)} %get-tuple-element.84.test_ref, bf16[8,128,1024]{2,1,0:T(8,128)(2,1)} %get-tuple-element.89.source_ref, bf16[2,384,1024]{2,1,0:T(8,128)(2,1)} %get-tuple-element.86.basis_ref), custom_call_target="tpu_custom_call" | custom-call | flops 4831838208 | bytes 4718592 | tf_op jit(solution)/shard_map/pallas_call | solution.py:227
  28.2 0.0 collective-permute-done.refs_7_
  28.2 0.1 collective-permute-start.4
  28.2 0.0 collective-permute-done.3.refs_6_
  28.3 2.0 %collective-permute-done.4.refs_8_ = bf16[3,256,384]{2,1,0:T(8,128)(2,1)S(1)} collective-permute-done((bf16[3,256,384]{2,1,0:T(8,128)(2,1)S(1)}, bf16[3,256,384]{2,1,0:T(8,128)(2,1)S(1)}, u32[]{:S(2)}, u32[]{:S(2)}) %collective-permute-start.4) | collective-permute-done | bytes 589856 | tf_op jit(solution)/shard_map/ppermute | solution.py:18
  30.2 0.8 copy-done.6
  31.0 6.9 %shard_map.89.first_ref = bf16[8,2,3,48,384]{4,3,2,1,0:T(8,128)(2,1)} custom-call(s32[8]{0:T(128)} %get-tuple-element.79.order_ref.refs_0_, s32[8]{0:T(128)} %refs_1_.3, s32[8]{0:T(128)} %get-tuple-element.80.refs_2_, s32[2]{0:T(128)} %refs_3_.3, bf16[2,3,384,1024]{3,2,1,0:T(8,128)(2,1)} %shard_map.88.refs_4_, ...), custom_call_target="tpu_custom_call" | custom-call | flops 1811939328 | bytes 6488064 | tf_op jit(solution)/shard_map/pallas_call | solution.py:329
  37.9 5.9 %all-to-all-start.2 = ((bf16[8,2,3,48,384]{4,3,2,1,0:T(8,128)(2,1)}), bf16[8,2,3,48,384]{4,3,2,1,0:T(8,128)(2,1)S(1)}, u32[]{:S(2)}, u32[]{:S(2)}) async-start(bf16[8,2,3,48,384]{4,3,2,1,0:T(8,128)(2,1)} %shard_map.89.first_ref), calls=%async_computation.2 | async-start | bytes 3538944 | tf_op jit(solution)/shard_map/all_to_all | solution.py:501
  43.9 0.5 collective-permute-start.1
  44.4 0.0 collective-permute-start.5
  44.4 19.0 %shard_map.90.refs_4_ = bf16[2,5,384,1024]{3,2,1,0:T(8,128)(2,1)} custom-call(s32[8]{0:T(128)} %get-tuple-element.79.order_ref.refs_0_, bf16[2,1024,128]{2,1,0:T(8,128)(2,1)} %get-tuple-element.84.test_ref, bf16[8,128,1024]{2,1,0:T(8,128)(2,1)} %get-tuple-element.89.source_ref, bf16[2,384,1024]{2,1,0:T(8,128)(2,1)} %get-tuple-element.86.basis_ref), custom_call_target="tpu_custom_call" | custom-call | flops 8053063680 | bytes 7864320 | tf_op jit(solution)/shard_map/pallas_call | solution.py:227
  63.4 4.2 %collective-permute-done.1.refs_7_ = bf16[5,256,384]{2,1,0:T(8,128)(2,1)} collective-permute-done((bf16[5,256,384]{2,1,0:T(8,128)(2,1)S(1)}, bf16[5,256,384]{2,1,0:T(8,128)(2,1)}, u32[]{:S(2)}, u32[]{:S(2)}) %collective-permute-start.1) | collective-permute-done | bytes 983072 | tf_op jit(solution)/shard_map/ppermute | solution.py:18
  67.6 0.0 collective-permute-start.6
  67.6 0.0 collective-permute-done.5.refs_6_
  67.6 2.9 %collective-permute-done.6.refs_8_ = bf16[5,256,384]{2,1,0:T(8,128)(2,1)} collective-permute-done((bf16[5,256,384]{2,1,0:T(8,128)(2,1)}, bf16[5,256,384]{2,1,0:T(8,128)(2,1)}, u32[]{:S(2)}, u32[]{:S(2)}) %collective-permute-start.6) | collective-permute-done | bytes 983072 | tf_op jit(solution)/shard_map/ppermute | solution.py:18
  70.5 10.8 %shard_map.91 = (bf16[8,2,5,48,384]{4,3,2,1,0:T(8,128)(2,1)}, bf16[8,2,48,1408]{3,2,1,0:T(8,128)(2,1)}, bf16[8,2,48,512]{3,2,1,0:T(8,128)(2,1)S(1)}) custom-call(s32[8]{0:T(128)} %get-tuple-element.79.order_ref.refs_0_, s32[8]{0:T(128)} %refs_1_.3, s32[8]{0:T(128)} %get-tuple-element.80.refs_2_, s32[2]{0:T(128)} %refs_3_.3, ...), custom_call_target="tpu_custom_call" | custom-call | flops 3019898880 | bytes 10813440 | tf_op jit(solution)/shard_map/pallas_call | solution.py:329
  81.2 4.2 %all-to-all-done.2 = bf16[8,2,3,48,384]{4,3,2,1,0:T(8,128)(2,1)S(1)} async-done(((bf16[8,2,3,48,384]{4,3,2,1,0:T(8,128)(2,1)}), bf16[8,2,3,48,384]{4,3,2,1,0:T(8,128)(2,1)S(1)}, u32[]{:S(2)}, u32[]{:S(2)}) %all-to-all-start.2) | async-done | bytes 1769504 | tf_op jit(solution)/shard_map/all_to_all | solution.py:501
  85.4 1.2 copy-done
  86.6 3.8 %all-to-all-start.3 = ((bf16[8,2,48,1408]{3,2,1,0:T(8,128)(2,1)}), bf16[8,2,48,1408]{3,2,1,0:T(8,128)(2,1)S(1)}, u32[]{:S(2)}, u32[]{:S(2)}) async-start(bf16[8,2,48,1408]{3,2,1,0:T(8,128)(2,1)} %get-tuple-element.92), calls=%async_computation.3 | async-start | bytes 4325376 | tf_op jit(solution)/shard_map/all_to_all | solution.py:508
  90.4 9.7 %shard_map.93 = bf16[8,2,48,512]{3,2,1,0:T(8,128)(2,1)} custom-call(s32[8]{0:T(128)} %get-tuple-element.79.order_ref.refs_0_, bf16[8,2,3,48,384]{4,3,2,1,0:T(8,128)(2,1)} %shard_map.89.first_ref, bf16[8,2,5,48,384]{4,3,2,1,0:T(8,128)(2,1)} %get-tuple-element.100.rest_ref, bf16[8,384,512]{2,1,0:T(8,128)(2,1)} %coeff_ref.1), custom_call_target="tpu_custom_call" | custom-call | flops 2415919104 | bytes 4718592 | tf_op jit(solution)/shard_map/pallas_call | solution.py:374
  100.1 1.0 dynamic-slice_bitcast_fusion
  101.2 2.0 %collective-permute-start.10 = (bf16[4,2,48,512]{3,2,1,0:T(8,128)(2,1)S(1)}, bf16[4,2,48,512]{3,2,1,0:T(8,128)(2,1)}, u32[]{:S(2)}, u32[]{:S(2)}) collective-permute-start(bf16[4,2,48,512]{3,2,1,0:T(8,128)(2,1)S(1)} %dynamic-slice_bitcast_fusion), channel_id=1, source_target_pairs={{0,1},{1,0},{2,3},{3,2},{4,5},{5,4},{6,7},{7,6},{8,9},{9,8},{10,11... | collective-permute-start | bytes 1179656 | tf_op jit(solution)/shard_map/ppermute | solution.py:18
  103.2 21.5 %collective-permute-done.10 = bf16[4,2,48,512]{3,2,1,0:T(8,128)(2,1)} collective-permute-done((bf16[4,2,48,512]{3,2,1,0:T(8,128)(2,1)S(1)}, bf16[4,2,48,512]{3,2,1,0:T(8,128)(2,1)}, u32[]{:S(2)}, u32[]{:S(2)}) %collective-permute-start.10) | collective-permute-done | bytes 393248 | tf_op jit(solution)/shard_map/ppermute | solution.py:18
  124.7 1.2 fusion
  125.9 0.7 dynamic-slice_bitcast_fusion.3
  126.7 0.0 collective-permute-start.11
  126.7 7.8 %collective-permute-start.12 = (bf16[2,48,512]{2,1,0:T(8,128)(2,1)}, bf16[2,48,512]{2,1,0:T(8,128)(2,1)S(1)}, u32[]{:S(2)}, u32[]{:S(2)}) collective-permute-start(bf16[2,48,512]{2,1,0:T(8,128)(2,1)} %get-tuple-element.103), channel_id=1, source_target_pairs={{0,4},{1,5},{2,6},{3,7},{4,0},{5,1},{6,2},{7,3},{8,12},{9,13},{10,... | collective-permute-start | bytes 294920 | tf_op jit(solution)/shard_map/ppermute | solution.py:18
  134.5 0.0 collective-permute-start.13
  134.5 0.6 collective-permute-start.7
  135.1 3.8 %collective-permute-start.8 = (s32[16]{0:T(128)S(1)}, s32[16]{0:T(128)S(1)}, u32[]{:S(2)}, u32[]{:S(2)}) collective-permute-start(s32[16]{0:T(128)S(1)} %copy-done.8), channel_id=1, source_target_pairs={{0,4},{1,5},{2,6},{3,7},{4,0},{5,1},{6,2},{7,3},{8,12},{9,13},{10,... | collective-permute-start | bytes 200 | tf_op jit(solution)/shard_map/ppermute | solution.py:18
  138.9 0.0 collective-permute-done.7.refs_1_
  138.9 3.0 %collective-permute-start.9 = (s32[16]{0:T(128)S(1)}, s32[16]{0:T(128)}, u32[]{:S(2)}, u32[]{:S(2)}) collective-permute-start(s32[16]{0:T(128)S(1)} %copy-done.8), channel_id=1, source_target_pairs={{0,6},{1,7},{2,4},{3,5},{4,2},{5,3},{6,0},{7,1},{8,14},{9,15},{10,... | collective-permute-start | bytes 200 | tf_op jit(solution)/shard_map/ppermute | solution.py:18
  141.9 6.6 %collective-permute-done.8.refs_2_ = s32[16]{0:T(128)S(1)} collective-permute-done((s32[16]{0:T(128)S(1)}, s32[16]{0:T(128)S(1)}, u32[]{:S(2)}, u32[]{:S(2)}) %collective-permute-start.8) | collective-permute-done | bytes 96 | tf_op jit(solution)/shard_map/ppermute | solution.py:18
  148.6 0.5 copy-done.10
  149.1 0.0 collective-permute-done.9.refs_3_
  149.1 2.7 %shard_map.92 = (s32[64]{0:T(128)S(1)}, s32[64]{0:T(128)S(1)}, s32[64]{0:T(128)S(1)}, s32[1]{0:T(128)}) custom-call(s32[1]{0:T(128)} %bitcast.me_ref, s32[16]{0:T(128)} %get-tuple-element.94.refs_0_, s32[16]{0:T(128)} %copy-done.9, s32[16]{0:T(128)} %copy-done.10, s32[16]{0:T(128)} %collective-permute-done.9.refs_3_), custom_call_target="tpu_custom_call" | custom-call | tf_op jit(solution)/shard_map/pallas_call | solution.py:129
  152.5 0.0 collective-permute-done.11
  152.5 0.0 collective-permute-done.13
  152.5 1.6 fusion.3
  154.1 7.6 %conditional.1 = (bf16[2,48,64,384]{3,2,1,0:T(8,128)(2,1)}) conditional(s32[]{:T(128)} %bitcast.4, (s32[64]{0:T(128)S(1)}, s32[64]{0:T(128)S(1)}, s32[64]{0:T(128)S(1)}, bf16[8,2,3,48,384]{4,3,2,1,0:T(8,128)(2,1)}, bf16[8,2,48,1408]{3,2,1,0:T(8,128)(2,1)S(1)}) %tuple.35, (bf16[8,2,48,512]{3,2,1,0:T(8,128)(2,1)S(1)}, ...), branch_computations={%region_0.1_spmd, %region_1.2_spmd, %region_2.3_spmd} | conditional | flops 5898240 | bytes 14549028 | solution.py:523
  154.1 7.6 %branch_0_fun.1 = bf16[2,48,64,384]{3,2,1,0:T(8,128)(2,1)} custom-call(s32[64]{0:T(128)S(1)} %get-tuple-element.26.order_ref, s32[64]{0:T(128)S(1)} %get-tuple-element.27.counts_ref, s32[64]{0:T(128)S(1)} %get-tuple-element.40.offsets_ref, bf16[8,2,3,48,384]{4,3,2,1,0:T(8,128)(2,1)} %get-tuple-element.41.whole_ref, ...), custom_call_target="tpu_custom_call" | custom-call | tf_op jit(solution)/shard_map/cond/branch_0_fun/pallas_call | solution.py:442
  (16 shorter events, 0.0 us)
Async XLA Ops:
  3.4 24.7 %collective-permute-start = (bf16[3,256,384]{2,1,0:T(8,128)(2,1)}, bf16[3,256,384]{2,1,0:T(8,128)(2,1)S(1)}, u32[]{:S(2)}, u32[]{:S(2)}) collective-permute-start(bf16[3,256,384]{2,1,0:T(8,128)(2,1)} %get-tuple-element.82.refs_5_), channel_id=1, source_target_pairs={{0,16},{8,24},{16,0},{24,8},{1,17},{9,25},{17,1},{25,9},{2,18},{10... | collective-permute-start | bytes 1769480 | tf_op jit(solution)/shard_map/ppermute | solution.py:18
  6.5 3.7 %collective-permute-start.2 = (s32[8]{0:T(128)}, s32[8]{0:T(128)S(1)}, u32[]{:S(2)}, u32[]{:S(2)}) collective-permute-start(s32[8]{0:T(128)} %refs_1_.3), channel_id=1, source_target_pairs={{0,1},{1,0},{2,3},{3,2},{4,5},{5,4},{6,7},{7,6},{8,9},{9,8},{10,11... | collective-permute-start | bytes 104 | tf_op jit(solution)/shard_map/ppermute | solution.py:18
  7.9 20.3 %collective-permute-start.3 = (bf16[3,256,384]{2,1,0:T(8,128)(2,1)}, bf16[3,256,384]{2,1,0:T(8,128)(2,1)S(1)}, u32[]{:S(2)}, u32[]{:S(2)}) collective-permute-start(bf16[3,256,384]{2,1,0:T(8,128)(2,1)} %get-tuple-element.82.refs_5_), channel_id=1, source_target_pairs={{0,8},{8,0},{16,24},{24,16},{1,9},{9,1},{17,25},{25,17},{2,10},{10... | collective-permute-start | bytes 1769480 | tf_op jit(solution)/shard_map/ppermute | solution.py:18
  10.1 0.5 copy-start.7
  28.2 2.1 %copy-start.4 = (bf16[3,256,384]{2,1,0:T(8,128)(2,1)}, bf16[3,256,384]{2,1,0:T(8,128)(2,1)S(1)}, u32[]{:S(2)}) copy-start(bf16[3,256,384]{2,1,0:T(8,128)(2,1)S(1)} %collective-permute-done.refs_7_) | copy-start | bytes 1769476
  28.2 2.1 %collective-permute-start.4 = (bf16[3,256,384]{2,1,0:T(8,128)(2,1)S(1)}, bf16[3,256,384]{2,1,0:T(8,128)(2,1)S(1)}, u32[]{:S(2)}, u32[]{:S(2)}) collective-permute-start(bf16[3,256,384]{2,1,0:T(8,128)(2,1)S(1)} %collective-permute-done.refs_7_), channel_id=1, source_target_pairs={{0,8},{8,0},{16,24},{24,16},{1,9},{9,1},{17,25},{25,17},{2,10},{10... | collective-permute-start | bytes 1769480 | tf_op jit(solution)/shard_map/ppermute | solution.py:18
  28.2 2.0 %copy-start.5 = (bf16[3,256,384]{2,1,0:T(8,128)(2,1)}, bf16[3,256,384]{2,1,0:T(8,128)(2,1)S(1)}, u32[]{:S(2)}) copy-start(bf16[3,256,384]{2,1,0:T(8,128)(2,1)S(1)} %collective-permute-done.3.refs_6_) | copy-start | bytes 1769476
  30.2 0.8 copy-start.6
  37.9 5.9 %copy-start.3 = (bf16[5,256,384]{2,1,0:T(8,128)(2,1)S(1)}, bf16[5,256,384]{2,1,0:T(8,128)(2,1)}, u32[]{:S(2)}) copy-start(bf16[5,256,384]{2,1,0:T(8,128)(2,1)} %get-tuple-element.83.refs_5_) | copy-start | bytes 2949124
  37.9 47.4 %all-to-all-start.2 = ((bf16[8,2,3,48,384]{4,3,2,1,0:T(8,128)(2,1)}), bf16[8,2,3,48,384]{4,3,2,1,0:T(8,128)(2,1)S(1)}, u32[]{:S(2)}, u32[]{:S(2)}) async-start(bf16[8,2,3,48,384]{4,3,2,1,0:T(8,128)(2,1)} %shard_map.89.first_ref), calls=%async_computation.2 | async-start | bytes 3538944 | tf_op jit(solution)/shard_map/all_to_all | solution.py:501
  43.9 23.7 %collective-permute-start.1 = (bf16[5,256,384]{2,1,0:T(8,128)(2,1)S(1)}, bf16[5,256,384]{2,1,0:T(8,128)(2,1)}, u32[]{:S(2)}, u32[]{:S(2)}) collective-permute-start(bf16[5,256,384]{2,1,0:T(8,128)(2,1)S(1)} %copy-done.3), channel_id=1, source_target_pairs={{0,16},{8,24},{16,0},{24,8},{1,17},{9,25},{17,1},{25,9},{2,18},{10... | collective-permute-start | bytes 2949128 | tf_op jit(solution)/shard_map/ppermute | solution.py:18
  44.4 23.2 %collective-permute-start.5 = (bf16[5,256,384]{2,1,0:T(8,128)(2,1)S(1)}, bf16[5,256,384]{2,1,0:T(8,128)(2,1)}, u32[]{:S(2)}, u32[]{:S(2)}) collective-permute-start(bf16[5,256,384]{2,1,0:T(8,128)(2,1)S(1)} %copy-done.3), channel_id=1, source_target_pairs={{0,8},{8,0},{16,24},{24,16},{1,9},{9,1},{17,25},{25,17},{2,10},{10... | collective-permute-start | bytes 2949128 | tf_op jit(solution)/shard_map/ppermute | solution.py:18
  67.6 2.9 %collective-permute-start.6 = (bf16[5,256,384]{2,1,0:T(8,128)(2,1)}, bf16[5,256,384]{2,1,0:T(8,128)(2,1)}, u32[]{:S(2)}, u32[]{:S(2)}) collective-permute-start(bf16[5,256,384]{2,1,0:T(8,128)(2,1)} %collective-permute-done.1.refs_7_), channel_id=1, source_target_pairs={{0,8},{8,0},{16,24},{24,16},{1,9},{9,1},{17,25},{25,17},{2,10},{10... | collective-permute-start | bytes 2949128 | tf_op jit(solution)/shard_map/ppermute | solution.py:18
  85.4 1.2 copy-start
  86.6 67.5 %all-to-all-start.3 = ((bf16[8,2,48,1408]{3,2,1,0:T(8,128)(2,1)}), bf16[8,2,48,1408]{3,2,1,0:T(8,128)(2,1)S(1)}, u32[]{:S(2)}, u32[]{:S(2)}) async-start(bf16[8,2,48,1408]{3,2,1,0:T(8,128)(2,1)} %get-tuple-element.92), calls=%async_computation.3 | async-start | bytes 4325376 | tf_op jit(solution)/shard_map/all_to_all | solution.py:508
  90.4 44.1 %copy-start.8 = (s32[16]{0:T(128)S(1)}, s32[16]{0:T(128)}, u32[]{:S(2)}) copy-start(s32[16]{0:T(128)} %get-tuple-element.94.refs_0_) | copy-start | bytes 196
  101.2 23.6 %collective-permute-start.10 = (bf16[4,2,48,512]{3,2,1,0:T(8,128)(2,1)S(1)}, bf16[4,2,48,512]{3,2,1,0:T(8,128)(2,1)}, u32[]{:S(2)}, u32[]{:S(2)}) collective-permute-start(bf16[4,2,48,512]{3,2,1,0:T(8,128)(2,1)S(1)} %dynamic-slice_bitcast_fusion), channel_id=1, source_target_pairs={{0,1},{1,0},{2,3},{3,2},{4,5},{5,4},{6,7},{7,6},{8,9},{9,8},{10,11... | collective-permute-start | bytes 1179656 | tf_op jit(solution)/shard_map/ppermute | solution.py:18
  126.7 25.9 %collective-permute-start.11 = (bf16[2,48,512]{2,1,0:T(8,128)(2,1)}, bf16[2,48,512]{2,1,0:T(8,128)(2,1)S(1)}, u32[]{:S(2)}, u32[]{:S(2)}) collective-permute-start(bf16[2,48,512]{2,1,0:T(8,128)(2,1)} %get-tuple-element.101), channel_id=1, source_target_pairs={{0,2},{1,3},{2,0},{3,1},{4,6},{5,7},{6,4},{7,5},{8,10},{9,11},{10,... | collective-permute-start | bytes 294920 | tf_op jit(solution)/shard_map/ppermute | solution.py:18
  126.7 25.9 %collective-permute-start.12 = (bf16[2,48,512]{2,1,0:T(8,128)(2,1)}, bf16[2,48,512]{2,1,0:T(8,128)(2,1)S(1)}, u32[]{:S(2)}, u32[]{:S(2)}) collective-permute-start(bf16[2,48,512]{2,1,0:T(8,128)(2,1)} %get-tuple-element.103), channel_id=1, source_target_pairs={{0,4},{1,5},{2,6},{3,7},{4,0},{5,1},{6,2},{7,3},{8,12},{9,13},{10,... | collective-permute-start | bytes 294920 | tf_op jit(solution)/shard_map/ppermute | solution.py:18
  134.5 18.0 %collective-permute-start.13 = (bf16[2,48,512]{2,1,0:T(8,128)(2,1)}, bf16[2,48,512]{2,1,0:T(8,128)(2,1)}, u32[]{:S(2)}, u32[]{:S(2)}) collective-permute-start(bf16[2,48,512]{2,1,0:T(8,128)(2,1)} %get-tuple-element.102), channel_id=1, source_target_pairs={{0,6},{1,7},{2,4},{3,5},{4,2},{5,3},{6,0},{7,1},{8,14},{9,15},{10,... | collective-permute-start | bytes 294920 | tf_op jit(solution)/shard_map/ppermute | solution.py:18
  134.5 4.4 %collective-permute-start.7 = (s32[16]{0:T(128)S(1)}, s32[16]{0:T(128)S(1)}, u32[]{:S(2)}, u32[]{:S(2)}) collective-permute-start(s32[16]{0:T(128)S(1)} %copy-done.8), channel_id=1, source_target_pairs={{0,2},{1,3},{2,0},{3,1},{4,6},{5,7},{6,4},{7,5},{8,10},{9,11},{10,... | collective-permute-start | bytes 200 | tf_op jit(solution)/shard_map/ppermute | solution.py:18
  135.1 13.5 %collective-permute-start.8 = (s32[16]{0:T(128)S(1)}, s32[16]{0:T(128)S(1)}, u32[]{:S(2)}, u32[]{:S(2)}) collective-permute-start(s32[16]{0:T(128)S(1)} %copy-done.8), channel_id=1, source_target_pairs={{0,4},{1,5},{2,6},{3,7},{4,0},{5,1},{6,2},{7,3},{8,12},{9,13},{10,... | collective-permute-start | bytes 200 | tf_op jit(solution)/shard_map/ppermute | solution.py:18
  138.9 9.7 %copy-start.9 = (s32[16]{0:T(128)}, s32[16]{0:T(128)S(1)}, u32[]{:S(2)}) copy-start(s32[16]{0:T(128)S(1)} %collective-permute-done.7.refs_1_) | copy-start | bytes 196
  138.9 10.2 %collective-permute-start.9 = (s32[16]{0:T(128)S(1)}, s32[16]{0:T(128)}, u32[]{:S(2)}, u32[]{:S(2)}) collective-permute-start(s32[16]{0:T(128)S(1)} %copy-done.8), channel_id=1, source_target_pairs={{0,6},{1,7},{2,4},{3,5},{4,2},{5,3},{6,0},{7,1},{8,14},{9,15},{10,... | collective-permute-start | bytes 200 | tf_op jit(solution)/shard_map/ppermute | solution.py:18
  148.6 0.5 copy-start.10
where the time goes:
time: 162 us
  Pallas kernels  76.9 us (47%)
  waiting for transfers between devices  43.6 us (27%)
  starting transfers between devices  32.2 us (20%)
  local copies, waits for them, and re-layouts  4.83 us (3%)
  other arithmetic  2.81 us (2%)
    ppermute x14, waiting for transfers between devices, exchange(): return lax.ppermute(x, axis, [(a, a ^ flip) for a in range(size)])  39.4 us
    pallas_call x2, Pallas kernels, left_products(): pl.pallas_call(left_kernel, grid_spec=pltpu.PrefetchScalarGridSpec(num_sc...  31.7 us
    ppermute x14, starting transfers between devices, exchange(): return lax.ppermute(x, axis, [(a, a ^ flip) for a in range(size)])  22.4 us
    pallas_call x2, Pallas kernels, tiles(): pl.pallas_call(functools.partial(tile_kernel, nshard, first, packed), gri...  17.7 us
    pallas_call x1, Pallas kernels, project(): pl.pallas_call(functools.partial(project_kernel, cut), grid_spec=pltpu.Pr...  9.69 us
    pallas_call x1, Pallas kernels, unpack(): pl.pallas_call(functools.partial(unpack_kernel, cut), grid_spec=pltpu.Pre...  7.58 us
    all_to_all x1, starting transfers between devices, body(): lax.all_to_all(tiles_a, 'src', split_axis=0, concat_axis=0, tiled=True)  5.93 us
    pallas_call x1, Pallas kernels, distance_features(): pl.pallas_call(functools.partial(features_kernel, nshard), out_shape=(jax...  4.76 us
  transfers between devices with their start and end apart: 16, of which 7 were waited for; matrix products, arithmetic and copies ran while one was open for 3% of the time, Pallas kernels for 37%

commit v1 on v0

--- a/solution.py
+++ b/solution.py
@@ -135,13 +135,8 @@
     )(me, *groups)
 
 
-def features_kernel(nshard, me_ref, test_ref, source_ref, basis_ref, *refs):
-    *counts_refs, test_out_ref, source_out_ref, basis_out_ref, joined_ref, rows_ref = refs
+def features_kernel(nshard, me_ref, test_ref, source_ref, basis_ref, test_out_ref, source_out_ref, basis_out_ref, rows_ref):
     part = source_ref.shape[2] // nshard
-    nblock = counts_refs[0].shape[0]
-    for place, counts_ref in enumerate(counts_refs):
-        for j in range(nblock):
-            joined_ref[place * nblock + j] = counts_ref[j]
 
     def three_terms(x):
         high = x.astype(jnp.bfloat16).astype(jnp.float32)
@@ -178,7 +173,7 @@
 NFEATURE = 128
 
 
-def distance_features(nshard, me, test_points, source_points, test_basis, counts):
+def distance_features(nshard, me, test_points, source_points, test_basis):
     ntest, _, npoint = test_points.shape
     nsource, _, nq = source_points.shape
     kmax = test_basis.shape[2]
@@ -189,13 +184,12 @@
             jax.ShapeDtypeStruct((ntest, npoint, NFEATURE), jnp.bfloat16),
             jax.ShapeDtypeStruct((nsource, NFEATURE, nq), jnp.bfloat16),
             jax.ShapeDtypeStruct((ntest, kmax, npoint), jnp.bfloat16),
-            jax.ShapeDtypeStruct((len(counts) * nsource,), jnp.int32),
-        ),
-        in_specs=[smem, vmem, vmem, vmem] + [smem] * len(counts),
-        out_specs=(vmem, vmem, vmem, smem),
+        ),
+        in_specs=[smem, vmem, vmem, vmem],
+        out_specs=(vmem, vmem, vmem),
         scratch_shapes=[pltpu.VMEM((NFEATURE, max(npoint, nq)), jnp.float32)],
         compiler_params=pltpu.CompilerParams(vmem_limit_bytes=VMEM_LIMIT),
-    )(me, test_points.transpose(1, 0, 2), source_points.transpose(1, 0, 2), test_basis, *counts)
+    )(me, test_points.transpose(1, 0, 2), source_points.transpose(1, 0, 2), test_basis)
 
 
 def left_kernel(order_ref, test_ref, source_ref, basis_ref, out_ref):
@@ -346,7 +340,8 @@
     )(*tables, test_counts, left, *shards)
 
 
-def project_kernel(cut, order_ref, first_ref, rest_ref, coeff_ref, sum_ref, total_ref):
+def project_kernel(cut, order_ref, first_ref, rest_ref, coeff_ref, *refs):
+    *counts_refs, sum_ref, joined_ref, total_ref = refs
     j = pl.program_id(0)
     ndest, ntest, _, rows, width = first_ref.shape
 
@@ -365,12 +360,17 @@
             for dest in range(ndest):
                 top = (i * ndest + dest) * rows
                 sum_ref[dest, i] = total_ref[top : top + rows, :].astype(sum_ref.dtype)
-
-
-def project(order, first, rest, coefficients):
+        nblock = counts_refs[0].shape[0]
+        for place, counts_ref in enumerate(counts_refs):
+            for k in range(nblock):
+                joined_ref[place * nblock + k] = counts_ref[k]
+
+
+def project(order, first, rest, coefficients, counts):
     ndest, ntest, cut, rows, width = first.shape
     nsource, _, ncol = coefficients.shape
     block = (ndest, ntest, 1, rows, width)
+    smem = pl.BlockSpec(memory_space=pltpu.SMEM)
     return pl.pallas_call(
         functools.partial(project_kernel, cut),
         grid_spec=pltpu.PrefetchScalarGridSpec(
@@ -380,18 +380,22 @@
                 pl.BlockSpec(block, lambda j, order: (0, 0, jnp.minimum(j, cut - 1), 0, 0)),
                 pl.BlockSpec(block, lambda j, order: (0, 0, jnp.maximum(j - cut, 0), 0, 0)),
                 pl.BlockSpec((1, width, ncol), lambda j, order: (order[j], 0, 0)),
-            ],
-            out_specs=pl.BlockSpec((ndest, ntest, rows, ncol), lambda j, order: (0, 0, 0, 0)),
+            ]
+            + [smem] * len(counts),
+            out_specs=(pl.BlockSpec((ndest, ntest, rows, ncol), lambda j, order: (0, 0, 0, 0)), smem),
             scratch_shapes=[pltpu.VMEM((ndest * ntest * rows, ncol), jnp.float32)],
         ),
-        out_shape=jax.ShapeDtypeStruct((ndest, ntest, rows, ncol), jnp.bfloat16),
+        out_shape=(
+            jax.ShapeDtypeStruct((ndest, ntest, rows, ncol), jnp.bfloat16),
+            jax.ShapeDtypeStruct((len(counts) * nsource,), jnp.int32),
+        ),
         compiler_params=pltpu.CompilerParams(vmem_limit_bytes=VMEM_LIMIT),
         cost_estimate=pl.CostEstimate(
             flops=2 * ndest * ntest * rows * width * ncol * nsource,
             bytes_accessed=2 * ndest * ntest * rows * width * nsource,
             transcendentals=0,
         ),
-    )(order, first, rest, coefficients)
+    )(order, first, rest, coefficients, *counts)
 
 
 def unpack_kernel(cut, order_ref, counts_ref, offsets_ref, whole_ref, packed_ref, out_ref, rows_ref):
@@ -465,21 +469,18 @@
     ntest_axis = lax.axis_size("test")
     me_test = lax.axis_index("test")
     cut = max(1, nsource * 3 // 8)
-    held = {}
 
     def gather(name, shard, left):
         got = {0: shard}
         bits = list(bits_down(ntest_axis))
         for bit in bits:
-            if bit == bits[-1]:
+            if bit == bits[-1] and name == "a":
                 names = [o for o in got if o != 0]
                 tied = lax.optimization_barrier(tuple(got[o] for o in names) + (left,))
                 got.update(zip(names, tied[:-1]))
                 left = tied[-1]
             for offset in list(got):
                 got[offset ^ bit] = exchange(got[offset], "test", bit)
-            if bit == bits[0]:
-                held[name] = got[bit]
         return [got[offset] for offset in sorted(got)], left
 
     most = (nsource - cut) * kmax
@@ -488,26 +489,28 @@
 
     order, offsets, basis_a, basis_b = pick(cut, source_counts, source_basis)
     tables = (order, source_counts, offsets)
-    inner = max(1, nsrc // 4)
-    near = [source_counts] + [exchange(source_counts, "src", flip) for flip in range(1, inner)]
-    test_features, source_features, basis_rows, joined = distance_features(
-        ntest_axis, jnp.reshape(me_test, (1,)), test_points, source_points, test_basis, near
+    test_features, source_features, basis_rows = distance_features(
+        ntest_axis, jnp.reshape(me_test, (1,)), test_points, source_points, test_basis
     )
-    groups = [joined] + [exchange(joined, "src", flip) for flip in range(inner, nsrc, inner)]
 
     left_a = left_products(order, test_features, source_features, basis_rows, 0, cut)
     shards_a, left_a = gather("a", basis_a, left_a)
     (tiles_a,) = tiles(nsrc, 0, tables, test_counts, left_a, shards_a, None)
     moved_a = lax.all_to_all(tiles_a, "src", split_axis=0, concat_axis=0, tiled=True)
 
-    rest, _ = lax.optimization_barrier((basis_b, held["a"]))
+    rest, _ = lax.optimization_barrier((basis_b, source_features))
     features_b, _ = lax.optimization_barrier((source_features, tiles_a))
     left_b = left_products(order, test_features, features_b, basis_rows, cut, nsource)
     shards_b, left_b = gather("b", rest, left_b)
     tiles_b, packed, beyond = tiles(nsrc, cut, tables, test_counts, left_b, shards_b, main)
     moved_b = lax.all_to_all(packed, "src", split_axis=0, concat_axis=0, tiled=True)
 
-    projected = sum_rows(project(order, tiles_a, tiles_b, coefficients), "src")
+    inner = max(1, nsrc // 4)
+    counts, _ = lax.optimization_barrier((source_counts, tiles_a))
+    near = [counts] + [exchange(counts, "src", flip) for flip in range(1, inner)]
+    sums, joined = project(order, tiles_a, tiles_b, coefficients, near)
+    groups = [joined] + [exchange(joined, "src", flip) for flip in range(inner, nsrc, inner)]
+    projected = sum_rows(sums, "src")
     me_src, _ = lax.optimization_barrier((jnp.reshape(lax.axis_index("src"), (1,)), packed))
     all_counts, all_order, all_offsets, branch = all_tables(cut, nsource, widths, me_src, groups)
     spread = (all_order, all_counts, all_offsets)

time: 162 us -> 194 us (1.20)
  blocking collectives: 0 us -> 15.9 us
  waiting for transfers between devices: 43.6 us -> 55.9 us
    ppermute x14, waiting for transfers between devices: 39.4 us -> 55.9 us  [exchange(): return lax.ppermute(x, axis, [(a, a ^ flip) for a in range(size)])]
    all_to_all x0 -> x1, blocking collectives: none -> 15.9 us  [finish(): lax.all_to_all(beyond[..., :width - main], 'src', split_axis=0, concat_ax...]
    all_to_all x1, waiting for transfers between devices: 4.16 us -> 0.01 us  [body(): lax.all_to_all(tiles_a, 'src', split_axis=0, concat_axis=0, tiled=True)]
  transfers between devices with their start and end apart: 16 -> 16, of which waited for: 7 -> 6; matrix products, arithmetic and copies ran while one was open for 3% -> 2% of each run, Pallas kernels for 37% -> 31%
where the time goes in v1:
time: 194 us; the launch traced here: 193 us
  Pallas kernels  77.9 us (40%)
  waiting for transfers between devices  55.9 us (29%)
  starting transfers between devices  32.7 us (17%)
  blocking collectives  15.9 us (8%)
  local copies, waits for them, and re-layouts  4.94 us (3%)
  other arithmetic  4.49 us (2%)
    ppermute x14, waiting for transfers between devices, exchange(): return lax.ppermute(x, axis, [(a, a ^ flip) for a in range(size)])  55.9 us
    pallas_call x2, Pallas kernels, left_products(): pl.pallas_call(left_kernel, grid_spec=pltpu.PrefetchScalarGridSpec(num_sc...  31.6 us
    ppermute x14, starting transfers between devices, exchange(): return lax.ppermute(x, axis, [(a, a ^ flip) for a in range(size)])  21.3 us
    pallas_call x2, Pallas kernels, tiles(): pl.pallas_call(functools.partial(tile_kernel, nshard, first, packed), gri...  18.3 us
    all_to_all x1, blocking collectives, finish(): lax.all_to_all(beyond[..., :width - main], 'src', split_axis=0, concat_ax...  15.9 us
    pallas_call x1, Pallas kernels, project(): pl.pallas_call(functools.partial(project_kernel, cut), grid_spec=pltpu.Pr...  9.88 us
    pallas_call x1, Pallas kernels, unpack(): pl.pallas_call(functools.partial(unpack_kernel, cut), grid_spec=pltpu.Pre...  7.81 us
    all_to_all x1, starting transfers between devices, body(): lax.all_to_all(tiles_a, 'src', split_axis=0, concat_axis=0, tiled=True)  5.97 us
  transfers between devices with their start and end apart: 16, of which 6 were waited for; matrix products, arithmetic and copies ran while one was open for 2% of the time, Pallas kernels for 31%

profile of v1, /device:TPU:0, one launch (start us, length us, event | category | flops | bytes accessed | tf_op | source)
XLA Modules:
  0.0 193.2 jit_solution(9796094507514700286)
XLA Ops:
  0.6 2.8 %shard_map.86 = (s32[8]{0:T(128)}, s32[8]{0:T(128)}, bf16[3,256,384]{2,1,0:T(8,128)(2,1)}, bf16[5,256,384]{2,1,0:T(8,128)(2,1)}) custom-call(s32[8]{0:T(128)} %refs_0_, bf16[8,256,384]{2,1,0:T(8,128)(2,1)} %basis_ref.2), custom_call_target="tpu_custom_call" | custom-call | tf_op jit(solution)/shard_map/pallas_call | solution.py:84
  3.4 3.0 %collective-permute-start = (bf16[3,256,384]{2,1,0:T(8,128)(2,1)}, bf16[3,256,384]{2,1,0:T(8,128)(2,1)S(1)}, u32[]{:S(2)}, u32[]{:S(2)}) collective-permute-start(bf16[3,256,384]{2,1,0:T(8,128)(2,1)} %get-tuple-element.83.refs_5_), channel_id=1, source_target_pairs={{0,16},{8,24},{16,0},{24,8},{1,17},{9,25},{17,1},{25,9},{2,18},{10... | collective-permute-start | bytes 1769480 | tf_op jit(solution)/shard_map/ppermute | solution.py:18
  6.5 0.0 collective-permute-start.1
  6.5 4.7 %shard_map.87 = (bf16[2,1024,128]{2,1,0:T(8,128)(2,1)}, bf16[8,128,1024]{2,1,0:T(8,128)(2,1)}, bf16[2,384,1024]{2,1,0:T(8,128)(2,1)}) custom-call(s32[1]{0:T(128)} %bitcast.1.me_ref, f32[3,2,1024]{2,1,0:T(2,128)} %bitcast.25, f32[3,8,1024]{2,1,0:T(8,128)} %bitcast.24, bf16[2,1024,384]{2,1,0:T(8,128)(2,1)} %basis_ref.3), custom_call_target="tpu_custom_call" | custom-call | tf_op jit(solution)/shard_map/pallas_call | solution.py:181
  11.2 12.7 %shard_map.88.refs_4_ = bf16[2,3,384,1024]{3,2,1,0:T(8,128)(2,1)} custom-call(s32[8]{0:T(128)} %get-tuple-element.79.order_ref.refs_0_, bf16[2,1024,128]{2,1,0:T(8,128)(2,1)} %get-tuple-element.81.test_ref, bf16[8,128,1024]{2,1,0:T(8,128)(2,1)} %get-tuple-element.87.source_ref, bf16[2,384,1024]{2,1,0:T(8,128)(2,1)} %get-tuple-element.84.basis_ref), custom_call_target="tpu_custom_call" | custom-call | flops 4831838208 | bytes 4718592 | tf_op jit(solution)/shard_map/pallas_call | solution.py:221
  23.9 0.0 collective-permute-done.refs_7_
  23.9 0.6 collective-permute-start.2
  24.5 0.0 collective-permute-done.1.refs_6_
  24.5 1.6 collective-permute-done.2.refs_8_
  26.1 0.8 copy-done.6
  26.9 6.9 %shard_map.89.first_ref = bf16[8,2,3,48,384]{4,3,2,1,0:T(8,128)(2,1)} custom-call(s32[8]{0:T(128)} %get-tuple-element.79.order_ref.refs_0_, s32[8]{0:T(128)} %refs_0_, s32[8]{0:T(128)} %get-tuple-element.80.refs_2_, s32[2]{0:T(128)} %refs_3_.3, bf16[2,3,384,1024]{3,2,1,0:T(8,128)(2,1)} %shard_map.88.refs_4_, bf16[3,256,384]{2,1,0:T(8,128)(2,1)} %get-tuple-element.83.refs_5_, ...), custom_call_target="tpu_custom_call" | custom-call | flops 1811939328 | bytes 6488064 | tf_op jit(solution)/shard_map/pallas_call | solution.py:323
  33.8 6.0 %all-to-all-start.2 = ((bf16[8,2,3,48,384]{4,3,2,1,0:T(8,128)(2,1)}), bf16[8,2,3,48,384]{4,3,2,1,0:T(8,128)(2,1)S(1)}, u32[]{:S(2)}, u32[]{:S(2)}) async-start(bf16[8,2,3,48,384]{4,3,2,1,0:T(8,128)(2,1)} %shard_map.89.first_ref), calls=%async_computation.2 | async-start | bytes 3538944 | tf_op jit(solution)/shard_map/all_to_all | solution.py:499
  39.8 0.5 collective-permute-start.4
  40.3 0.0 collective-permute-start.3
  40.3 23.4 %collective-permute-done.4.refs_7_ = bf16[5,256,384]{2,1,0:T(8,128)(2,1)} collective-permute-done((bf16[5,256,384]{2,1,0:T(8,128)(2,1)S(1)}, bf16[5,256,384]{2,1,0:T(8,128)(2,1)}, u32[]{:S(2)}, u32[]{:S(2)}) %collective-permute-start.4) | collective-permute-done | bytes 983072 | tf_op jit(solution)/shard_map/ppermute | solution.py:18
  63.7 0.0 collective-permute-start.5
  63.7 18.9 %shard_map.90.refs_4_ = bf16[2,5,384,1024]{3,2,1,0:T(8,128)(2,1)} custom-call(s32[8]{0:T(128)} %get-tuple-element.79.order_ref.refs_0_, bf16[2,1024,128]{2,1,0:T(8,128)(2,1)} %get-tuple-element.81.test_ref, bf16[8,128,1024]{2,1,0:T(8,128)(2,1)} %get-tuple-element.87.source_ref, bf16[2,384,1024]{2,1,0:T(8,128)(2,1)} %get-tuple-element.84.basis_ref), custom_call_target="tpu_custom_call" | custom-call | flops 8053063680 | bytes 7864320 | tf_op jit(solution)/shard_map/pallas_call | solution.py:221
  82.6 0.0 collective-permute-done.5.refs_8_
  82.6 11.4 %shard_map.91 = (bf16[8,2,5,48,384]{4,3,2,1,0:T(8,128)(2,1)}, bf16[8,2,48,1408]{3,2,1,0:T(8,128)(2,1)}, bf16[8,2,48,512]{3,2,1,0:T(8,128)(2,1)S(1)}) custom-call(s32[8]{0:T(128)} %get-tuple-element.79.order_ref.refs_0_, s32[8]{0:T(128)} %refs_0_, s32[8]{0:T(128)} %get-tuple-element.80.refs_2_, s32[2]{0:T(128)} %refs_3_.3, ...), custom_call_target="tpu_custom_call" | custom-call | flops 3019898880 | bytes 10813440 | tf_op jit(solution)/shard_map/pallas_call | solution.py:323
  94.1 0.0 all-to-all-done.2
  94.1 1.2 copy-done
  95.3 5.4 %all-to-all-start.3 = ((bf16[8,2,48,1408]{3,2,1,0:T(8,128)(2,1)}), bf16[8,2,48,1408]{3,2,1,0:T(8,128)(2,1)S(1)}, u32[]{:S(2)}, u32[]{:S(2)}) async-start(bf16[8,2,48,1408]{3,2,1,0:T(8,128)(2,1)} %get-tuple-element.90), calls=%async_computation.3 | async-start | bytes 4325376 | tf_op jit(solution)/shard_map/all_to_all | solution.py:506
  100.6 2.0 %collective-permute-start.6 = (s32[8]{0:T(128)S(1)}, s32[8]{0:T(128)S(1)}, u32[]{:S(2)}, u32[]{:S(2)}) collective-permute-start(s32[8]{0:T(128)S(1)} %copy-done.7), channel_id=1, source_target_pairs={{0,1},{1,0},{2,3},{3,2},{4,5},{5,4},{6,7},{7,6},{8,9},{9,8},{10,11... | collective-permute-start | bytes 104 | tf_op jit(solution)/shard_map/ppermute | solution.py:18
  102.7 16.2 %collective-permute-done.6.refs_1_ = s32[8]{0:T(128)S(1)} collective-permute-done((s32[8]{0:T(128)S(1)}, s32[8]{0:T(128)S(1)}, u32[]{:S(2)}, u32[]{:S(2)}) %collective-permute-start.6) | collective-permute-done | bytes 64 | tf_op jit(solution)/shard_map/ppermute | solution.py:18
  118.9 0.6 copy-done.10
  119.5 9.9 %shard_map.92 = (bf16[8,2,48,512]{3,2,1,0:T(8,128)(2,1)}, s32[16]{0:T(128)}) custom-call(s32[8]{0:T(128)} %get-tuple-element.79.order_ref.refs_0_, bf16[8,2,3,48,384]{4,3,2,1,0:T(8,128)(2,1)} %shard_map.89.first_ref, bf16[8,2,5,48,384]{4,3,2,1,0:T(8,128)(2,1)} %get-tuple-element.92.rest_ref, bf16[8,384,512]{2,1,0:T(8,128)(2,1)} %coeff_ref.1, s32[8]{0:T(128)} %refs_0_, ...), custom_call_target="tpu_custom_call" | custom-call | flops 2415919104 | bytes 4718592 | tf_op jit(solution)/shard_map/pallas_call | solution.py:374
  129.3 1.0 dynamic-slice_bitcast_fusion
  130.4 2.5 %collective-permute-start.10 = (bf16[4,2,48,512]{3,2,1,0:T(8,128)(2,1)S(1)}, bf16[4,2,48,512]{3,2,1,0:T(8,128)(2,1)}, u32[]{:S(2)}, u32[]{:S(2)}) collective-permute-start(bf16[4,2,48,512]{3,2,1,0:T(8,128)(2,1)S(1)} %dynamic-slice_bitcast_fusion), channel_id=1, source_target_pairs={{0,1},{1,0},{2,3},{3,2},{4,5},{5,4},{6,7},{7,6},{8,9},{9,8},{10,11... | collective-permute-start | bytes 1179656 | tf_op jit(solution)/shard_map/ppermute | solution.py:18
  132.9 12.9 %collective-permute-done.10 = bf16[4,2,48,512]{3,2,1,0:T(8,128)(2,1)} collective-permute-done((bf16[4,2,48,512]{3,2,1,0:T(8,128)(2,1)S(1)}, bf16[4,2,48,512]{3,2,1,0:T(8,128)(2,1)}, u32[]{:S(2)}, u32[]{:S(2)}) %collective-permute-start.10) | collective-permute-done | bytes 393248 | tf_op jit(solution)/shard_map/ppermute | solution.py:18
  145.7 1.2 fusion
  147.0 0.7 dynamic-slice_bitcast_fusion.3
  147.7 2.7 %collective-permute-start.11 = (bf16[2,48,512]{2,1,0:T(8,128)(2,1)}, bf16[2,48,512]{2,1,0:T(8,128)(2,1)S(1)}, u32[]{:S(2)}, u32[]{:S(2)}) collective-permute-start(bf16[2,48,512]{2,1,0:T(8,128)(2,1)} %get-tuple-element.101), channel_id=1, source_target_pairs={{0,2},{1,3},{2,0},{3,1},{4,6},{5,7},{6,4},{7,5},{8,10},{9,11},{10,... | collective-permute-start | bytes 294920 | tf_op jit(solution)/shard_map/ppermute | solution.py:18
  150.3 2.4 %collective-permute-start.12 = (bf16[2,48,512]{2,1,0:T(8,128)(2,1)}, bf16[2,48,512]{2,1,0:T(8,128)(2,1)S(1)}, u32[]{:S(2)}, u32[]{:S(2)}) collective-permute-start(bf16[2,48,512]{2,1,0:T(8,128)(2,1)} %get-tuple-element.103), channel_id=1, source_target_pairs={{0,4},{1,5},{2,6},{3,7},{4,0},{5,1},{6,2},{7,3},{8,12},{9,13},{10,... | collective-permute-start | bytes 294920 | tf_op jit(solution)/shard_map/ppermute | solution.py:18
  152.7 0.4 collective-permute-start.13
  153.1 0.7 collective-permute-start.7
  153.8 3.3 %collective-permute-start.8 = (s32[16]{0:T(128)}, s32[16]{0:T(128)S(1)}, u32[]{:S(2)}, u32[]{:S(2)}) collective-permute-start(s32[16]{0:T(128)} %get-tuple-element.94.refs_0_), channel_id=1, source_target_pairs={{0,4},{1,5},{2,6},{3,7},{4,0},{5,1},{6,2},{7,3},{8,12},{9,13},{10,... | collective-permute-start | bytes 200 | tf_op jit(solution)/shard_map/ppermute | solution.py:18
  157.1 3.2 %collective-permute-start.9 = (s32[16]{0:T(128)}, s32[16]{0:T(128)}, u32[]{:S(2)}, u32[]{:S(2)}) collective-permute-start(s32[16]{0:T(128)} %get-tuple-element.94.refs_0_), channel_id=1, source_target_pairs={{0,6},{1,7},{2,4},{3,5},{4,2},{5,3},{6,0},{7,1},{8,14},{9,15},{10,... | collective-permute-start | bytes 200 | tf_op jit(solution)/shard_map/ppermute | solution.py:18
  160.3 1.1 collective-permute-done.8.refs_2_
  161.5 0.6 copy-done.9
  162.1 0.7 collective-permute-done.9.refs_3_
  162.8 2.7 %shard_map.93 = (s32[64]{0:T(128)S(1)}, s32[64]{0:T(128)S(1)}, s32[64]{0:T(128)S(1)}, s32[1]{0:T(128)}) custom-call(s32[1]{0:T(128)} %bitcast.me_ref, s32[16]{0:T(128)} %get-tuple-element.94.refs_0_, s32[16]{0:T(128)} %copy-done.8, s32[16]{0:T(128)} %copy-done.9, s32[16]{0:T(128)} %collective-permute-done.9.refs_3_), custom_call_target="tpu_custom_call" | custom-call | tf_op jit(solution)/shard_map/pallas_call | solution.py:129
  166.1 0.0 collective-permute-done.11
  166.2 0.0 collective-permute-done.13
  166.2 1.6 fusion.3
  167.8 25.5 %conditional.1 = (bf16[2,48,64,384]{3,2,1,0:T(8,128)(2,1)}) conditional(s32[]{:T(128)} %bitcast.4, (s32[64]{0:T(128)S(1)}, s32[64]{0:T(128)S(1)}, s32[64]{0:T(128)S(1)}, bf16[8,2,3,48,384]{4,3,2,1,0:T(8,128)(2,1)}, bf16[8,2,48,1408]{3,2,1,0:T(8,128)(2,1)S(1)}) %tuple.35, (bf16[8,2,48,512]{3,2,1,0:T(8,128)(2,1)S(1)}, ...), branch_computations={%region_0.1_spmd, %region_1.2_spmd, %region_2.3_spmd} | conditional | flops 5898240 | bytes 14549028 | solution.py:526
  167.8 15.9 %all_to_all.18 = bf16[8,2,48,256]{3,2,1,0:T(8,128)(2,1)S(1)} all-to-all(bf16[8,2,48,256]{3,2,1,0:T(8,128)(2,1)S(1)} %slice.2), channel_id=1, replica_groups=mesh['test'=4,'src'=8] {'src'}, dimensions={0} | all-to-all | bytes 786432 | tf_op jit(solution)/shard_map/cond/branch_1_fun/all_to_all | solution.py:520
  183.7 1.7 pad_maximum_fusion.packed_ref
  185.4 7.8 %branch_1_fun.1 = bf16[2,48,64,384]{3,2,1,0:T(8,128)(2,1)} custom-call(s32[64]{0:T(128)S(1)} %get-tuple-element.43.order_ref, s32[64]{0:T(128)S(1)} %get-tuple-element.44.counts_ref, s32[64]{0:T(128)S(1)} %get-tuple-element.45.offsets_ref, bf16[8,2,3,48,384]{4,3,2,1,0:T(8,128)(2,1)S(1)} %copy-done.1, bf16[8,2,48,1664]{3,2,1,0:T(8,128)(2,1)} %pad_maximum_fusion.packed_ref), custom_call_target="tpu_custom_call" | custom-call | tf_op jit(solution)/shard_map/cond/branch_1_fun/pallas_call | solution.py:446
  (21 shorter events, 0.1 us)
Async XLA Ops:
  3.4 20.5 %collective-permute-start = (bf16[3,256,384]{2,1,0:T(8,128)(2,1)}, bf16[3,256,384]{2,1,0:T(8,128)(2,1)S(1)}, u32[]{:S(2)}, u32[]{:S(2)}) collective-permute-start(bf16[3,256,384]{2,1,0:T(8,128)(2,1)} %get-tuple-element.83.refs_5_), channel_id=1, source_target_pairs={{0,16},{8,24},{16,0},{24,8},{1,17},{9,25},{17,1},{25,9},{2,18},{10... | collective-permute-start | bytes 1769480 | tf_op jit(solution)/shard_map/ppermute | solution.py:18
  6.5 18.0 %collective-permute-start.1 = (bf16[3,256,384]{2,1,0:T(8,128)(2,1)}, bf16[3,256,384]{2,1,0:T(8,128)(2,1)S(1)}, u32[]{:S(2)}, u32[]{:S(2)}) collective-permute-start(bf16[3,256,384]{2,1,0:T(8,128)(2,1)} %get-tuple-element.83.refs_5_), channel_id=1, source_target_pairs={{0,8},{8,0},{16,24},{24,16},{1,9},{9,1},{17,25},{25,17},{2,10},{10... | collective-permute-start | bytes 1769480 | tf_op jit(solution)/shard_map/ppermute | solution.py:18
  23.9 2.2 %copy-start.4 = (bf16[3,256,384]{2,1,0:T(8,128)(2,1)}, bf16[3,256,384]{2,1,0:T(8,128)(2,1)S(1)}, u32[]{:S(2)}) copy-start(bf16[3,256,384]{2,1,0:T(8,128)(2,1)S(1)} %collective-permute-done.refs_7_) | copy-start | bytes 1769476
  23.9 2.2 %collective-permute-start.2 = (bf16[3,256,384]{2,1,0:T(8,128)(2,1)S(1)}, bf16[3,256,384]{2,1,0:T(8,128)(2,1)S(1)}, u32[]{:S(2)}, u32[]{:S(2)}) collective-permute-start(bf16[3,256,384]{2,1,0:T(8,128)(2,1)S(1)} %collective-permute-done.refs_7_), channel_id=1, source_target_pairs={{0,8},{8,0},{16,24},{24,16},{1,9},{9,1},{17,25},{25,17},{2,10},{10... | collective-permute-start | bytes 1769480 | tf_op jit(solution)/shard_map/ppermute | solution.py:18
  24.5 1.6 copy-start.5
  26.1 0.8 copy-start.6
  33.8 6.0 %copy-start.3 = (bf16[5,256,384]{2,1,0:T(8,128)(2,1)S(1)}, bf16[5,256,384]{2,1,0:T(8,128)(2,1)}, u32[]{:S(2)}) copy-start(bf16[5,256,384]{2,1,0:T(8,128)(2,1)} %get-tuple-element.89.refs_5_) | copy-start | bytes 2949124
  33.8 60.2 %all-to-all-start.2 = ((bf16[8,2,3,48,384]{4,3,2,1,0:T(8,128)(2,1)}), bf16[8,2,3,48,384]{4,3,2,1,0:T(8,128)(2,1)S(1)}, u32[]{:S(2)}, u32[]{:S(2)}) async-start(bf16[8,2,3,48,384]{4,3,2,1,0:T(8,128)(2,1)} %shard_map.89.first_ref), calls=%async_computation.2 | async-start | bytes 3538944 | tf_op jit(solution)/shard_map/all_to_all | solution.py:499
  39.8 23.9 %collective-permute-start.4 = (bf16[5,256,384]{2,1,0:T(8,128)(2,1)S(1)}, bf16[5,256,384]{2,1,0:T(8,128)(2,1)}, u32[]{:S(2)}, u32[]{:S(2)}) collective-permute-start(bf16[5,256,384]{2,1,0:T(8,128)(2,1)S(1)} %copy-done.3), channel_id=1, source_target_pairs={{0,16},{8,24},{16,0},{24,8},{1,17},{9,25},{17,1},{25,9},{2,18},{10... | collective-permute-start | bytes 2949128 | tf_op jit(solution)/shard_map/ppermute | solution.py:18
  40.3 42.3 %collective-permute-start.3 = (bf16[5,256,384]{2,1,0:T(8,128)(2,1)S(1)}, bf16[5,256,384]{2,1,0:T(8,128)(2,1)}, u32[]{:S(2)}, u32[]{:S(2)}) collective-permute-start(bf16[5,256,384]{2,1,0:T(8,128)(2,1)S(1)} %copy-done.3), channel_id=1, source_target_pairs={{0,8},{8,0},{16,24},{24,16},{1,9},{9,1},{17,25},{25,17},{2,10},{10... | collective-permute-start | bytes 2949128 | tf_op jit(solution)/shard_map/ppermute | solution.py:18
  63.7 18.9 %collective-permute-start.5 = (bf16[5,256,384]{2,1,0:T(8,128)(2,1)}, bf16[5,256,384]{2,1,0:T(8,128)(2,1)}, u32[]{:S(2)}, u32[]{:S(2)}) collective-permute-start(bf16[5,256,384]{2,1,0:T(8,128)(2,1)} %collective-permute-done.4.refs_7_), channel_id=1, source_target_pairs={{0,8},{8,0},{16,24},{24,16},{1,9},{9,1},{17,25},{25,17},{2,10},{10... | collective-permute-start | bytes 2949128 | tf_op jit(solution)/shard_map/ppermute | solution.py:18
  94.1 6.6 %copy-start.7 = (s32[8]{0:T(128)S(1)}, s32[8]{0:T(128)}, u32[]{:S(2)}) copy-start(s32[8]{0:T(128)} %refs_0_) | copy-start | bytes 100
  94.1 1.2 copy-start
  95.3 72.5 %all-to-all-start.3 = ((bf16[8,2,48,1408]{3,2,1,0:T(8,128)(2,1)}), bf16[8,2,48,1408]{3,2,1,0:T(8,128)(2,1)S(1)}, u32[]{:S(2)}, u32[]{:S(2)}) async-start(bf16[8,2,48,1408]{3,2,1,0:T(8,128)(2,1)} %get-tuple-element.90), calls=%async_computation.3 | async-start | bytes 4325376 | tf_op jit(solution)/shard_map/all_to_all | solution.py:506
  100.6 18.2 %collective-permute-start.6 = (s32[8]{0:T(128)S(1)}, s32[8]{0:T(128)S(1)}, u32[]{:S(2)}, u32[]{:S(2)}) collective-permute-start(s32[8]{0:T(128)S(1)} %copy-done.7), channel_id=1, source_target_pairs={{0,1},{1,0},{2,3},{3,2},{4,5},{5,4},{6,7},{7,6},{8,9},{9,8},{10,11... | collective-permute-start | bytes 104 | tf_op jit(solution)/shard_map/ppermute | solution.py:18
  118.9 0.6 copy-start.10
  130.4 15.4 %collective-permute-start.10 = (bf16[4,2,48,512]{3,2,1,0:T(8,128)(2,1)S(1)}, bf16[4,2,48,512]{3,2,1,0:T(8,128)(2,1)}, u32[]{:S(2)}, u32[]{:S(2)}) collective-permute-start(bf16[4,2,48,512]{3,2,1,0:T(8,128)(2,1)S(1)} %dynamic-slice_bitcast_fusion), channel_id=1, source_target_pairs={{0,1},{1,0},{2,3},{3,2},{4,5},{5,4},{6,7},{7,6},{8,9},{9,8},{10,11... | collective-permute-start | bytes 1179656 | tf_op jit(solution)/shard_map/ppermute | solution.py:18
  147.7 18.5 %collective-permute-start.11 = (bf16[2,48,512]{2,1,0:T(8,128)(2,1)}, bf16[2,48,512]{2,1,0:T(8,128)(2,1)S(1)}, u32[]{:S(2)}, u32[]{:S(2)}) collective-permute-start(bf16[2,48,512]{2,1,0:T(8,128)(2,1)} %get-tuple-element.101), channel_id=1, source_target_pairs={{0,2},{1,3},{2,0},{3,1},{4,6},{5,7},{6,4},{7,5},{8,10},{9,11},{10,... | collective-permute-start | bytes 294920 | tf_op jit(solution)/shard_map/ppermute | solution.py:18
  150.3 15.8 %collective-permute-start.12 = (bf16[2,48,512]{2,1,0:T(8,128)(2,1)}, bf16[2,48,512]{2,1,0:T(8,128)(2,1)S(1)}, u32[]{:S(2)}, u32[]{:S(2)}) collective-permute-start(bf16[2,48,512]{2,1,0:T(8,128)(2,1)} %get-tuple-element.103), channel_id=1, source_target_pairs={{0,4},{1,5},{2,6},{3,7},{4,0},{5,1},{6,2},{7,3},{8,12},{9,13},{10,... | collective-permute-start | bytes 294920 | tf_op jit(solution)/shard_map/ppermute | solution.py:18
  152.7 13.5 %collective-permute-start.13 = (bf16[2,48,512]{2,1,0:T(8,128)(2,1)}, bf16[2,48,512]{2,1,0:T(8,128)(2,1)}, u32[]{:S(2)}, u32[]{:S(2)}) collective-permute-start(bf16[2,48,512]{2,1,0:T(8,128)(2,1)} %get-tuple-element.102), channel_id=1, source_target_pairs={{0,6},{1,7},{2,4},{3,5},{4,2},{5,3},{6,0},{7,1},{8,14},{9,15},{10,... | collective-permute-start | bytes 294920 | tf_op jit(solution)/shard_map/ppermute | solution.py:18
  153.1 4.0 %collective-permute-start.7 = (s32[16]{0:T(128)}, s32[16]{0:T(128)S(1)}, u32[]{:S(2)}, u32[]{:S(2)}) collective-permute-start(s32[16]{0:T(128)} %get-tuple-element.94.refs_0_), channel_id=1, source_target_pairs={{0,2},{1,3},{2,0},{3,1},{4,6},{5,7},{6,4},{7,5},{8,10},{9,11},{10,... | collective-permute-start | bytes 200 | tf_op jit(solution)/shard_map/ppermute | solution.py:18
  153.8 7.7 %collective-permute-start.8 = (s32[16]{0:T(128)}, s32[16]{0:T(128)S(1)}, u32[]{:S(2)}, u32[]{:S(2)}) collective-permute-start(s32[16]{0:T(128)} %get-tuple-element.94.refs_0_), channel_id=1, source_target_pairs={{0,4},{1,5},{2,6},{3,7},{4,0},{5,1},{6,2},{7,3},{8,12},{9,13},{10,... | collective-permute-start | bytes 200 | tf_op jit(solution)/shard_map/ppermute | solution.py:18
  157.1 5.7 %copy-start.8 = (s32[16]{0:T(128)}, s32[16]{0:T(128)S(1)}, u32[]{:S(2)}) copy-start(s32[16]{0:T(128)S(1)} %collective-permute-done.7.refs_1_) | copy-start | bytes 196
  157.1 5.7 %collective-permute-start.9 = (s32[16]{0:T(128)}, s32[16]{0:T(128)}, u32[]{:S(2)}, u32[]{:S(2)}) collective-permute-start(s32[16]{0:T(128)} %get-tuple-element.94.refs_0_), channel_id=1, source_target_pairs={{0,6},{1,7},{2,4},{3,5},{4,2},{5,3},{6,0},{7,1},{8,14},{9,15},{10,... | collective-permute-start | bytes 200 | tf_op jit(solution)/shard_map/ppermute | solution.py:18
  161.5 0.6 copy-start.9
  167.8 17.6 %copy-start.1 = (bf16[8,2,3,48,384]{4,3,2,1,0:T(8,128)(2,1)S(1)}, bf16[8,2,3,48,384]{4,3,2,1,0:T(8,128)(2,1)}, u32[]{:S(2)}) copy-start(bf16[8,2,3,48,384]{4,3,2,1,0:T(8,128)(2,1)} %get-tuple-element.46.whole_ref) | copy-start | bytes 5308420 | tf_op jit(solution)/shard_map/cond

commit v2 on v1

--- a/solution.py
+++ b/solution.py
@@ -135,71 +135,61 @@
     )(me, *groups)
 
 
-def features_kernel(nshard, me_ref, test_ref, source_ref, basis_ref, test_out_ref, source_out_ref, basis_out_ref, rows_ref):
-    part = source_ref.shape[2] // nshard
-
+NFEATURE = 128
+
+
+def fill_features(rows_ref, points, is_test):
     def three_terms(x):
         high = x.astype(jnp.bfloat16).astype(jnp.float32)
         middle = (x - high).astype(jnp.bfloat16).astype(jnp.float32)
         return high, middle, x - high - middle
 
-    def fill(centred, is_test):
-        norm = jnp.sum(centred * centred, axis=0, keepdims=True)
-        terms = three_terms(centred)
-        norms = three_terms(norm + softening if is_test else norm)
-        for a in range(3):
-            for b in range(3):
-                place = 3 * (3 * a + b)
-                rows_ref[place : place + 3, :] = -2.0 * terms[a] if is_test else terms[b]
-        for a in range(3):
-            rows_ref[27 + a : 28 + a, :] = norms[a] if is_test else jnp.ones_like(norm)
-            rows_ref[30 + a : 31 + a, :] = jnp.ones_like(norm) if is_test else norms[a]
-        return rows_ref[...]
-
-    rows_ref[...] = jnp.zeros_like(rows_ref)
-    for i in range(test_ref.shape[1]):
-        rows = fill(test_ref[:, i, :] - 0.5, True)
-        test_out_ref[i] = rows.T.astype(jnp.bfloat16)
-        basis_out_ref[i] = basis_ref[i].T
-    for j in range(source_ref.shape[1]):
-        pieces = []
-        for offset in range(nshard):
-            start = pl.multiple_of((me_ref[0] ^ offset) * part, part)
-            pieces.append(source_ref[:, j, pl.ds(start, part)])
-        rows = fill(jnp.concatenate(pieces, axis=1) - 0.5, False)
-        source_out_ref[j] = rows.astype(jnp.bfloat16)
-
-
-NFEATURE = 128
-
-
-def distance_features(nshard, me, test_points, source_points, test_basis):
-    ntest, _, npoint = test_points.shape
-    nsource, _, nq = source_points.shape
-    kmax = test_basis.shape[2]
-    smem, vmem = pl.BlockSpec(memory_space=pltpu.SMEM), pl.BlockSpec(memory_space=pltpu.VMEM)
-    return pl.pallas_call(
-        functools.partial(features_kernel, nshard),
-        out_shape=(
-            jax.ShapeDtypeStruct((ntest, npoint, NFEATURE), jnp.bfloat16),
-            jax.ShapeDtypeStruct((nsource, NFEATURE, nq), jnp.bfloat16),
-            jax.ShapeDtypeStruct((ntest, kmax, npoint), jnp.bfloat16),
-        ),
-        in_specs=[smem, vmem, vmem, vmem],
-        out_specs=(vmem, vmem, vmem),
-        scratch_shapes=[pltpu.VMEM((NFEATURE, max(npoint, nq)), jnp.float32)],
-        compiler_params=pltpu.CompilerParams(vmem_limit_bytes=VMEM_LIMIT),
-    )(me, test_points.transpose(1, 0, 2), source_points.transpose(1, 0, 2), test_basis)
-
-
-def left_kernel(order_ref, test_ref, source_ref, basis_ref, out_ref):
+    centred = points - 0.5
+    norm = jnp.sum(centred * centred, axis=0, keepdims=True)
+    terms = three_terms(centred)
+    norms = three_terms(norm + softening if is_test else norm)
+    for a in range(3):
+        for b in range(3):
+            place = 3 * (3 * a + b)
+            rows_ref[place : place + 3, :] = -2.0 * terms[a] if is_test else terms[b]
+    for a in range(3):
+        rows_ref[27 + a : 28 + a, :] = norms[a] if is_test else jnp.ones_like(norm)
+        rows_ref[30 + a : 31 + a, :] = jnp.ones_like(norm) if is_test else norms[a]
+
+
+def left_kernel(
+    nshard, first, me_ref, order_ref, test_ref, source_ref, basis_ref, out_ref,
+    rows_ref, features_ref, turned_ref, near_ref,
+):
+    j = pl.program_id(0)
+    ntest = test_ref.shape[1]
     nq = source_ref.shape[2]
+    part = nq // nshard
     block = min(QBLOCK, nq)
-    steps = [(i, start) for i in range(test_ref.shape[0]) for start in range(0, nq, block)]
+
+    @pl.when(j == 0)
+    def _():
+        rows_ref[...] = jnp.zeros_like(rows_ref)
+        for i in range(ntest):
+            fill_features(rows_ref, test_ref[:, i, :], True)
+            features_ref[i] = rows_ref[...].T.astype(jnp.bfloat16)
+            turned_ref[i] = basis_ref[i].T
+
+    source = order_ref[first + j]
+    for comp in range(3):
+        rows_ref[comp : comp + 1, :] = source_ref[comp, pl.ds(source, 1), :]
+    pieces = []
+    for offset in range(nshard):
+        start = pl.multiple_of((me_ref[0] ^ offset) * part, part)
+        pieces.append(rows_ref[0:3, pl.ds(start, part)])
+    fill_features(rows_ref, jnp.concatenate(pieces, axis=1), False)
+    near_ref[...] = rows_ref[...].astype(jnp.bfloat16)
+
+    steps = [(i, start) for i in range(ntest) for start in range(0, nq, block)]
 
     def kernel_block(i, start):
         squared = jnp.dot(
-            test_ref[i], source_ref[0, :, start : start + block], preferred_element_type=jnp.float32
+            features_ref[i], near_ref[:, start : start + block], preferred_element_type=jnp.float32
         )
         return lax.rsqrt(squared.astype(jnp.bfloat16))
 
@@ -209,26 +199,32 @@
         if place + 1 < len(steps):
             ready = kernel_block(*steps[place + 1])
         out_ref[i, 0, :, start : start + block] = jnp.dot(
-            basis_ref[i], now, preferred_element_type=jnp.float32
+            turned_ref[i], now, preferred_element_type=jnp.float32
         ).astype(jnp.bfloat16)
 
 
-def left_products(order, test_features, source_features, basis_rows, first, last):
-    ntest, npoint, nfeature = test_features.shape
-    nq = source_features.shape[2]
-    kmax = basis_rows.shape[1]
+def left_products(nshard, me, order, test_points, source_points, test_basis, first, last):
+    _, ntest, npoint = test_points.shape
+    nall, nq = source_points.shape[1:]
+    kmax = test_basis.shape[2]
     nsource = last - first
     return pl.pallas_call(
-        left_kernel,
+        functools.partial(left_kernel, nshard, first),
         grid_spec=pltpu.PrefetchScalarGridSpec(
-            num_scalar_prefetch=1,
+            num_scalar_prefetch=2,
             grid=(nsource,),
             in_specs=[
-                pl.BlockSpec((ntest, npoint, nfeature), lambda j, order: (0, 0, 0)),
-                pl.BlockSpec((1, nfeature, nq), lambda j, order: (order[first + j], 0, 0)),
-                pl.BlockSpec((ntest, kmax, npoint), lambda j, order: (0, 0, 0)),
+                pl.BlockSpec((3, ntest, npoint), lambda j, *_: (0, 0, 0)),
+                pl.BlockSpec((3, nall, nq), lambda j, *_: (0, 0, 0)),
+                pl.BlockSpec((ntest, npoint, kmax), lambda j, *_: (0, 0, 0)),
             ],
-            out_specs=pl.BlockSpec((ntest, 1, kmax, nq), lambda j, order: (0, j, 0, 0)),
+            out_specs=pl.BlockSpec((ntest, 1, kmax, nq), lambda j, *_: (0, j, 0, 0)),
+            scratch_shapes=[
+                pltpu.VMEM((NFEATURE, npoint), jnp.float32),
+                pltpu.VMEM((ntest, npoint, NFEATURE), jnp.bfloat16),
+                pltpu.VMEM((ntest, kmax, npoint), jnp.bfloat16),
+                pltpu.VMEM((NFEATURE, nq), jnp.bfloat16),
+            ],
         ),
         out_shape=jax.ShapeDtypeStruct((ntest, nsource, kmax, nq), jnp.bfloat16),
         compiler_params=pltpu.CompilerParams(vmem_limit_bytes=VMEM_LIMIT),
@@ -237,7 +233,7 @@
             bytes_accessed=2 * ntest * nsource * kmax * nq,
             transcendentals=ntest * nsource * npoint * nq,
         ),
-    )(order, test_features, source_features, basis_rows)
+    )(me, order, test_points, source_points, test_basis)
 
 
 def tile_kernel(nshard, first, packed, *refs):
@@ -470,17 +466,21 @@
     me_test = lax.axis_index("test")
     cut = max(1, nsource * 3 // 8)
 
+    held = {}
+
     def gather(name, shard, left):
         got = {0: shard}
         bits = list(bits_down(ntest_axis))
         for bit in bits:
-            if bit == bits[-1] and name == "a":
+            if bit == bits[-1]:
                 names = [o for o in got if o != 0]
                 tied = lax.optimization_barrier(tuple(got[o] for o in names) + (left,))
                 got.update(zip(names, tied[:-1]))
                 left = tied[-1]
             for offset in list(got):
                 got[offset ^ bit] = exchange(got[offset], "test", bit)
+            if bit == bits[0]:
+                held[name] = got[bit]
         return [got[offset] for offset in sorted(got)], left
 
     most = (nsource - cut) * kmax
@@ -489,26 +489,25 @@
 
     order, offsets, basis_a, basis_b = pick(cut, source_counts, source_basis)
     tables = (order, source_counts, offsets)
-    test_features, source_features, basis_rows = distance_features(
-        ntest_axis, jnp.reshape(me_test, (1,)), test_points, source_points, test_basis
-    )
-
-    left_a = left_products(order, test_features, source_features, basis_rows, 0, cut)
+    me = jnp.reshape(me_test, (1,))
+    test_points, source_points = test_points.transpose(1, 0, 2), source_points.transpose(1, 0, 2)
+
+    left_a = left_products(ntest_axis, me, order, test_points, source_points, test_basis, 0, cut)
     shards_a, left_a = gather("a", basis_a, left_a)
+    inner = max(1, nsrc // 4)
+    near = [exchange(source_counts, "src", flip) for flip in range(1, inner)]
+    *near, left_a = lax.optimization_barrier((*near, left_a))
     (tiles_a,) = tiles(nsrc, 0, tables, test_counts, left_a, shards_a, None)
     moved_a = lax.all_to_all(tiles_a, "src", split_axis=0, concat_axis=0, tiled=True)
 
-    rest, _ = lax.optimization_barrier((basis_b, source_features))
-    features_b, _ = lax.optimization_barrier((source_features, tiles_a))
-    left_b = left_products(order, test_features, features_b, basis_rows, cut, nsource)
+    rest, _ = lax.optimization_barrier((basis_b, held["a"]))
+    later, _ = lax.optimization_barrier((source_points, tiles_a))
+    left_b = left_products(ntest_axis, me, order, test_points, later, test_basis, cut, nsource)
     shards_b, left_b = gather("b", rest, left_b)
     tiles_b, packed, beyond = tiles(nsrc, cut, tables, test_counts, left_b, shards_b, main)
     moved_b = lax.all_to_all(packed, "src", split_axis=0, concat_axis=0, tiled=True)
 
-    inner = max(1, nsrc // 4)
-    counts, _ = lax.optimization_barrier((source_counts, tiles_a))
-    near = [counts] + [exchange(counts, "src", flip) for flip in range(1, inner)]
-    sums, joined = project(order, tiles_a, tiles_b, coefficients, near)
+    sums, joined = project(order, tiles_a, tiles_b, coefficients, [source_counts] + near)
     groups = [joined] + [exchange(joined, "src", flip) for flip in range(inner, nsrc, inner)]
     projected = sum_rows(sums, "src")
     me_src, _ = lax.optimization_barrier((jnp.reshape(lax.axis_index("src"), (1,)), packed))

time: 194 us -> 156 us (0.80)
  waiting for transfers between devices: 55.9 us -> 38.9 us
  blocking collectives: 15.9 us -> 0 us
  Pallas kernels: 77.9 us -> 73.1 us
    ppermute x14, waiting for transfers between devices: 55.9 us -> 34.3 us  [exchange(): return lax.ppermute(x, axis, [(a, a ^ flip) for a in range(size)])]
    all_to_all x1 -> x0, blocking collectives: 15.9 us -> none  [finish(): lax.all_to_all(beyond[..., :width - main], 'src', split_axis=0, concat_ax...]
    all_to_all x1, waiting for transfers between devices: 0.01 us -> 4.58 us  [body(): lax.all_to_all(tiles_a, 'src', split_axis=0, concat_axis=0, tiled=True)]
    pallas_call x3 -> x2, Pallas kernels: 36.4 us -> 33.4 us  [left_products(): pl.pallas_call(functools.partial(left_kernel, nshard, first), grid_spec=p...]
    ppermute x14, starting transfers between devices: 21.3 us -> 23.8 us  [exchange(): return lax.ppermute(x, axis, [(a, a ^ flip) for a in range(size)])]
  transfers between devices with their start and end apart: 16 -> 16, of which waited for: 6 -> 6; matrix products, arithmetic and copies ran while one was open for 2% -> 3% of each run, Pallas kernels for 31% -> 36%
where the time goes in v2:
time: 156 us; the launch traced here: 155 us
  Pallas kernels  73.1 us (47%)
  waiting for transfers between devices  38.9 us (25%)
  starting transfers between devices  34.1 us (22%)
  local copies, waits for them, and re-layouts  4.51 us (3%)
  other arithmetic  2.81 us (2%)
    ppermute x14, waiting for transfers between devices, exchange(): return lax.ppermute(x, axis, [(a, a ^ flip) for a in range(size)])  34.3 us
    pallas_call x2, Pallas kernels, left_products(): pl.pallas_call(functools.partial(left_kernel, nshard, first), grid_spec=p...  33.4 us
    ppermute x14, starting transfers between devices, exchange(): return lax.ppermute(x, axis, [(a, a ^ flip) for a in range(size)])  23.8 us
    pallas_call x2, Pallas kernels, tiles(): pl.pallas_call(functools.partial(tile_kernel, nshard, first, packed), gri...  16.7 us
    pallas_call x1, Pallas kernels, project(): pl.pallas_call(functools.partial(project_kernel, cut), grid_spec=pltpu.Pr...  9.87 us
    pallas_call x1, Pallas kernels, unpack(): pl.pallas_call(functools.partial(unpack_kernel, cut), grid_spec=pltpu.Pre...  7.58 us
    all_to_all x1, starting transfers between devices, body(): lax.all_to_all(tiles_a, 'src', split_axis=0, concat_axis=0, tiled=True)  6.51 us
    all_to_all x1, waiting for transfers between devices, body(): lax.all_to_all(tiles_a, 'src', split_axis=0, concat_axis=0, tiled=True)  4.58 us
  transfers between devices with their start and end apart: 16, of which 6 were waited for; matrix products, arithmetic and copies ran while one was open for 3% of the time, Pallas kernels for 36%

profile of v2, /device:TPU:0, one launch (start us, length us, event | category | flops | bytes accessed | tf_op | source)
XLA Modules:
  0.0 154.8 jit_solution(8105744462183644773)
XLA Ops:
  0.6 2.9 %shard_map.86 = (s32[8]{0:T(128)}, s32[8]{0:T(128)}, bf16[3,256,384]{2,1,0:T(8,128)(2,1)}, bf16[5,256,384]{2,1,0:T(8,128)(2,1)}) custom-call(s32[8]{0:T(128)} %refs_0_.1, bf16[8,256,384]{2,1,0:T(8,128)(2,1)} %basis_ref.3), custom_call_target="tpu_custom_call" | custom-call | tf_op jit(solution)/shard_map/pallas_call | solution.py:84
  3.5 3.0 %collective-permute-start = (bf16[3,256,384]{2,1,0:T(8,128)(2,1)}, bf16[3,256,384]{2,1,0:T(8,128)(2,1)S(1)}, u32[]{:S(2)}, u32[]{:S(2)}) collective-permute-start(bf16[3,256,384]{2,1,0:T(8,128)(2,1)} %get-tuple-element.82.refs_5_), channel_id=1, source_target_pairs={{0,16},{8,24},{16,0},{24,8},{1,17},{9,25},{17,1},{25,9},{2,18},{10... | collective-permute-start | bytes 1769480 | tf_op jit(solution)/shard_map/ppermute | solution.py:18
  6.5 0.0 collective-permute-start.3
  6.5 13.6 %shard_map.87.refs_4_ = bf16[2,3,384,1024]{3,2,1,0:T(8,128)(2,1)} custom-call(s32[1]{0:T(128)} %bitcast.1.me_ref, s32[8]{0:T(128)} %get-tuple-element.79.order_ref.refs_0_, f32[3,2,1024]{2,1,0:T(2,128)} %bitcast.26, f32[3,8,1024]{2,1,0:T(8,128)} %bitcast.24, bf16[2,1024,384]{2,1,0:T(8,128)(2,1)} %basis_ref.5), custom_call_target="tpu_custom_call" | custom-call | flops 4831838208 | bytes 4718592 | tf_op jit(solution)/shard_map/pallas_call | solution.py:211
  20.1 0.0 collective-permute-done.refs_7_
  20.1 0.5 collective-permute-start.4
  20.7 1.5 collective-permute-start.2
  22.2 2.0 %collective-permute-done.2.refs_1_ = s32[8]{0:T(128)S(1)} collective-permute-done((s32[8]{0:T(128)S(1)}, s32[8]{0:T(128)S(1)}, u32[]{:S(2)}, u32[]{:S(2)}) %collective-permute-start.2) | collective-permute-done | bytes 64 | tf_op jit(solution)/shard_map/ppermute | solution.py:18
  24.2 0.0 collective-permute-done.3.refs_6_
  24.2 0.0 collective-permute-done.4.refs_8_
  24.2 0.8 copy-done.5
  25.0 0.2 copy-done.6
  25.2 6.3 %shard_map.88.first_ref = bf16[8,2,3,48,384]{4,3,2,1,0:T(8,128)(2,1)} custom-call(s32[8]{0:T(128)} %get-tuple-element.79.order_ref.refs_0_, s32[8]{0:T(128)} %refs_0_.1, s32[8]{0:T(128)} %get-tuple-element.80.refs_2_, s32[2]{0:T(128)} %refs_3_.3, bf16[2,3,384,1024]{3,2,1,0:T(8,128)(2,1)} %shard_map.87.refs_4_, ...), custom_call_target="tpu_custom_call" | custom-call | flops 1811939328 | bytes 6488064 | tf_op jit(solution)/shard_map/pallas_call | solution.py:319
  31.6 6.5 %all-to-all-start.2 = ((bf16[8,2,3,48,384]{4,3,2,1,0:T(8,128)(2,1)}), bf16[8,2,3,48,384]{4,3,2,1,0:T(8,128)(2,1)S(1)}, u32[]{:S(2)}, u32[]{:S(2)}) async-start(bf16[8,2,3,48,384]{4,3,2,1,0:T(8,128)(2,1)} %shard_map.88.first_ref), calls=%async_computation.2 | async-start | bytes 3538944 | tf_op jit(solution)/shard_map/all_to_all | solution.py:501
  38.1 1.3 collective-permute-start.1
  39.4 0.0 collective-permute-start.5
  39.4 19.8 %shard_map.89.refs_4_ = bf16[2,5,384,1024]{3,2,1,0:T(8,128)(2,1)} custom-call(s32[1]{0:T(128)} %bitcast.1.me_ref, s32[8]{0:T(128)} %get-tuple-element.79.order_ref.refs_0_, f32[3,2,1024]{2,1,0:T(2,128)} %bitcast.27, f32[3,8,1024]{2,1,0:T(8,128)} %bitcast.25, bf16[2,1024,384]{2,1,0:T(8,128)(2,1)} %basis_ref.5), custom_call_target="tpu_custom_call" | custom-call | flops 8053063680 | bytes 7864320 | tf_op jit(solution)/shard_map/pallas_call | solution.py:211
  59.2 1.5 collective-permute-done.1.refs_7_
  60.6 0.0 collective-permute-start.6
  60.6 0.0 collective-permute-done.5.refs_6_
  60.7 2.9 %collective-permute-done.6.refs_8_ = bf16[5,256,384]{2,1,0:T(8,128)(2,1)} collective-permute-done((bf16[5,256,384]{2,1,0:T(8,128)(2,1)}, bf16[5,256,384]{2,1,0:T(8,128)(2,1)}, u32[]{:S(2)}, u32[]{:S(2)}) %collective-permute-start.6) | collective-permute-done | bytes 983072 | tf_op jit(solution)/shard_map/ppermute | solution.py:18
  63.6 10.3 %shard_map.90 = (bf16[8,2,5,48,384]{4,3,2,1,0:T(8,128)(2,1)}, bf16[8,2,48,1408]{3,2,1,0:T(8,128)(2,1)}, bf16[8,2,48,512]{3,2,1,0:T(8,128)(2,1)S(1)}) custom-call(s32[8]{0:T(128)} %get-tuple-element.79.order_ref.refs_0_, s32[8]{0:T(128)} %refs_0_.1, s32[8]{0:T(128)} %get-tuple-element.80.refs_2_, s32[2]{0:T(128)} %refs_3_.3, ...), custom_call_target="tpu_custom_call" | custom-call | flops 3019898880 | bytes 10813440 | tf_op jit(solution)/shard_map/pallas_call | solution.py:319
  73.9 4.6 %all-to-all-done.2 = bf16[8,2,3,48,384]{4,3,2,1,0:T(8,128)(2,1)S(1)} async-done(((bf16[8,2,3,48,384]{4,3,2,1,0:T(8,128)(2,1)}), bf16[8,2,3,48,384]{4,3,2,1,0:T(8,128)(2,1)S(1)}, u32[]{:S(2)}, u32[]{:S(2)}) %all-to-all-start.2) | async-done | bytes 1769504 | tf_op jit(solution)/shard_map/all_to_all | solution.py:501
  78.5 1.2 copy-done
  79.7 3.8 %all-to-all-start.3 = ((bf16[8,2,48,1408]{3,2,1,0:T(8,128)(2,1)}), bf16[8,2,48,1408]{3,2,1,0:T(8,128)(2,1)S(1)}, u32[]{:S(2)}, u32[]{:S(2)}) async-start(bf16[8,2,48,1408]{3,2,1,0:T(8,128)(2,1)} %get-tuple-element.90), calls=%async_computation.3 | async-start | bytes 4325376 | tf_op jit(solution)/shard_map/all_to_all | solution.py:508
  83.5 9.9 %shard_map.91 = (bf16[8,2,48,512]{3,2,1,0:T(8,128)(2,1)}, s32[16]{0:T(128)}) custom-call(s32[8]{0:T(128)} %get-tuple-element.79.order_ref.refs_0_, bf16[8,2,3,48,384]{4,3,2,1,0:T(8,128)(2,1)} %shard_map.88.first_ref, bf16[8,2,5,48,384]{4,3,2,1,0:T(8,128)(2,1)} %get-tuple-element.92.rest_ref, bf16[8,384,512]{2,1,0:T(8,128)(2,1)} %coeff_ref.1, s32[8]{0:T(128)} %refs_0_.1, ...), custom_call_target="tpu_custom_call" | custom-call | flops 2415919104 | bytes 4718592 | tf_op jit(solution)/shard_map/pallas_call | solution.py:370
  93.4 1.0 dynamic-slice_bitcast_fusion
  94.4 1.9 %collective-permute-start.10 = (bf16[4,2,48,512]{3,2,1,0:T(8,128)(2,1)S(1)}, bf16[4,2,48,512]{3,2,1,0:T(8,128)(2,1)}, u32[]{:S(2)}, u32[]{:S(2)}) collective-permute-start(bf16[4,2,48,512]{3,2,1,0:T(8,128)(2,1)S(1)} %dynamic-slice_bitcast_fusion), channel_id=1, source_target_pairs={{0,1},{1,0},{2,3},{3,2},{4,5},{5,4},{6,7},{7,6},{8,9},{9,8},{10,11... | collective-permute-start | bytes 1179656 | tf_op jit(solution)/shard_map/ppermute | solution.py:18
  96.3 21.5 %collective-permute-done.10 = bf16[4,2,48,512]{3,2,1,0:T(8,128)(2,1)} collective-permute-done((bf16[4,2,48,512]{3,2,1,0:T(8,128)(2,1)S(1)}, bf16[4,2,48,512]{3,2,1,0:T(8,128)(2,1)}, u32[]{:S(2)}, u32[]{:S(2)}) %collective-permute-start.10) | collective-permute-done | bytes 393248 | tf_op jit(solution)/shard_map/ppermute | solution.py:18
  117.8 1.2 fusion
  119.0 0.7 dynamic-slice_bitcast_fusion.3
  119.7 0.0 collective-permute-start.11
  119.7 7.9 %collective-permute-start.12 = (bf16[2,48,512]{2,1,0:T(8,128)(2,1)}, bf16[2,48,512]{2,1,0:T(8,128)(2,1)S(1)}, u32[]{:S(2)}, u32[]{:S(2)}) collective-permute-start(bf16[2,48,512]{2,1,0:T(8,128)(2,1)} %get-tuple-element.103), channel_id=1, source_target_pairs={{0,4},{1,5},{2,6},{3,7},{4,0},{5,1},{6,2},{7,3},{8,12},{9,13},{10,... | collective-permute-start | bytes 294920 | tf_op jit(solution)/shard_map/ppermute | solution.py:18
  127.6 0.0 collective-permute-start.13
  127.6 0.6 collective-permute-start.7
  128.2 3.8 %collective-permute-start.8 = (s32[16]{0:T(128)}, s32[16]{0:T(128)S(1)}, u32[]{:S(2)}, u32[]{:S(2)}) collective-permute-start(s32[16]{0:T(128)} %get-tuple-element.94.refs_0_), channel_id=1, source_target_pairs={{0,4},{1,5},{2,6},{3,7},{4,0},{5,1},{6,2},{7,3},{8,12},{9,13},{10,... | collective-permute-start | bytes 200 | tf_op jit(solution)/shard_map/ppermute | solution.py:18
  132.0 0.0 collective-permute-done.7.refs_1_
  132.0 3.2 %collective-permute-start.9 = (s32[16]{0:T(128)}, s32[16]{0:T(128)}, u32[]{:S(2)}, u32[]{:S(2)}) collective-permute-start(s32[16]{0:T(128)} %get-tuple-element.94.refs_0_), channel_id=1, source_target_pairs={{0,6},{1,7},{2,4},{3,5},{4,2},{5,3},{6,0},{7,1},{8,14},{9,15},{10,... | collective-permute-start | bytes 200 | tf_op jit(solution)/shard_map/ppermute | solution.py:18
  135.3 6.4 %collective-permute-done.8.refs_2_ = s32[16]{0:T(128)S(1)} collective-permute-done((s32[16]{0:T(128)}, s32[16]{0:T(128)S(1)}, u32[]{:S(2)}, u32[]{:S(2)}) %collective-permute-start.8) | collective-permute-done | bytes 96 | tf_op jit(solution)/shard_map/ppermute | solution.py:18
  141.7 0.5 copy-done.9
  142.2 0.0 collective-permute-done.9.refs_3_
  142.2 2.8 %shard_map.92 = (s32[64]{0:T(128)S(1)}, s32[64]{0:T(128)S(1)}, s32[64]{0:T(128)S(1)}, s32[1]{0:T(128)}) custom-call(s32[1]{0:T(128)} %bitcast.me_ref, s32[16]{0:T(128)} %get-tuple-element.94.refs_0_, s32[16]{0:T(128)} %copy-done.8, s32[16]{0:T(128)} %copy-done.9, s32[16]{0:T(128)} %collective-permute-done.9.refs_3_), custom_call_target="tpu_custom_call" | custom-call | tf_op jit(solution)/shard_map/pallas_call | solution.py:129
  145.6 0.0 collective-permute-done.11
  145.6 0.0 collective-permute-done.12
  145.6 1.6 %fusion.3 = bf16[2,48,512]{2,1,0:T(8,128)(2,1)} fusion(bf16[2,48,512]{2,1,0:T(8,128)(2,1)} %collective-permute-done.13, bf16[2,48,512]{2,1,0:T(8,128)(2,1)S(1)} %collective-permute-done.12, bf16[2,48,512]{2,1,0:T(8,128)(2,1)S(1)} %collective-permute-done.11, bf16[4,2,48,512]{3,2,1,0:T(8,128)(2,1)S(1)} %fusion, s32[]{:T(128)S(6)} %select_n.36), kind=kLoop, calls=%fused_computation.8 | loop fusion | flops 393216 | bytes 491524 | tf_op jit(solution)/shard_map/convert_element_type | solution.py:45
  147.2 0.0 all-to-all-done.3
  147.2 7.6 %conditional.1 = (bf16[2,48,64,384]{3,2,1,0:T(8,128)(2,1)}) conditional(s32[]{:T(128)} %bitcast.4, (s32[64]{0:T(128)S(1)}, s32[64]{0:T(128)S(1)}, s32[64]{0:T(128)S(1)}, bf16[8,2,3,48,384]{4,3,2,1,0:T(8,128)(2,1)}, bf16[8,2,48,1408]{3,2,1,0:T(8,128)(2,1)S(1)}) %tuple.37, (bf16[8,2,48,512]{3,2,1,0:T(8,128)(2,1)S(1)}, ...), branch_computations={%region_0.1_spmd, %region_1.2_spmd, %region_2.3_spmd} | conditional | flops 5898240 | bytes 14549028 | solution.py:525
  147.2 7.6 %branch_0_fun.1 = bf16[2,48,64,384]{3,2,1,0:T(8,128)(2,1)} custom-call(s32[64]{0:T(128)S(1)} %get-tuple-element.26.order_ref, s32[64]{0:T(128)S(1)} %get-tuple-element.27.counts_ref, s32[64]{0:T(128)S(1)} %get-tuple-element.40.offsets_ref, bf16[8,2,3,48,384]{4,3,2,1,0:T(8,128)(2,1)} %get-tuple-element.41.whole_ref, ...), custom_call_target="tpu_custom_call" | custom-call | tf_op jit(solution)/shard_map/cond/branch_0_fun/pallas_call | solution.py:442
  (15 shorter events, 0.0 us)
Async XLA Ops:
  3.5 16.6 %collective-permute-start = (bf16[3,256,384]{2,1,0:T(8,128)(2,1)}, bf16[3,256,384]{2,1,0:T(8,128)(2,1)S(1)}, u32[]{:S(2)}, u32[]{:S(2)}) collective-permute-start(bf16[3,256,384]{2,1,0:T(8,128)(2,1)} %get-tuple-element.82.refs_5_), channel_id=1, source_target_pairs={{0,16},{8,24},{16,0},{24,8},{1,17},{9,25},{17,1},{25,9},{2,18},{10... | collective-permute-start | bytes 1769480 | tf_op jit(solution)/shard_map/ppermute | solution.py:18
  6.5 17.7 %collective-permute-start.3 = (bf16[3,256,384]{2,1,0:T(8,128)(2,1)}, bf16[3,256,384]{2,1,0:T(8,128)(2,1)S(1)}, u32[]{:S(2)}, u32[]{:S(2)}) collective-permute-start(bf16[3,256,384]{2,1,0:T(8,128)(2,1)} %get-tuple-element.82.refs_5_), channel_id=1, source_target_pairs={{0,8},{8,0},{16,24},{24,16},{1,9},{9,1},{17,25},{25,17},{2,10},{10... | collective-permute-start | bytes 1769480 | tf_op jit(solution)/shard_map/ppermute | solution.py:18
  6.5 14.1 %copy-start.7 = (s32[8]{0:T(128)S(1)}, s32[8]{0:T(128)}, u32[]{:S(2)}) copy-start(s32[8]{0:T(128)} %refs_0_.1) | copy-start | bytes 100
  20.1 4.1 %copy-start.4 = (bf16[3,256,384]{2,1,0:T(8,128)(2,1)}, bf16[3,256,384]{2,1,0:T(8,128)(2,1)S(1)}, u32[]{:S(2)}) copy-start(bf16[3,256,384]{2,1,0:T(8,128)(2,1)S(1)} %collective-permute-done.refs_7_) | copy-start | bytes 1769476
  20.1 4.1 %collective-permute-start.4 = (bf16[3,256,384]{2,1,0:T(8,128)(2,1)S(1)}, bf16[3,256,384]{2,1,0:T(8,128)(2,1)S(1)}, u32[]{:S(2)}, u32[]{:S(2)}) collective-permute-start(bf16[3,256,384]{2,1,0:T(8,128)(2,1)S(1)} %collective-permute-done.refs_7_), channel_id=1, source_target_pairs={{0,8},{8,0},{16,24},{24,16},{1,9},{9,1},{17,25},{25,17},{2,10},{10... | collective-permute-start | bytes 1769480 | tf_op jit(solution)/shard_map/ppermute | solution.py:18
  20.7 3.5 %collective-permute-start.2 = (s32[8]{0:T(128)S(1)}, s32[8]{0:T(128)S(1)}, u32[]{:S(2)}, u32[]{:S(2)}) collective-permute-start(s32[8]{0:T(128)S(1)} %copy-done.7), channel_id=1, source_target_pairs={{0,1},{1,0},{2,3},{3,2},{4,5},{5,4},{6,7},{7,6},{8,9},{9,8},{10,11... | collective-permute-start | bytes 104 | tf_op jit(solution)/shard_map/ppermute | solution.py:18
  24.2 7.4 %copy-start.10 = (s32[8]{0:T(128)}, s32[8]{0:T(128)S(1)}, u32[]{:S(2)}) copy-start(s32[8]{0:T(128)S(1)} %collective-permute-done.2.refs_1_) | copy-start | bytes 100
  24.2 0.8 copy-start.5
  24.2 1.0 copy-start.6
  31.6 6.5 %copy-start.3 = (bf16[5,256,384]{2,1,0:T(8,128)(2,1)S(1)}, bf16[5,256,384]{2,1,0:T(8,128)(2,1)}, u32[]{:S(2)}) copy-start(bf16[5,256,384]{2,1,0:T(8,128)(2,1)} %get-tuple-element.83.refs_5_) | copy-start | bytes 2949124
  31.6 46.9 %all-to-all-start.2 = ((bf16[8,2,3,48,384]{4,3,2,1,0:T(8,128)(2,1)}), bf16[8,2,3,48,384]{4,3,2,1,0:T(8,128)(2,1)S(1)}, u32[]{:S(2)}, u32[]{:S(2)}) async-start(bf16[8,2,3,48,384]{4,3,2,1,0:T(8,128)(2,1)} %shard_map.88.first_ref), calls=%async_computation.2 | async-start | bytes 3538944 | tf_op jit(solution)/shard_map/all_to_all | solution.py:501
  38.1 22.6 %collective-permute-start.1 = (bf16[5,256,384]{2,1,0:T(8,128)(2,1)S(1)}, bf16[5,256,384]{2,1,0:T(8,128)(2,1)}, u32[]{:S(2)}, u32[]{:S(2)}) collective-permute-start(bf16[5,256,384]{2,1,0:T(8,128)(2,1)S(1)} %copy-done.3), channel_id=1, source_target_pairs={{0,16},{8,24},{16,0},{24,8},{1,17},{9,25},{17,1},{25,9},{2,18},{10... | collective-permute-start | bytes 2949128 | tf_op jit(solution)/shard_map/ppermute | solution.py:18
  39.4 21.3 %collective-permute-start.5 = (bf16[5,256,384]{2,1,0:T(8,128)(2,1)S(1)}, bf16[5,256,384]{2,1,0:T(8,128)(2,1)}, u32[]{:S(2)}, u32[]{:S(2)}) collective-permute-start(bf16[5,256,384]{2,1,0:T(8,128)(2,1)S(1)} %copy-done.3), channel_id=1, source_target_pairs={{0,8},{8,0},{16,24},{24,16},{1,9},{9,1},{17,25},{25,17},{2,10},{10... | collective-permute-start | bytes 2949128 | tf_op jit(solution)/shard_map/ppermute | solution.py:18
  60.6 2.9 %collective-permute-start.6 = (bf16[5,256,384]{2,1,0:T(8,128)(2,1)}, bf16[5,256,384]{2,1,0:T(8,128)(2,1)}, u32[]{:S(2)}, u32[]{:S(2)}) collective-permute-start(bf16[5,256,384]{2,1,0:T(8,128)(2,1)} %collective-permute-done.1.refs_7_), channel_id=1, source_target_pairs={{0,8},{8,0},{16,24},{24,16},{1,9},{9,1},{17,25},{25,17},{2,10},{10... | collective-permute-start | bytes 2949128 | tf_op jit(solution)/shard_map/ppermute | solution.py:18
  78.5 1.2 copy-start
  79.7 67.5 %all-to-all-start.3 = ((bf16[8,2,48,1408]{3,2,1,0:T(8,128)(2,1)}), bf16[8,2,48,1408]{3,2,1,0:T(8,128)(2,1)S(1)}, u32[]{:S(2)}, u32[]{:S(2)}) async-start(bf16[8,2,48,1408]{3,2,1,0:T(8,128)(2,1)} %get-tuple-element.90), calls=%async_computation.3 | async-start | bytes 4325376 | tf_op jit(solution)/shard_map/all_to_all | solution.py:508
  94.4 23.4 %collective-permute-start.10 = (bf16[4,2,48,512]{3,2,1,0:T(8,128)(2,1)S(1)}, bf16[4,2,48,512]{3,2,1,0:T(8,128)(2,1)}, u32[]{:S(2)}, u32[]{:S(2)}) collective-permute-start(bf16[4,2,48,512]{3,2,1,0:T(8,128)(2,1)S(1)} %dynamic-slice_bitcast_fusion), channel_id=1, source_target_pairs={{0,1},{1,0},{2,3},{3,2},{4,5},{5,4},{6,7},{7,6},{8,9},{9,8},{10,11... | collective-permute-start | bytes 1179656 | tf_op jit(solution)/shard_map/ppermute | solution.py:18
  119.7 25.9 %collective-permute-start.11 = (bf16[2,48,512]{2,1,0:T(8,128)(2,1)}, bf16[2,48,512]{2,1,0:T(8,128)(2,1)S(1)}, u32[]{:S(2)}, u32[]{:S(2)}) collective-permute-start(bf16[2,48,512]{2,1,0:T(8,128)(2,1)} %get-tuple-element.101), channel_id=1, source_target_pairs={{0,2},{1,3},{2,0},{3,1},{4,6},{5,7},{6,4},{7,5},{8,10},{9,11},{10,... | collective-permute-start | bytes 294920 | tf_op jit(solution)/shard_map/ppermute | solution.py:18
  119.7 25.9 %collective-permute-start.12 = (bf16[2,48,512]{2,1,0:T(8,128)(2,1)}, bf16[2,48,512]{2,1,0:T(8,128)(2,1)S(1)}, u32[]{:S(2)}, u32[]{:S(2)}) collective-permute-start(bf16[2,48,512]{2,1,0:T(8,128)(2,1)} %get-tuple-element.103), channel_id=1, source_target_pairs={{0,4},{1,5},{2,6},{3,7},{4,0},{5,1},{6,2},{7,3},{8,12},{9,13},{10,... | collective-permute-start | bytes 294920 | tf_op jit(solution)/shard_map/ppermute | solution.py:18
  127.6 18.0 %collective-permute-start.13 = (bf16[2,48,512]{2,1,0:T(8,128)(2,1)}, bf16[2,48,512]{2,1,0:T(8,128)(2,1)}, u32[]{:S(2)}, u32[]{:S(2)}) collective-permute-start(bf16[2,48,512]{2,1,0:T(8,128)(2,1)} %get-tuple-element.102), channel_id=1, source_target_pairs={{0,6},{1,7},{2,4},{3,5},{4,2},{5,3},{6,0},{7,1},{8,14},{9,15},{10,... | collective-permute-start | bytes 294920 | tf_op jit(solution)/shard_map/ppermute | solution.py:18
  127.6 4.4 %collective-permute-start.7 = (s32[16]{0:T(128)}, s32[16]{0:T(128)S(1)}, u32[]{:S(2)}, u32[]{:S(2)}) collective-permute-start(s32[16]{0:T(128)} %get-tuple-element.94.refs_0_), channel_id=1, source_target_pairs={{0,2},{1,3},{2,0},{3,1},{4,6},{5,7},{6,4},{7,5},{8,10},{9,11},{10,... | collective-permute-start | bytes 200 | tf_op jit(solution)/shard_map/ppermute | solution.py:18
  128.2 13.5 %collective-permute-start.8 = (s32[16]{0:T(128)}, s32[16]{0:T(128)S(1)}, u32[]{:S(2)}, u32[]{:S(2)}) collective-permute-start(s32[16]{0:T(128)} %get-tuple-element.94.refs_0_), channel_id=1, source_target_pairs={{0,4},{1,5},{2,6},{3,7},{4,0},{5,1},{6,2},{7,3},{8,12},{9,13},{10,... | collective-permute-start | bytes 200 | tf_op jit(solution)/shard_map/ppermute | solution.py:18
  132.0 10.2 %copy-start.8 = (s32[16]{0:T(128)}, s32[16]{0:T(128)S(1)}, u32[]{:S(2)}) copy-start(s32[16]{0:T(128)S(1)} %collective-permute-done.7.refs_1_) | copy-start | bytes 196
  132.0 10.2 %collective-permute-start.9 = (s32[16]{0:T(128)}, s32[16]{0:T(128)}, u32[]{:S(2)}, u32[]{:S(2)}) collective-permute-start(s32[16]{0:T(128)} %get-tuple-element.94.refs_0_), channel_id=1, source_target_pairs={{0,6},{1,7},{2,4},{3,5},{4,2},{5,3},{6,0},{7,1},{8,14},{9,15},{10,... | collective-permute-start | bytes 200 | tf_op jit(solution)/shard_map/ppermute | solution.py:18
  141.7 0.5 copy-start.9

commit v3 on v2

--- a/solution.py
+++ b/solution.py
@@ -11,6 +11,7 @@
 QBLOCK = 256
 LANES = 128
 VMEM_LIMIT = 60 * 1024 * 1024
+SMALL_VMEM_LIMIT = 32 * 1024 * 1024
 
 
 def exchange(x, axis, flip):
@@ -239,11 +240,19 @@
 def tile_kernel(nshard, first, packed, *refs):
     order_ref, source_counts_ref, offsets_ref, test_counts_ref, left_ref = refs[:5]
     shard_refs = refs[5 : 5 + nshard]
+    j = pl.program_id(0)
     if packed:
         tile_ref, main_ref, over_ref, pack_ref = refs[5 + nshard :]
     else:
-        (tile_ref,) = refs[5 + nshard :]
-    j = pl.program_id(0)
+        *near_refs, tile_ref, joined_ref = refs[5 + nshard :]
+
+        @pl.when(j == 0)
+        def _():
+            nblock = source_counts_ref.shape[0]
+            for place, near_ref in enumerate([source_counts_ref] + near_refs):
+                for k in range(nblock):
+                    joined_ref[place * nblock + k] = near_ref[k]
+
     ntest, _, kmax, _ = left_ref.shape
     ndest, _, _, rows, width = tile_ref.shape
     count = source_counts_ref[order_ref[first + j]]
@@ -301,7 +310,7 @@
             over_ref[...] = pack_ref[:, :, :, main : main + over_ref.shape[3]]
 
 
-def tiles(ndest, first, tables, test_counts, left, shards, main):
+def tiles(ndest, first, tables, test_counts, left, shards, main, near=()):
     ntest, nsource, kmax, nq = left.shape
     nshard = len(shards)
     part, width = shards[0].shape[1:]
@@ -316,13 +325,17 @@
             shapes.append(jax.ShapeDtypeStruct(shape, jnp.bfloat16))
             specs.append(pl.BlockSpec(shape, lambda j, *_: (0, 0, 0, 0)))
         scratch.append(pltpu.VMEM((ndest, ntest, rows, nsource * width + LANES), jnp.bfloat16))
+    else:
+        shapes.append(jax.ShapeDtypeStruct(((1 + len(near)) * tables[1].shape[0],), jnp.int32))
+        specs.append(pl.BlockSpec(memory_space=pltpu.SMEM))
     return pl.pallas_call(
         functools.partial(tile_kernel, nshard, first, packed),
         grid_spec=pltpu.PrefetchScalarGridSpec(
             num_scalar_prefetch=4,
             grid=(nsource,),
             in_specs=[pl.BlockSpec((ntest, 1, kmax, nq), lambda j, *_: (0, j, 0, 0))]
-            + [pl.BlockSpec((1, part, width), lambda j, *_: (j, 0, 0))] * nshard,
+            + [pl.BlockSpec((1, part, width), lambda j, *_: (j, 0, 0))] * nshard
+            + [pl.BlockSpec(memory_space=pltpu.SMEM)] * len(near),
             out_specs=specs,
             scratch_shapes=scratch,
         ),
@@ -333,65 +346,68 @@
             bytes_accessed=2 * ntest * nsource * kmax * (nq + width),
             transcendentals=0,
         ),
-    )(*tables, test_counts, left, *shards)
-
-
-def project_kernel(cut, order_ref, first_ref, rest_ref, coeff_ref, *refs):
-    *counts_refs, sum_ref, joined_ref, total_ref = refs
+    )(*tables, test_counts, left, *shards, *near)
+
+
+def project_kernel(order_ref, tile_ref, coeff_ref, *refs):
+    *start_refs, sum_ref, total_ref = refs
     j = pl.program_id(0)
-    ndest, ntest, _, rows, width = first_ref.shape
-
-    def add(tile_ref, fresh):
-        whole = [tile_ref[dest, i, 0] for i in range(ntest) for dest in range(ndest)]
-        term = jnp.dot(jnp.concatenate(whole, axis=0), coeff_ref[0], preferred_element_type=jnp.float32)
-        total_ref[...] = term if fresh else total_ref[...] + term
-
-    pl.when(j == 0)(lambda: add(first_ref, True))
-    pl.when((j > 0) & (j < cut))(lambda: add(first_ref, False))
-    pl.when(j >= cut)(lambda: add(rest_ref, False))
+    ndest, ntest, _, rows, _ = tile_ref.shape
+    whole = [tile_ref[dest, i, 0] for i in range(ntest) for dest in range(ndest)]
+    term = jnp.dot(jnp.concatenate(whole, axis=0), coeff_ref[0], preferred_element_type=jnp.float32)
+
+    @pl.when(j == 0)
+    def _():
+        total_ref[...] = term + start_refs[0][...] if start_refs else term
+
+    @pl.when(j > 0)
+    def _():
+        total_ref[...] += term
 
     @pl.when(j == pl.num_programs(0) - 1)
     def _():
+        if not start_refs:
+            sum_ref[...] = total_ref[...]
+            return
         for i in range(ntest):
             for dest in range(ndest):
                 top = (i * ndest + dest) * rows
                 sum_ref[dest, i] = total_ref[top : top + rows, :].astype(sum_ref.dtype)
-        nblock = counts_refs[0].shape[0]
-        for place, counts_ref in enumerate(counts_refs):
-            for k in range(nblock):
-                joined_ref[place * nblock + k] = counts_ref[k]
-
-
-def project(order, first, rest, coefficients, counts):
-    ndest, ntest, cut, rows, width = first.shape
-    nsource, _, ncol = coefficients.shape
-    block = (ndest, ntest, 1, rows, width)
-    smem = pl.BlockSpec(memory_space=pltpu.SMEM)
+
+
+def project(order, first, tiles, coefficients, start):
+    ndest, ntest, nsource, rows, width = tiles.shape
+    ncol = coefficients.shape[2]
+    total_spec = pl.BlockSpec((ntest * ndest * rows, ncol), lambda j, order: (0, 0))
+    if start is None:
+        started = []
+        sum_spec = total_spec
+        sum_shape = jax.ShapeDtypeStruct((ntest * ndest * rows, ncol), jnp.float32)
+    else:
+        started = [start]
+        sum_spec = pl.BlockSpec((ndest, ntest, rows, ncol), lambda j, order: (0, 0, 0, 0))
+        sum_shape = jax.ShapeDtypeStruct((ndest, ntest, rows, ncol), jnp.bfloat16)
     return pl.pallas_call(
-        functools.partial(project_kernel, cut),
+        project_kernel,
         grid_spec=pltpu.PrefetchScalarGridSpec(
             num_scalar_prefetch=1,
             grid=(nsource,),
             in_specs=[
-                pl.BlockSpec(block, lambda j, order: (0, 0, jnp.minimum(j, cut - 1), 0, 0)),
-                pl.BlockSpec(block, lambda j, order: (0, 0, jnp.maximum(j - cut, 0), 0, 0)),
-                pl.BlockSpec((1, width, ncol), lambda j, order: (order[j], 0, 0)),
+                pl.BlockSpec((ndest, ntest, 1, rows, width), lambda j, order: (0, 0, j, 0, 0)),
+                pl.BlockSpec((1, width, ncol), lambda j, order: (order[first + j], 0, 0)),
             ]
-            + [smem] * len(counts),
-            out_specs=(pl.BlockSpec((ndest, ntest, rows, ncol), lambda j, order: (0, 0, 0, 0)), smem),
-            scratch_shapes=[pltpu.VMEM((ndest * ntest * rows, ncol), jnp.float32)],
-        ),
-        out_shape=(
-            jax.ShapeDtypeStruct((ndest, ntest, rows, ncol), jnp.bfloat16),
-            jax.ShapeDtypeStruct((len(counts) * nsource,), jnp.int32),
-        ),
-        compiler_params=pltpu.CompilerParams(vmem_limit_bytes=VMEM_LIMIT),
+            + [total_spec] * len(started),
+            out_specs=sum_spec,
+            scratch_shapes=[pltpu.VMEM((ntest * ndest * rows, ncol), jnp.float32)],
+        ),
+        out_shape=sum_shape,
+        compiler_params=pltpu.CompilerParams(vmem_limit_bytes=SMALL_VMEM_LIMIT),
         cost_estimate=pl.CostEstimate(
             flops=2 * ndest * ntest * rows * width * ncol * nsource,
             bytes_accessed=2 * ndest * ntest * rows * width * nsource,
             transcendentals=0,
         ),
-    )(order, first, rest, coefficients, *counts)
+    )(order, tiles, coefficients, *started)
 
 
 def unpack_kernel(cut, order_ref, counts_ref, offsets_ref, whole_ref, packed_ref, out_ref, rows_ref):
@@ -452,7 +468,7 @@
             scratch_shapes=[pltpu.VMEM((nall, rows, width), jnp.float32)],
         ),
         out_shape=jax.ShapeDtypeStruct((ntest, rows, nall, width), jnp.bfloat16),
-        compiler_params=pltpu.CompilerParams(vmem_limit_bytes=VMEM_LIMIT),
+        compiler_params=pltpu.CompilerParams(vmem_limit_bytes=SMALL_VMEM_LIMIT),
     )(*tables, whole, packed)
 
 
@@ -497,7 +513,8 @@
     inner = max(1, nsrc // 4)
     near = [exchange(source_counts, "src", flip) for flip in range(1, inner)]
     *near, left_a = lax.optimization_barrier((*near, left_a))
-    (tiles_a,) = tiles(nsrc, 0, tables, test_counts, left_a, shards_a, None)
+    tiles_a, joined = tiles(nsrc, 0, tables, test_counts, left_a, shards_a, None, near)
+    groups = [joined] + [exchange(joined, "src", flip) for flip in range(inner, nsrc, inner)]
     moved_a = lax.all_to_all(tiles_a, "src", split_axis=0, concat_axis=0, tiled=True)
 
     rest, _ = lax.optimization_barrier((basis_b, held["a"]))
@@ -505,10 +522,11 @@
     left_b = left_products(ntest_axis, me, order, test_points, later, test_basis, cut, nsource)
     shards_b, left_b = gather("b", rest, left_b)
     tiles_b, packed, beyond = tiles(nsrc, cut, tables, test_counts, left_b, shards_b, main)
+    sums_a = project(order, 0, tiles_a, coefficients, None)
+    packed, sums_a, *groups = lax.optimization_barrier((packed, sums_a, *groups))
     moved_b = lax.all_to_all(packed, "src", split_axis=0, concat_axis=0, tiled=True)
 
-    sums, joined = project(order, tiles_a, tiles_b, coefficients, [source_counts] + near)
-    groups = [joined] + [exchange(joined, "src", flip) for flip in range(inner, nsrc, inner)]
+    sums = project(order, cut, tiles_b, coefficients, sums_a)
     projected = sum_rows(sums, "src")
     me_src, _ = lax.optimization_barrier((jnp.reshape(lax.axis_index("src"), (1,)), packed))
     all_counts, all_order, all_offsets, branch = all_tables(cut, nsource, widths, me_src, groups)

time: 156 us -> 153 us (0.981)
  local copies, waits for them, and re-layouts: 4.51 us -> 7.84 us
  starting transfers between devices: 34.1 us -> 31.4 us
  Pallas kernels: 73.1 us -> 71.5 us
    unnamed x18 -> x36, local copies, waits for them, and re-layouts: 2.76 us -> 7.79 us
    all_to_all x1, waiting for transfers between devices: 4.58 us -> 0.01 us  [body(): lax.all_to_all(tiles_a, 'src', split_axis=0, concat_axis=0, tiled=True)]
    ppermute x14, starting transfers between devices: 23.8 us -> 19.9 us  [exchange(): return lax.ppermute(x, axis, [(a, a ^ flip) for a in range(size)])]
    ppermute x14, waiting for transfers between devices: 34.3 us -> 38 us  [exchange(): return lax.ppermute(x, axis, [(a, a ^ flip) for a in range(size)])]
    pallas_call x1 -> x2, Pallas kernels: 9.87 us -> 7.61 us  [project(): pl.pallas_call(project_kernel, grid_spec=pltpu.PrefetchScalarGridSpec(num...]
    all_to_all x1, starting transfers between devices: 3.79 us -> 5.71 us  [body(): lax.all_to_all(packed, 'src', split_axis=0, concat_axis=0, tiled=True)]
  transfers between devices with their start and end apart: 16 -> 16, of which waited for: 6 -> 4; matrix products, arithmetic and copies ran while one was open for 3% -> 1% of each run, Pallas kernels for 36% -> 36%
where the time goes in v3:
time: 153 us; the launch traced here: 152 us
  Pallas kernels  71.5 us (47%)
  waiting for transfers between devices  38 us (25%)
  starting transfers between devices  31.4 us (21%)
  local copies, waits for them, and re-layouts  7.84 us (5%)
  other arithmetic  1.79 us (1%)
  between operations  1.53 us (1%)
    ppermute x14, waiting for transfers between devices, exchange(): return lax.ppermute(x, axis, [(a, a ^ flip) for a in range(size)])  38 us
    pallas_call x2, Pallas kernels, left_products(): pl.pallas_call(functools.partial(left_kernel, nshard, first), grid_spec=p...  33.4 us
    ppermute x14, starting transfers between devices, exchange(): return lax.ppermute(x, axis, [(a, a ^ flip) for a in range(size)])  19.9 us
    pallas_call x2, Pallas kernels, tiles(): pl.pallas_call(functools.partial(tile_kernel, nshard, first, packed), gri...  17.1 us
    pallas_call x1, Pallas kernels, unpack(): pl.pallas_call(functools.partial(unpack_kernel, cut), grid_spec=pltpu.Pre...  7.92 us
    unnamed x36, local copies, waits for them, and re-layouts  7.79 us
    pallas_call x2, Pallas kernels, project(): pl.pallas_call(project_kernel, grid_spec=pltpu.PrefetchScalarGridSpec(num...  7.61 us
    all_to_all x1, starting transfers between devices, body(): lax.all_to_all(tiles_a, 'src', split_axis=0, concat_axis=0, tiled=True)  5.8 us
  transfers between devices with their start and end apart: 16, of which 4 were waited for; matrix products, arithmetic and copies ran while one was open for 1% of the time, Pallas kernels for 36%

profile of v3, /device:TPU:0, one launch (start us, length us, event | category | flops | bytes accessed | tf_op | source)
XLA Modules:
  0.0 152.1 jit_solution(5308217320111359173)
XLA Ops:
  0.6 2.8 %shard_map.86 = (s32[8]{0:T(128)}, s32[8]{0:T(128)}, bf16[3,256,384]{2,1,0:T(8,128)(2,1)}, bf16[5,256,384]{2,1,0:T(8,128)(2,1)}) custom-call(s32[8]{0:T(128)} %refs_1_.3, bf16[8,256,384]{2,1,0:T(8,128)(2,1)} %basis_ref.3), custom_call_target="tpu_custom_call" | custom-call | tf_op jit(solution)/shard_map/pallas_call | solution.py:85
  3.4 3.0 %collective-permute-start = (bf16[3,256,384]{2,1,0:T(8,128)(2,1)}, bf16[3,256,384]{2,1,0:T(8,128)(2,1)S(1)}, u32[]{:S(2)}, u32[]{:S(2)}) collective-permute-start(bf16[3,256,384]{2,1,0:T(8,128)(2,1)} %get-tuple-element.88.refs_5_), channel_id=1, source_target_pairs={{0,16},{8,24},{16,0},{24,8},{1,17},{9,25},{17,1},{25,9},{2,18},{10... | collective-permute-start | bytes 1769480 | tf_op jit(solution)/shard_map/ppermute | solution.py:19
  6.5 0.0 collective-permute-start.3
  6.5 13.6 %shard_map.87.refs_4_ = bf16[2,3,384,1024]{3,2,1,0:T(8,128)(2,1)} custom-call(s32[1]{0:T(128)} %bitcast.1.me_ref, s32[8]{0:T(128)} %get-tuple-element.85.order_ref.refs_0_, f32[3,2,1024]{2,1,0:T(2,128)} %bitcast.26, f32[3,8,1024]{2,1,0:T(8,128)} %bitcast.24, bf16[2,1024,384]{2,1,0:T(8,128)(2,1)} %basis_ref.5), custom_call_target="tpu_custom_call" | custom-call | flops 4831838208 | bytes 4718592 | tf_op jit(solution)/shard_map/pallas_call | solution.py:212
  20.1 0.0 collective-permute-done.refs_7_
  20.1 0.5 collective-permute-start.4
  20.6 1.5 collective-permute-start.2
  22.0 2.1 %collective-permute-done.2.refs_9_ = s32[8]{0:T(128)S(1)} collective-permute-done((s32[8]{0:T(128)S(1)}, s32[8]{0:T(128)S(1)}, u32[]{:S(2)}, u32[]{:S(2)}) %collective-permute-start.2) | collective-permute-done | bytes 64 | tf_op jit(solution)/shard_map/ppermute | solution.py:19
  24.1 0.0 collective-permute-done.3.refs_6_
  24.1 0.0 collective-permute-done.4.refs_8_
  24.2 0.5 copy-done.13
  24.7 0.2 copy-done.10
  25.0 0.2 copy-done.11
  25.2 6.5 %shard_map.88 = (bf16[8,2,3,48,384]{4,3,2,1,0:T(8,128)(2,1)}, s32[16]{0:T(128)}) custom-call(s32[8]{0:T(128)} %get-tuple-element.85.order_ref.refs_0_, s32[8]{0:T(128)} %refs_1_.3, s32[8]{0:T(128)} %get-tuple-element.86.refs_2_, s32[2]{0:T(128)} %refs_3_.3, bf16[2,3,384,1024]{3,2,1,0:T(8,128)(2,1)} %shard_map.87.refs_4_, ...), custom_call_target="tpu_custom_call" | custom-call | flops 1811939328 | bytes 6488064 | tf_op jit(solution)/shard_map/pallas_call | solution.py:331
  31.7 5.8 %all-to-all-start.2 = ((bf16[8,2,3,48,384]{4,3,2,1,0:T(8,128)(2,1)}), bf16[8,2,3,48,384]{4,3,2,1,0:T(8,128)(2,1)}, u32[]{:S(2)}, u32[]{:S(2)}) async-start(bf16[8,2,3,48,384]{4,3,2,1,0:T(8,128)(2,1)} %get-tuple-element.94.tile_ref), calls=%async_computation.2 | async-start | bytes 3538944 | tf_op jit(solution)/shard_map/all_to_all | solution.py:518
  37.5 0.0 copy-start
  37.5 1.3 collective-permute-start.1
  38.8 0.0 collective-permute-start.5
  38.8 19.8 %shard_map.89.refs_4_ = bf16[2,5,384,1024]{3,2,1,0:T(8,128)(2,1)} custom-call(s32[1]{0:T(128)} %bitcast.1.me_ref, s32[8]{0:T(128)} %get-tuple-element.85.order_ref.refs_0_, f32[3,2,1024]{2,1,0:T(2,128)} %bitcast.27, f32[3,8,1024]{2,1,0:T(8,128)} %bitcast.25, bf16[2,1024,384]{2,1,0:T(8,128)(2,1)} %basis_ref.5), custom_call_target="tpu_custom_call" | custom-call | flops 8053063680 | bytes 7864320 | tf_op jit(solution)/shard_map/pallas_call | solution.py:212
  58.6 1.7 %collective-permute-done.1.refs_7_ = bf16[5,256,384]{2,1,0:T(8,128)(2,1)} collective-permute-done((bf16[5,256,384]{2,1,0:T(8,128)(2,1)}, bf16[5,256,384]{2,1,0:T(8,128)(2,1)}, u32[]{:S(2)}, u32[]{:S(2)}) %collective-permute-start.1) | collective-permute-done | bytes 983072 | tf_op jit(solution)/shard_map/ppermute | solution.py:19
  60.3 0.0 collective-permute-start.6
  60.3 1.7 %collective-permute-start.7 = (s32[16]{0:T(128)S(1)}, s32[16]{0:T(128)S(1)}, u32[]{:S(2)}, u32[]{:S(2)}) collective-permute-start(s32[16]{0:T(128)S(1)} %copy-done.14), channel_id=1, source_target_pairs={{0,2},{1,3},{2,0},{3,1},{4,6},{5,7},{6,4},{7,5},{8,10},{9,11},{10,... | collective-permute-start | bytes 200 | tf_op jit(solution)/shard_map/ppermute | solution.py:19
  62.0 2.4 %collective-permute-start.8 = (s32[16]{0:T(128)S(1)}, s32[16]{0:T(128)S(1)}, u32[]{:S(2)}, u32[]{:S(2)}) collective-permute-start(s32[16]{0:T(128)S(1)} %copy-done.14), channel_id=1, source_target_pairs={{0,4},{1,5},{2,6},{3,7},{4,0},{5,1},{6,2},{7,3},{8,12},{9,13},{10,... | collective-permute-start | bytes 200 | tf_op jit(solution)/shard_map/ppermute | solution.py:19
  64.4 0.3 collective-permute-start.9
  64.7 1.5 copy-done.1
  66.2 3.0 %shard_map.91.refs_0_ = f32[768,512]{1,0:T(8,128)S(1)} custom-call(s32[8]{0:T(128)S(1)} %copy-done.6, bf16[8,2,3,48,384]{4,3,2,1,0:T(8,128)(2,1)S(1)} %copy-done.1, bf16[8,384,512]{2,1,0:T(8,128)(2,1)S(1)} %copy-done), custom_call_target="tpu_custom_call" | custom-call | flops 905969664 | bytes 1769472 | tf_op jit(solution)/shard_map/pallas_call | solution.py:390
  69.2 1.1 copy-done.2
  70.3 0.0 collective-permute-done.5.refs_6_
  70.3 10.5 %shard_map.90 = (bf16[8,2,5,48,384]{4,3,2,1,0:T(8,128)(2,1)}, bf16[8,2,48,1408]{3,2,1,0:T(8,128)(2,1)}, bf16[8,2,48,512]{3,2,1,0:T(8,128)(2,1)}) custom-call(s32[8]{0:T(128)} %get-tuple-element.85.order_ref.refs_0_, s32[8]{0:T(128)} %refs_1_.3, s32[8]{0:T(128)} %get-tuple-element.86.refs_2_, s32[2]{0:T(128)} %refs_3_.3, ...), custom_call_target="tpu_custom_call" | custom-call | flops 3019898880 | bytes 10813440 | tf_op jit(solution)/shard_map/pallas_call | solution.py:331
  80.9 0.0 collective-permute-done.7.refs_1_
  80.9 0.0 collective-permute-done.8.refs_2_
  80.9 5.7 %all-to-all-start.3 = ((bf16[8,2,48,1408]{3,2,1,0:T(8,128)(2,1)}), bf16[8,2,48,1408]{3,2,1,0:T(8,128)(2,1)}, u32[]{:S(2)}, u32[]{:S(2)}) async-start(bf16[8,2,48,1408]{3,2,1,0:T(8,128)(2,1)} %get-tuple-element.100), calls=%async_computation.3 | async-start | bytes 4325376 | tf_op jit(solution)/shard_map/all_to_all | solution.py:527
  86.7 1.4 copy-done.3
  88.1 1.8 %copy-done.5 = bf16[8,2,5,48,384]{4,3,2,1,0:T(8,128)(2,1)S(1)} copy-done((bf16[8,2,5,48,384]{4,3,2,1,0:T(8,128)(2,1)S(1)}, bf16[8,2,5,48,384]{4,3,2,1,0:T(8,128)(2,1)}, u32[]{:S(2)}) %copy-start.5) | copy-done | bytes 2949144
  89.9 4.6 %shard_map.93 = bf16[8,2,48,512]{3,2,1,0:T(8,128)(2,1)S(1)} custom-call(s32[8]{0:T(128)S(1)} %copy-done.7, bf16[8,2,5,48,384]{4,3,2,1,0:T(8,128)(2,1)S(1)} %copy-done.5, bf16[8,384,512]{2,1,0:T(8,128)(2,1)S(1)} %copy-done, f32[768,512]{1,0:T(8,128)S(1)} %copy-done.3), custom_call_target="tpu_custom_call" | custom-call | flops 1509949440 | bytes 2949120 | tf_op jit(solution)/shard_map/pallas_call | solution.py:390
  94.6 0.0 copy-start.4
  94.6 0.9 copy-done.4
  95.5 2.1 %collective-permute-start.10 = (bf16[4,2,48,512]{3,2,1,0:T(8,128)(2,1)S(1)}, bf16[4,2,48,512]{3,2,1,0:T(8,128)(2,1)S(1)}, u32[]{:S(2)}, u32[]{:S(2)}) collective-permute-start(bf16[4,2,48,512]{3,2,1,0:T(8,128)(2,1)S(1)} %dynamic-slice_bitcast_fusion), channel_id=1, source_target_pairs={{0,1},{1,0},{2,3},{3,2},{4,5},{5,4},{6,7},{7,6},{8,9},{9,8},{10,11... | collective-permute-start | bytes 1179656 | tf_op jit(solution)/shard_map/ppermute | solution.py:19
  97.6 21.9 %collective-permute-done.10 = bf16[4,2,48,512]{3,2,1,0:T(8,128)(2,1)S(1)} collective-permute-done((bf16[4,2,48,512]{3,2,1,0:T(8,128)(2,1)S(1)}, bf16[4,2,48,512]{3,2,1,0:T(8,128)(2,1)S(1)}, u32[]{:S(2)}, u32[]{:S(2)}) %collective-permute-start.10) | collective-permute-done | bytes 393248 | tf_op jit(solution)/shard_map/ppermute | solution.py:19
  119.4 1.1 fusion
  120.6 0.1 collective-permute-start.11
  120.7 7.1 %collective-permute-start.12 = (bf16[2,48,512]{2,1,0:T(8,128)(2,1)S(1)}, bf16[2,48,512]{2,1,0:T(8,128)(2,1)S(1)}, u32[]{:S(2)}, u32[]{:S(2)}) collective-permute-start(bf16[2,48,512]{2,1,0:T(8,128)(2,1)S(1)} %get-tuple-element.115), channel_id=1, source_target_pairs={{0,4},{1,5},{2,6},{3,7},{4,0},{5,1},{6,2},{7,3},{8,12},{9,13},{10,... | collective-permute-start | bytes 294920 | tf_op jit(solution)/shard_map/ppermute | solution.py:19
  127.7 0.0 collective-permute-start.13
  127.7 2.7 %shard_map.92 = (s32[64]{0:T(128)S(1)}, s32[64]{0:T(128)S(1)}, s32[64]{0:T(128)S(1)}, s32[1]{0:T(128)}) custom-call(s32[1]{0:T(128)} %bitcast.me_ref, s32[16]{0:T(128)} %get-tuple-element.102.refs_0_, s32[16]{0:T(128)} %copy-done.15, s32[16]{0:T(128)} %copy-done.16, s32[16]{0:T(128)} %copy-done.17), custom_call_target="tpu_custom_call" | custom-call | tf_op jit(solution)/shard_map/pallas_call | solution.py:130
  131.1 12.4 %collective-permute-done.12 = bf16[2,48,512]{2,1,0:T(8,128)(2,1)S(1)} collective-permute-done((bf16[2,48,512]{2,1,0:T(8,128)(2,1)S(1)}, bf16[2,48,512]{2,1,0:T(8,128)(2,1)S(1)}, u32[]{:S(2)}, u32[]{:S(2)}) %collective-permute-start.12) | collective-permute-done | bytes 98336 | tf_op jit(solution)/shard_map/ppermute | solution.py:19
  143.5 0.7 fusion.3
  144.2 7.9 %conditional.1 = (bf16[2,48,64,384]{3,2,1,0:T(8,128)(2,1)}) conditional(s32[]{:T(128)} %bitcast.4, (s32[64]{0:T(128)S(1)}, s32[64]{0:T(128)S(1)}, s32[64]{0:T(128)S(1)}, bf16[8,2,3,48,384]{4,3,2,1,0:T(8,128)(2,1)}, bf16[8,2,48,1408]{3,2,1,0:T(8,128)(2,1)}) %tuple.31, (bf16[8,2,48,512]{3,2,1,0:T(8,128)(2,1)S(1)}, ...), branch_computations={%region_0.1_spmd, %region_1.2_spmd, %region_2.3_spmd} | conditional | flops 5898240 | bytes 7471112 | solution.py:543
  144.2 7.9 %branch_0_fun.1 = bf16[2,48,64,384]{3,2,1,0:T(8,128)(2,1)} custom-call(s32[64]{0:T(128)S(1)} %get-tuple-element.26.order_ref, s32[64]{0:T(128)S(1)} %get-tuple-element.27.counts_ref, s32[64]{0:T(128)S(1)} %get-tuple-element.40.offsets_ref, bf16[8,2,3,48,384]{4,3,2,1,0:T(8,128)(2,1)} %get-tuple-element.41.whole_ref, ...), custom_call_target="tpu_custom_call" | custom-call | tf_op jit(solution)/shard_map/cond/branch_0_fun/pallas_call | solution.py:458
  (34 shorter events, 0.1 us)
Async XLA Ops:
  3.4 16.6 %collective-permute-start = (bf16[3,256,384]{2,1,0:T(8,128)(2,1)}, bf16[3,256,384]{2,1,0:T(8,128)(2,1)S(1)}, u32[]{:S(2)}, u32[]{:S(2)}) collective-permute-start(bf16[3,256,384]{2,1,0:T(8,128)(2,1)} %get-tuple-element.88.refs_5_), channel_id=1, source_target_pairs={{0,16},{8,24},{16,0},{24,8},{1,17},{9,25},{17,1},{25,9},{2,18},{10... | collective-permute-start | bytes 1769480 | tf_op jit(solution)/shard_map/ppermute | solution.py:19
  6.5 17.7 %collective-permute-start.3 = (bf16[3,256,384]{2,1,0:T(8,128)(2,1)}, bf16[3,256,384]{2,1,0:T(8,128)(2,1)S(1)}, u32[]{:S(2)}, u32[]{:S(2)}) collective-permute-start(bf16[3,256,384]{2,1,0:T(8,128)(2,1)} %get-tuple-element.88.refs_5_), channel_id=1, source_target_pairs={{0,8},{8,0},{16,24},{24,16},{1,9},{9,1},{17,25},{25,17},{2,10},{10... | collective-permute-start | bytes 1769480 | tf_op jit(solution)/shard_map/ppermute | solution.py:19
  6.5 14.1 %copy-start.12 = (s32[8]{0:T(128)S(1)}, s32[8]{0:T(128)}, u32[]{:S(2)}) copy-start(s32[8]{0:T(128)} %refs_1_.3) | copy-start | bytes 100
  20.1 4.1 %copy-start.9 = (bf16[3,256,384]{2,1,0:T(8,128)(2,1)}, bf16[3,256,384]{2,1,0:T(8,128)(2,1)S(1)}, u32[]{:S(2)}) copy-start(bf16[3,256,384]{2,1,0:T(8,128)(2,1)S(1)} %collective-permute-done.refs_7_) | copy-start | bytes 1769476
  20.1 4.1 %collective-permute-start.4 = (bf16[3,256,384]{2,1,0:T(8,128)(2,1)S(1)}, bf16[3,256,384]{2,1,0:T(8,128)(2,1)S(1)}, u32[]{:S(2)}, u32[]{:S(2)}) collective-permute-start(bf16[3,256,384]{2,1,0:T(8,128)(2,1)S(1)} %collective-permute-done.refs_7_), channel_id=1, source_target_pairs={{0,8},{8,0},{16,24},{24,16},{1,9},{9,1},{17,25},{25,17},{2,10},{10... | collective-permute-start | bytes 1769480 | tf_op jit(solution)/shard_map/ppermute | solution.py:19
  20.6 3.5 %collective-permute-start.2 = (s32[8]{0:T(128)S(1)}, s32[8]{0:T(128)S(1)}, u32[]{:S(2)}, u32[]{:S(2)}) collective-permute-start(s32[8]{0:T(128)S(1)} %copy-done.12), channel_id=1, source_target_pairs={{0,1},{1,0},{2,3},{3,2},{4,5},{5,4},{6,7},{7,6},{8,9},{9,8},{10,11... | collective-permute-start | bytes 104 | tf_op jit(solution)/shard_map/ppermute | solution.py:19
  24.1 0.6 copy-start.13
  24.1 0.8 copy-start.10
  24.1 1.0 copy-start.11
  31.7 49.2 %all-to-all-start.2 = ((bf16[8,2,3,48,384]{4,3,2,1,0:T(8,128)(2,1)}), bf16[8,2,3,48,384]{4,3,2,1,0:T(8,128)(2,1)}, u32[]{:S(2)}, u32[]{:S(2)}) async-start(bf16[8,2,3,48,384]{4,3,2,1,0:T(8,128)(2,1)} %get-tuple-element.94.tile_ref), calls=%async_computation.2 | async-start | bytes 3538944 | tf_op jit(solution)/shard_map/all_to_all | solution.py:518
  37.5 22.8 %copy-start.14 = (s32[16]{0:T(128)S(1)}, s32[16]{0:T(128)}, u32[]{:S(2)}) copy-start(s32[16]{0:T(128)} %get-tuple-element.102.refs_0_) | copy-start | bytes 196
  37.5 27.2 %copy-start = (bf16[8,384,512]{2,1,0:T(8,128)(2,1)S(1)}, bf16[8,384,512]{2,1,0:T(8,128)(2,1)}, u32[]{:S(2)}) copy-start(bf16[8,384,512]{2,1,0:T(8,128)(2,1)} %coeff_ref.3) | copy-start | bytes 9437188
  37.5 27.2 %copy-start.6 = (s32[8]{0:T(128)S(1)}, s32[8]{0:T(128)}, u32[]{:S(2)}) copy-start(s32[8]{0:T(128)} %get-tuple-element.85.order_ref.refs_0_) | copy-start | bytes 100
  37.5 22.8 %collective-permute-start.1 = (bf16[5,256,384]{2,1,0:T(8,128)(2,1)}, bf16[5,256,384]{2,1,0:T(8,128)(2,1)}, u32[]{:S(2)}, u32[]{:S(2)}) collective-permute-start(bf16[5,256,384]{2,1,0:T(8,128)(2,1)} %get-tuple-element.89.refs_5_), channel_id=1, source_target_pairs={{0,16},{8,24},{16,0},{24,8},{1,17},{9,25},{17,1},{25,9},{2,18},{10... | collective-permute-start | bytes 2949128 | tf_op jit(solution)/shard_map/ppermute | solution.py:19
  38.8 31.5 %collective-permute-start.5 = (bf16[5,256,384]{2,1,0:T(8,128)(2,1)}, bf16[5,256,384]{2,1,0:T(8,128)(2,1)}, u32[]{:S(2)}, u32[]{:S(2)}) collective-permute-start(bf16[5,256,384]{2,1,0:T(8,128)(2,1)} %get-tuple-element.89.refs_5_), channel_id=1, source_target_pairs={{0,8},{8,0},{16,24},{24,16},{1,9},{9,1},{17,25},{25,17},{2,10},{10... | collective-permute-start | bytes 2949128 | tf_op jit(solution)/shard_map/ppermute | solution.py:19
  60.3 10.0 %collective-permute-start.6 = (bf16[5,256,384]{2,1,0:T(8,128)(2,1)}, bf16[5,256,384]{2,1,0:T(8,128)(2,1)}, u32[]{:S(2)}, u32[]{:S(2)}) collective-permute-start(bf16[5,256,384]{2,1,0:T(8,128)(2,1)} %collective-permute-done.1.refs_7_), channel_id=1, source_target_pairs={{0,8},{8,0},{16,24},{24,16},{1,9},{9,1},{17,25},{25,17},{2,10},{10... | collective-permute-start | bytes 2949128 | tf_op jit(solution)/shard_map/ppermute | solution.py:19
  60.3 20.6 %collective-permute-start.7 = (s32[16]{0:T(128)S(1)}, s32[16]{0:T(128)S(1)}, u32[]{:S(2)}, u32[]{:S(2)}) collective-permute-start(s32[16]{0:T(128)S(1)} %copy-done.14), channel_id=1, source_target_pairs={{0,2},{1,3},{2,0},{3,1},{4,6},{5,7},{6,4},{7,5},{8,10},{9,11},{10,... | collective-permute-start | bytes 200 | tf_op jit(solution)/shard_map/ppermute | solution.py:19
  62.0 18.9 %collective-permute-start.8 = (s32[16]{0:T(128)S(1)}, s32[16]{0:T(128)S(1)}, u32[]{:S(2)}, u32[]{:S(2)}) collective-permute-start(s32[16]{0:T(128)S(1)} %copy-done.14), channel_id=1, source_target_pairs={{0,4},{1,5},{2,6},{3,7},{4,0},{5,1},{6,2},{7,3},{8,12},{9,13},{10,... | collective-permute-start | bytes 200 | tf_op jit(solution)/shard_map/ppermute | solution.py:19
  64.4 16.5 %collective-permute-start.9 = (s32[16]{0:T(128)S(1)}, s32[16]{0:T(128)S(1)}, u32[]{:S(2)}, u32[]{:S(2)}) collective-permute-start(s32[16]{0:T(128)S(1)} %copy-done.14), channel_id=1, source_target_pairs={{0,6},{1,7},{2,4},{3,5},{4,2},{5,3},{6,0},{7,1},{8,14},{9,15},{10,... | collective-permute-start | bytes 200 | tf_op jit(solution)/shard_map/ppermute | solution.py:19
  64.7 1.5 copy-start.1
  69.2 1.1 copy-start.2
  80.9 5.8 %copy-start.7 = (s32[8]{0:T(128)S(1)}, s32[8]{0:T(128)}, u32[]{:S(2)}) copy-start(s32[8]{0:T(128)} %get-tuple-element.85.order_ref.refs_0_) | copy-start | bytes 100
  80.9 13.7 %copy-start.15 = (s32[16]{0:T(128)}, s32[16]{0:T(128)S(1)}, u32[]{:S(2)}) copy-start(s32[16]{0:T(128)S(1)} %collective-permute-done.7.refs_1_) | copy-start | bytes 196
  80.9 13.7 %copy-start.16 = (s32[16]{0:T(128)}, s32[16]{0:T(128)S(1)}, u32[]{:S(2)}) copy-start(s32[16]{0:T(128)S(1)} %collective-permute-done.8.refs_2_) | copy-start | bytes 196
  80.9 13.6 %copy-start.17 = (s32[16]{0:T(128)}, s32[16]{0:T(128)S(1)}, u32[]{:S(2)}) copy-start(s32[16]{0:T(128)S(1)} %collective-permute-done.9.refs_3_) | copy-start | bytes 196
  80.9 63.3 %all-to-all-start.3 = ((bf16[8,2,48,1408]{3,2,1,0:T(8,128)(2,1)}), bf16[8,2,48,1408]{3,2,1,0:T(8,128)(2,1)}, u32[]{:S(2)}, u32[]{:S(2)}) async-start(bf16[8,2,48,1408]{3,2,1,0:T(8,128)(2,1)} %get-tuple-element.100), calls=%async_computation.3 | async-start | bytes 4325376 | tf_op jit(solution)/shard_map/all_to_all | solution.py:527
  86.7 1.4 copy-start.3
  88.1 1.8 %copy-start.5 = (bf16[8,2,5,48,384]{4,3,2,1,0:T(8,128)(2,1)S(1)}, bf16[8,2,5,48,384]{4,3,2,1,0:T(8,128)(2,1)}, u32[]{:S(2)}) copy-start(bf16[8,2,5,48,384]{4,3,2,1,0:T(8,128)(2,1)} %get-tuple-element.111.tile_ref) | copy-start | bytes 8847364
  94.6 0.9 copy-start.4
  94.6 49.6 %copy-start.8 = (bf16[8,2,48,512]{3,2,1,0:T(8,128)(2,1)S(1)}, bf16[8,2,48,512]{3,2,1,0:T(8,128)(2,1)}, u32[]{:S(2)}) copy-start(bf16[8,2,48,512]{3,2,1,0:T(8,128)(2,1)} %get-tuple-element.110) | copy-start | bytes 2359300
  95.5 24.0 %collective-permute-start.10 = (bf16[4,2,48,512]{3,2,1,0:T(8,128)(2,1)S(1)}, bf16[4,2,48,512]{3,2,1,0:T(8,128)(2,1)S(1)}, u32[]{:S(2)}, u32[]{:S(2)}) collective-permute-start(bf16[4,2,48,512]{3,2,1,0:T(8,128)(2,1)S(1)} %dynamic-slice_bitcast_fusion), channel_id=1, source_target_pairs={{0,1},{1,0},{2,3},{3,2},{4,5},{5,4},{6,7},{7,6},{8,9},{9,8},{10,11... | collective-permute-start | bytes 1179656 | tf_op jit(solution)/shard_map/ppermute | solution.py:19
  120.6 10.6 %collective-permute-start.11 = (bf16[2,48,512]{2,1,0:T(8,128)(2,1)S(1)}, bf16[2,48,512]{2,1,0:T(8,128)(2,1)S(1)}, u32[]{:S(2)}, u32[]{:S(2)}) collective-permute-start(bf16[2,48,512]{2,1,0:T(8,128)(2,1)S(1)} %get-tuple-element.113), channel_id=1, source_target_pairs={{0,2},{1,3},{2,0},{3,1},{4,6},{5,7},{6,4},{7,5},{8,10},{9,11},{10,... | collective-permute-start | bytes 294920 | tf_op jit(solution)/shard_map/ppermute | solution.py:19
  120.7 22.8 %collective-permute-start.12 = (bf16[2,48,512]{2,1,0:T(8,128)(2,1)S(1)}, bf16[2,48,512]{2,1,0:T(8,128)(2,1)S(1)}, u32[]{:S(2)}, u32[]{:S(2)}) collective-permute-start(bf16[2,48,512]{2,1,0:T(8,128)(2,1)S(1)} %get-tuple-element.115), channel_id=1, source_target_pairs={{0,4},{1,5},{2,6},{3,7},{4,0},{5,1},{6,2},{7,3},{8,12},{9,13},{10,... | collective-permute-start | bytes 294920 | tf_op jit(solution)/shard_map/ppermute | solution.py:19
  127.7 15.8 %collective-permute-start.13 = (bf16[2,48,512]{2,1,0:T(8,128)(2,1)S(1)}, bf16[2,48,512]{2,1,0:T(8,128)(2,1)S(1)}, u32[]{:S(2)}, u32[]{:S(2)}) collective-permute-start(bf16[2,48,512]{2,1,0:T(8,128)(2,1)S(1)} %get-tuple-element.114), channel_id=1, source_target_pairs={{0,6},{1,7},{2,4},{3,5},{4,2},{5,3},{6,0},{7,1},{8,14},{9,15},{10,... | collective-permute-start | bytes 294920 | tf_op jit(solution)/shard_map/ppermute | solution.py:19

commit v4 on v3

--- a/solution.py
+++ b/solution.py
@@ -241,10 +241,10 @@
     order_ref, source_counts_ref, offsets_ref, test_counts_ref, left_ref = refs[:5]
     shard_refs = refs[5 : 5 + nshard]
     j = pl.program_id(0)
-    if packed:
-        tile_ref, main_ref, over_ref, pack_ref = refs[5 + nshard :]
+    if not packed:
+        (tile_ref,) = refs[5 + nshard :]
     else:
-        *near_refs, tile_ref, joined_ref = refs[5 + nshard :]
+        *near_refs, tile_ref, main_ref, over_ref, joined_ref, pack_ref = refs[5 + nshard :]
 
         @pl.when(j == 0)
         def _():
@@ -325,7 +325,6 @@
             shapes.append(jax.ShapeDtypeStruct(shape, jnp.bfloat16))
             specs.append(pl.BlockSpec(shape, lambda j, *_: (0, 0, 0, 0)))
         scratch.append(pltpu.VMEM((ndest, ntest, rows, nsource * width + LANES), jnp.bfloat16))
-    else:
         shapes.append(jax.ShapeDtypeStruct(((1 + len(near)) * tables[1].shape[0],), jnp.int32))
         specs.append(pl.BlockSpec(memory_space=pltpu.SMEM))
     return pl.pallas_call(
@@ -401,7 +400,7 @@
             scratch_shapes=[pltpu.VMEM((ntest * ndest * rows, ncol), jnp.float32)],
         ),
         out_shape=sum_shape,
-        compiler_params=pltpu.CompilerParams(vmem_limit_bytes=SMALL_VMEM_LIMIT),
+        compiler_params=pltpu.CompilerParams(vmem_limit_bytes=VMEM_LIMIT),
         cost_estimate=pl.CostEstimate(
             flops=2 * ndest * ntest * rows * width * ncol * nsource,
             bytes_accessed=2 * ndest * ntest * rows * width * nsource,
@@ -510,23 +509,25 @@
 
     left_a = left_products(ntest_axis, me, order, test_points, source_points, test_basis, 0, cut)
     shards_a, left_a = gather("a", basis_a, left_a)
-    inner = max(1, nsrc // 4)
-    near = [exchange(source_counts, "src", flip) for flip in range(1, inner)]
-    *near, left_a = lax.optimization_barrier((*near, left_a))
-    tiles_a, joined = tiles(nsrc, 0, tables, test_counts, left_a, shards_a, None, near)
-    groups = [joined] + [exchange(joined, "src", flip) for flip in range(inner, nsrc, inner)]
+    (tiles_a,) = tiles(nsrc, 0, tables, test_counts, left_a, shards_a, None)
     moved_a = lax.all_to_all(tiles_a, "src", split_axis=0, concat_axis=0, tiled=True)
 
     rest, _ = lax.optimization_barrier((basis_b, held["a"]))
     later, _ = lax.optimization_barrier((source_points, tiles_a))
     left_b = left_products(ntest_axis, me, order, test_points, later, test_basis, cut, nsource)
     shards_b, left_b = gather("b", rest, left_b)
-    tiles_b, packed, beyond = tiles(nsrc, cut, tables, test_counts, left_b, shards_b, main)
-    sums_a = project(order, 0, tiles_a, coefficients, None)
-    packed, sums_a, *groups = lax.optimization_barrier((packed, sums_a, *groups))
+    inner = max(1, nsrc // 4)
+    counts, _ = lax.optimization_barrier((source_counts, left_b))
+    near = [exchange(counts, "src", flip) for flip in range(1, inner)]
+    tiles_b, packed, beyond, joined = tiles(
+        nsrc, cut, tables, test_counts, left_b, shards_b, main, near
+    )
+    groups = [joined] + [exchange(joined, "src", flip) for flip in range(inner, nsrc, inner)]
+    packed, *groups = lax.optimization_barrier((packed, *groups))
     moved_b = lax.all_to_all(packed, "src", split_axis=0, concat_axis=0, tiled=True)
 
-    sums = project(order, cut, tiles_b, coefficients, sums_a)
+    sums = project(order, 0, tiles_a, coefficients, None)
+    sums = project(order, cut, tiles_b, coefficients, sums)
     projected = sum_rows(sums, "src")
     me_src, _ = lax.optimization_barrier((jnp.reshape(lax.axis_index("src"), (1,)), packed))
     all_counts, all_order, all_offsets, branch = all_tables(cut, nsource, widths, me_src, groups)

time: 153 us -> 154 us (level)
  Pallas kernels: 71.5 us -> 77.7 us
  local copies, waits for them, and re-layouts: 7.84 us -> 4.38 us
    pallas_call x2, Pallas kernels: 7.61 us -> 13.6 us  [project(): pl.pallas_call(project_kernel, grid_spec=pltpu.PrefetchScalarGridSpec(num...]
    unnamed x36 -> x20, local copies, waits for them, and re-layouts: 7.79 us -> 2.65 us
    all_to_all x1, starting transfers between devices: 5.71 us -> 3.79 us  [body(): lax.all_to_all(packed, 'src', split_axis=0, concat_axis=0, tiled=True)]
  transfers between devices with their start and end apart: 16 -> 16, of which waited for: 4 -> 8; matrix products, arithmetic and copies ran while one was open for 1% -> 3% of each run, Pallas kernels for 36% -> 39%
where the time goes in v4:
time: 154 us; the launch traced here: 153 us
  Pallas kernels  77.7 us (50%)
  waiting for transfers between devices  37 us (24%)
  starting transfers between devices  30.2 us (20%)
  local copies, waits for them, and re-layouts  4.38 us (3%)
  other arithmetic  2.8 us (2%)
    ppermute x14, waiting for transfers between devices, exchange(): return lax.ppermute(x, axis, [(a, a ^ flip) for a in range(size)])  37 us
    pallas_call x2, Pallas kernels, left_products(): pl.pallas_call(functools.partial(left_kernel, nshard, first), grid_spec=p...  33.2 us
    ppermute x14, starting transfers between devices, exchange(): return lax.ppermute(x, axis, [(a, a ^ flip) for a in range(size)])  20.4 us
    pallas_call x2, Pallas kernels, tiles(): pl.pallas_call(functools.partial(tile_kernel, nshard, first, packed), gri...  17.8 us
    pallas_call x2, Pallas kernels, project(): pl.pallas_call(project_kernel, grid_spec=pltpu.PrefetchScalarGridSpec(num...  13.6 us
    pallas_call x1, Pallas kernels, unpack(): pl.pallas_call(functools.partial(unpack_kernel, cut), grid_spec=pltpu.Pre...  7.58 us
    all_to_all x1, starting transfers between devices, body(): lax.all_to_all(tiles_a, 'src', split_axis=0, concat_axis=0, tiled=True)  6.09 us
    all_to_all x1, starting transfers between devices, body(): lax.all_to_all(packed, 'src', split_axis=0, concat_axis=0, tiled=True)  3.79 us
  transfers between devices with their start and end apart: 16, of which 8 were waited for; matrix products, arithmetic and copies ran while one was open for 3% of the time, Pallas kernels for 39%

profile of v4, /device:TPU:0, one launch (start us, length us, event | category | flops | bytes accessed | tf_op | source)
XLA Modules:
  0.0 153.4 jit_solution(13294014280506426708)
XLA Ops:
  0.6 2.9 %shard_map.86 = (s32[8]{0:T(128)}, s32[8]{0:T(128)}, bf16[3,256,384]{2,1,0:T(8,128)(2,1)}, bf16[5,256,384]{2,1,0:T(8,128)(2,1)}) custom-call(s32[8]{0:T(128)} %refs_1_.3, bf16[8,256,384]{2,1,0:T(8,128)(2,1)} %basis_ref.3), custom_call_target="tpu_custom_call" | custom-call | tf_op jit(solution)/shard_map/pallas_call | solution.py:85
  3.5 3.0 %collective-permute-start = (bf16[3,256,384]{2,1,0:T(8,128)(2,1)}, bf16[3,256,384]{2,1,0:T(8,128)(2,1)S(1)}, u32[]{:S(2)}, u32[]{:S(2)}) collective-permute-start(bf16[3,256,384]{2,1,0:T(8,128)(2,1)} %get-tuple-element.85.refs_5_), channel_id=1, source_target_pairs={{0,16},{8,24},{16,0},{24,8},{1,17},{9,25},{17,1},{25,9},{2,18},{10... | collective-permute-start | bytes 1769480 | tf_op jit(solution)/shard_map/ppermute | solution.py:19
  6.5 0.0 collective-permute-start.2
  6.5 13.5 %shard_map.87.refs_4_ = bf16[2,3,384,1024]{3,2,1,0:T(8,128)(2,1)} custom-call(s32[1]{0:T(128)} %bitcast.1.me_ref, s32[8]{0:T(128)} %get-tuple-element.82.order_ref.refs_0_, f32[3,2,1024]{2,1,0:T(2,128)} %bitcast.26, f32[3,8,1024]{2,1,0:T(8,128)} %bitcast.24, bf16[2,1024,384]{2,1,0:T(8,128)(2,1)} %basis_ref.5), custom_call_target="tpu_custom_call" | custom-call | flops 4831838208 | bytes 4718592 | tf_op jit(solution)/shard_map/pallas_call | solution.py:212
  20.0 0.1 collective-permute-done.refs_7_
  20.1 0.4 collective-permute-start.3
  20.5 0.0 collective-permute-done.2.refs_6_
  20.5 1.6 %collective-permute-done.3.refs_8_ = bf16[3,256,384]{2,1,0:T(8,128)(2,1)S(1)} collective-permute-done((bf16[3,256,384]{2,1,0:T(8,128)(2,1)S(1)}, bf16[3,256,384]{2,1,0:T(8,128)(2,1)S(1)}, u32[]{:S(2)}, u32[]{:S(2)}) %collective-permute-start.3) | collective-permute-done | bytes 589856 | tf_op jit(solution)/shard_map/ppermute | solution.py:19
  22.2 0.8 copy-done.6
  23.0 6.9 %shard_map.88.tile_ref = bf16[8,2,3,48,384]{4,3,2,1,0:T(8,128)(2,1)} custom-call(s32[8]{0:T(128)} %get-tuple-element.82.order_ref.refs_0_, s32[8]{0:T(128)} %refs_1_.3, s32[8]{0:T(128)} %get-tuple-element.83.refs_2_, s32[2]{0:T(128)} %refs_3_.3, bf16[2,3,384,1024]{3,2,1,0:T(8,128)(2,1)} %shard_map.87.refs_4_, ...), custom_call_target="tpu_custom_call" | custom-call | flops 1811939328 | bytes 6488064 | tf_op jit(solution)/shard_map/pallas_call | solution.py:330
  29.9 6.1 %all-to-all-start.2 = ((bf16[8,2,3,48,384]{4,3,2,1,0:T(8,128)(2,1)}), bf16[8,2,3,48,384]{4,3,2,1,0:T(8,128)(2,1)S(1)}, u32[]{:S(2)}, u32[]{:S(2)}) async-start(bf16[8,2,3,48,384]{4,3,2,1,0:T(8,128)(2,1)} %shard_map.88.tile_ref), calls=%async_computation.2 | async-start | bytes 3538944 | tf_op jit(solution)/shard_map/all_to_all | solution.py:513
  36.0 0.0 copy-start.7
  36.0 1.6 %collective-permute-start.1 = (bf16[5,256,384]{2,1,0:T(8,128)(2,1)S(1)}, bf16[5,256,384]{2,1,0:T(8,128)(2,1)}, u32[]{:S(2)}, u32[]{:S(2)}) collective-permute-start(bf16[5,256,384]{2,1,0:T(8,128)(2,1)S(1)} %copy-done.3), channel_id=1, source_target_pairs={{0,16},{8,24},{16,0},{24,8},{1,17},{9,25},{17,1},{25,9},{2,18},{10... | collective-permute-start | bytes 2949128 | tf_op jit(solution)/shard_map/ppermute | solution.py:19
  37.6 0.0 collective-permute-start.4
  37.6 19.7 %shard_map.89.refs_4_ = bf16[2,5,384,1024]{3,2,1,0:T(8,128)(2,1)} custom-call(s32[1]{0:T(128)} %bitcast.1.me_ref, s32[8]{0:T(128)} %get-tuple-element.82.order_ref.refs_0_, f32[3,2,1024]{2,1,0:T(2,128)} %bitcast.27, f32[3,8,1024]{2,1,0:T(8,128)} %bitcast.25, bf16[2,1024,384]{2,1,0:T(8,128)(2,1)} %basis_ref.5), custom_call_target="tpu_custom_call" | custom-call | flops 8053063680 | bytes 7864320 | tf_op jit(solution)/shard_map/pallas_call | solution.py:212
  57.3 2.5 %collective-permute-done.1.refs_7_ = bf16[5,256,384]{2,1,0:T(8,128)(2,1)} collective-permute-done((bf16[5,256,384]{2,1,0:T(8,128)(2,1)S(1)}, bf16[5,256,384]{2,1,0:T(8,128)(2,1)}, u32[]{:S(2)}, u32[]{:S(2)}) %collective-permute-start.1) | collective-permute-done | bytes 983072 | tf_op jit(solution)/shard_map/ppermute | solution.py:19
  59.8 0.0 collective-permute-start.5
  59.8 1.7 %collective-permute-start.6 = (s32[8]{0:T(128)S(1)}, s32[8]{0:T(128)S(1)}, u32[]{:S(2)}, u32[]{:S(2)}) collective-permute-start(s32[8]{0:T(128)S(1)} %copy-done.7), channel_id=1, source_target_pairs={{0,1},{1,0},{2,3},{3,2},{4,5},{5,4},{6,7},{7,6},{8,9},{9,8},{10,11... | collective-permute-start | bytes 104 | tf_op jit(solution)/shard_map/ppermute | solution.py:19
  61.5 0.0 collective-permute-done.4.refs_6_
  61.5 1.8 %collective-permute-done.6.refs_9_ = s32[8]{0:T(128)S(1)} collective-permute-done((s32[8]{0:T(128)S(1)}, s32[8]{0:T(128)S(1)}, u32[]{:S(2)}, u32[]{:S(2)}) %collective-permute-start.6) | collective-permute-done | bytes 64 | tf_op jit(solution)/shard_map/ppermute | solution.py:19
  63.3 0.0 collective-permute-done.5.refs_8_
  63.3 0.6 copy-done.8
  63.9 10.9 %shard_map.90 = (bf16[8,2,5,48,384]{4,3,2,1,0:T(8,128)(2,1)}, bf16[8,2,48,1408]{3,2,1,0:T(8,128)(2,1)}, bf16[8,2,48,512]{3,2,1,0:T(8,128)(2,1)S(1)}, s32[16]{0:T(128)}) custom-call(s32[8]{0:T(128)} %get-tuple-element.82.order_ref.refs_0_, s32[8]{0:T(128)} %refs_1_.3, s32[8]{0:T(128)} %get-tuple-element.83.refs_2_, s32[2]{0:T(128)} %refs_3_.3, ...), custom_call_target="tpu_custom_call" | custom-call | flops 3019898880 | bytes 10813440 | tf_op jit(solution)/shard_map/pallas_call | solution.py:330
  74.8 1.8 %collective-permute-start.7 = (s32[16]{0:T(128)}, s32[16]{0:T(128)S(1)}, u32[]{:S(2)}, u32[]{:S(2)}) collective-permute-start(s32[16]{0:T(128)} %get-tuple-element.97.refs_0_), channel_id=1, source_target_pairs={{0,2},{1,3},{2,0},{3,1},{4,6},{5,7},{6,4},{7,5},{8,10},{9,11},{10,... | collective-permute-start | bytes 200 | tf_op jit(solution)/shard_map/ppermute | solution.py:19
  76.5 2.4 %collective-permute-start.8 = (s32[16]{0:T(128)}, s32[16]{0:T(128)S(1)}, u32[]{:S(2)}, u32[]{:S(2)}) collective-permute-start(s32[16]{0:T(128)} %get-tuple-element.97.refs_0_), channel_id=1, source_target_pairs={{0,4},{1,5},{2,6},{3,7},{4,0},{5,1},{6,2},{7,3},{8,12},{9,13},{10,... | collective-permute-start | bytes 200 | tf_op jit(solution)/shard_map/ppermute | solution.py:19
  78.9 0.3 collective-permute-start.9
  79.2 2.0 %collective-permute-done.8.refs_2_ = s32[16]{0:T(128)S(1)} collective-permute-done((s32[16]{0:T(128)}, s32[16]{0:T(128)S(1)}, u32[]{:S(2)}, u32[]{:S(2)}) %collective-permute-start.8) | collective-permute-done | bytes 96 | tf_op jit(solution)/shard_map/ppermute | solution.py:19
  81.2 3.3 %collective-permute-done.9.refs_3_ = s32[16]{0:T(128)S(1)} collective-permute-done((s32[16]{0:T(128)}, s32[16]{0:T(128)S(1)}, u32[]{:S(2)}, u32[]{:S(2)}) %collective-permute-start.9) | collective-permute-done | bytes 96 | tf_op jit(solution)/shard_map/ppermute | solution.py:19
  84.5 0.6 copy-done.11
  85.0 0.7 copy-done
  85.7 3.8 %all-to-all-start.3 = ((bf16[8,2,48,1408]{3,2,1,0:T(8,128)(2,1)}), bf16[8,2,48,1408]{3,2,1,0:T(8,128)(2,1)S(1)}, u32[]{:S(2)}, u32[]{:S(2)}) async-start(bf16[8,2,48,1408]{3,2,1,0:T(8,128)(2,1)} %get-tuple-element.95), calls=%async_computation.3 | async-start | bytes 4325376 | tf_op jit(solution)/shard_map/all_to_all | solution.py:527
  89.5 5.7 %shard_map.92.refs_0_ = f32[768,512]{1,0:T(8,128)} custom-call(s32[8]{0:T(128)} %get-tuple-element.82.order_ref.refs_0_, bf16[8,2,3,48,384]{4,3,2,1,0:T(8,128)(2,1)} %shard_map.88.tile_ref, bf16[8,384,512]{2,1,0:T(8,128)(2,1)} %coeff_ref.3), custom_call_target="tpu_custom_call" | custom-call | flops 905969664 | bytes 1769472 | tf_op jit(solution)/shard_map/pallas_call | solution.py:389
  95.2 7.9 %shard_map.93 = bf16[8,2,48,512]{3,2,1,0:T(8,128)(2,1)} custom-call(s32[8]{0:T(128)} %get-tuple-element.82.order_ref.refs_0_, bf16[8,2,5,48,384]{4,3,2,1,0:T(8,128)(2,1)} %get-tuple-element.106.tile_ref, bf16[8,384,512]{2,1,0:T(8,128)(2,1)} %coeff_ref.3, f32[768,512]{1,0:T(8,128)} %shard_map.92.refs_0_), custom_call_target="tpu_custom_call" | custom-call | flops 1509949440 | bytes 2949120 | tf_op jit(solution)/shard_map/pallas_call | solution.py:389
  103.1 1.0 dynamic-slice_bitcast_fusion
  104.2 1.8 %collective-permute-start.10 = (bf16[4,2,48,512]{3,2,1,0:T(8,128)(2,1)S(1)}, bf16[4,2,48,512]{3,2,1,0:T(8,128)(2,1)}, u32[]{:S(2)}, u32[]{:S(2)}) collective-permute-start(bf16[4,2,48,512]{3,2,1,0:T(8,128)(2,1)S(1)} %dynamic-slice_bitcast_fusion), channel_id=1, source_target_pairs={{0,1},{1,0},{2,3},{3,2},{4,5},{5,4},{6,7},{7,6},{8,9},{9,8},{10,11... | collective-permute-start | bytes 1179656 | tf_op jit(solution)/shard_map/ppermute | solution.py:19
  105.9 15.9 %collective-permute-done.10 = bf16[4,2,48,512]{3,2,1,0:T(8,128)(2,1)} collective-permute-done((bf16[4,2,48,512]{3,2,1,0:T(8,128)(2,1)S(1)}, bf16[4,2,48,512]{3,2,1,0:T(8,128)(2,1)}, u32[]{:S(2)}, u32[]{:S(2)}) %collective-permute-start.10) | collective-permute-done | bytes 393248 | tf_op jit(solution)/shard_map/ppermute | solution.py:19
  121.8 1.2 fusion
  123.0 0.7 dynamic-slice_bitcast_fusion.3
  123.8 0.0 collective-permute-start.11
  123.8 7.3 %collective-permute-start.12 = (bf16[2,48,512]{2,1,0:T(8,128)(2,1)}, bf16[2,48,512]{2,1,0:T(8,128)(2,1)S(1)}, u32[]{:S(2)}, u32[]{:S(2)}) collective-permute-start(bf16[2,48,512]{2,1,0:T(8,128)(2,1)} %get-tuple-element.109), channel_id=1, source_target_pairs={{0,4},{1,5},{2,6},{3,7},{4,0},{5,1},{6,2},{7,3},{8,12},{9,13},{10,... | collective-permute-start | bytes 294920 | tf_op jit(solution)/shard_map/ppermute | solution.py:19
  131.1 2.7 %shard_map.91 = (s32[64]{0:T(128)S(1)}, s32[64]{0:T(128)S(1)}, s32[64]{0:T(128)S(1)}, s32[1]{0:T(128)}) custom-call(s32[1]{0:T(128)} %bitcast.me_ref, s32[16]{0:T(128)} %get-tuple-element.97.refs_0_, s32[16]{0:T(128)} %copy-done.9, s32[16]{0:T(128)} %copy-done.10, s32[16]{0:T(128)} %copy-done.11), custom_call_target="tpu_custom_call" | custom-call | tf_op jit(solution)/shard_map/pallas_call | solution.py:130
  134.4 0.0 collective-permute-done.11
  134.4 9.8 %collective-permute-done.12 = bf16[2,48,512]{2,1,0:T(8,128)(2,1)S(1)} collective-permute-done((bf16[2,48,512]{2,1,0:T(8,128)(2,1)}, bf16[2,48,512]{2,1,0:T(8,128)(2,1)S(1)}, u32[]{:S(2)}, u32[]{:S(2)}) %collective-permute-start.12) | collective-permute-done | bytes 98336 | tf_op jit(solution)/shard_map/ppermute | solution.py:19
  144.3 0.0 collective-permute-done.13
  144.3 1.6 %fusion.3 = bf16[2,48,512]{2,1,0:T(8,128)(2,1)} fusion(bf16[2,48,512]{2,1,0:T(8,128)(2,1)} %collective-permute-done.13, bf16[2,48,512]{2,1,0:T(8,128)(2,1)S(1)} %collective-permute-done.12, bf16[2,48,512]{2,1,0:T(8,128)(2,1)S(1)} %collective-permute-done.11, bf16[4,2,48,512]{3,2,1,0:T(8,128)(2,1)S(1)} %fusion, s32[]{:T(128)S(6)} %select_n.36), kind=kLoop, calls=%fused_computation.8 | loop fusion | flops 393216 | bytes 491524 | tf_op jit(solution)/shard_map/convert_element_type | solution.py:46
  145.8 0.0 all-to-all-done.3
  145.9 7.6 %conditional.1 = (bf16[2,48,64,384]{3,2,1,0:T(8,128)(2,1)}) conditional(s32[]{:T(128)} %bitcast.4, (s32[64]{0:T(128)S(1)}, s32[64]{0:T(128)S(1)}, s32[64]{0:T(128)S(1)}, bf16[8,2,3,48,384]{4,3,2,1,0:T(8,128)(2,1)}, bf16[8,2,48,1408]{3,2,1,0:T(8,128)(2,1)S(1)}) %tuple.39, (bf16[8,2,48,512]{3,2,1,0:T(8,128)(2,1)S(1)}, ...), branch_computations={%region_0.1_spmd, %region_1.2_spmd, %region_2.3_spmd} | conditional | flops 5898240 | bytes 14549028 | solution.py:544
  145.9 7.6 %branch_0_fun.1 = bf16[2,48,64,384]{3,2,1,0:T(8,128)(2,1)} custom-call(s32[64]{0:T(128)S(1)} %get-tuple-element.26.order_ref, s32[64]{0:T(128)S(1)} %get-tuple-element.27.counts_ref, s32[64]{0:T(128)S(1)} %get-tuple-element.40.offsets_ref, bf16[8,2,3,48,384]{4,3,2,1,0:T(8,128)(2,1)} %get-tuple-element.41.whole_ref, ...), custom_call_target="tpu_custom_call" | custom-call | tf_op jit(solution)/shard_map/cond/branch_0_fun/pallas_call | solution.py:457
  (18 shorter events, 0.0 us)
Async XLA Ops:
  3.5 16.6 %collective-permute-start = (bf16[3,256,384]{2,1,0:T(8,128)(2,1)}, bf16[3,256,384]{2,1,0:T(8,128)(2,1)S(1)}, u32[]{:S(2)}, u32[]{:S(2)}) collective-permute-start(bf16[3,256,384]{2,1,0:T(8,128)(2,1)} %get-tuple-element.85.refs_5_), channel_id=1, source_target_pairs={{0,16},{8,24},{16,0},{24,8},{1,17},{9,25},{17,1},{25,9},{2,18},{10... | collective-permute-start | bytes 1769480 | tf_op jit(solution)/shard_map/ppermute | solution.py:19
  6.5 14.0 %collective-permute-start.2 = (bf16[3,256,384]{2,1,0:T(8,128)(2,1)}, bf16[3,256,384]{2,1,0:T(8,128)(2,1)S(1)}, u32[]{:S(2)}, u32[]{:S(2)}) collective-permute-start(bf16[3,256,384]{2,1,0:T(8,128)(2,1)} %get-tuple-element.85.refs_5_), channel_id=1, source_target_pairs={{0,8},{8,0},{16,24},{24,16},{1,9},{9,1},{17,25},{25,17},{2,10},{10... | collective-permute-start | bytes 1769480 | tf_op jit(solution)/shard_map/ppermute | solution.py:19
  20.1 2.1 %copy-start.4 = (bf16[3,256,384]{2,1,0:T(8,128)(2,1)}, bf16[3,256,384]{2,1,0:T(8,128)(2,1)S(1)}, u32[]{:S(2)}) copy-start(bf16[3,256,384]{2,1,0:T(8,128)(2,1)S(1)} %collective-permute-done.refs_7_) | copy-start | bytes 1769476
  20.1 2.1 %collective-permute-start.3 = (bf16[3,256,384]{2,1,0:T(8,128)(2,1)S(1)}, bf16[3,256,384]{2,1,0:T(8,128)(2,1)S(1)}, u32[]{:S(2)}, u32[]{:S(2)}) collective-permute-start(bf16[3,256,384]{2,1,0:T(8,128)(2,1)S(1)} %collective-permute-done.refs_7_), channel_id=1, source_target_pairs={{0,8},{8,0},{16,24},{24,16},{1,9},{9,1},{17,25},{25,17},{2,10},{10... | collective-permute-start | bytes 1769480 | tf_op jit(solution)/shard_map/ppermute | solution.py:19
  20.5 1.6 %copy-start.5 = (bf16[3,256,384]{2,1,0:T(8,128)(2,1)}, bf16[3,256,384]{2,1,0:T(8,128)(2,1)S(1)}, u32[]{:S(2)}) copy-start(bf16[3,256,384]{2,1,0:T(8,128)(2,1)S(1)} %collective-permute-done.2.refs_6_) | copy-start | bytes 1769476
  22.2 0.8 copy-start.6
  29.9 6.1 %copy-start.3 = (bf16[5,256,384]{2,1,0:T(8,128)(2,1)S(1)}, bf16[5,256,384]{2,1,0:T(8,128)(2,1)}, u32[]{:S(2)}) copy-start(bf16[5,256,384]{2,1,0:T(8,128)(2,1)} %get-tuple-element.86.refs_5_) | copy-start | bytes 2949124
  29.9 54.6 %all-to-all-start.2 = ((bf16[8,2,3,48,384]{4,3,2,1,0:T(8,128)(2,1)}), bf16[8,2,3,48,384]{4,3,2,1,0:T(8,128)(2,1)S(1)}, u32[]{:S(2)}, u32[]{:S(2)}) async-start(bf16[8,2,3,48,384]{4,3,2,1,0:T(8,128)(2,1)} %shard_map.88.tile_ref), calls=%async_computation.2 | async-start | bytes 3538944 | tf_op jit(solution)/shard_map/all_to_all | solution.py:513
  36.0 23.8 %copy-start.7 = (s32[8]{0:T(128)S(1)}, s32[8]{0:T(128)}, u32[]{:S(2)}) copy-start(s32[8]{0:T(128)} %refs_1_.3) | copy-start | bytes 100
  36.0 23.8 %collective-permute-start.1 = (bf16[5,256,384]{2,1,0:T(8,128)(2,1)S(1)}, bf16[5,256,384]{2,1,0:T(8,128)(2,1)}, u32[]{:S(2)}, u32[]{:S(2)}) collective-permute-start(bf16[5,256,384]{2,1,0:T(8,128)(2,1)S(1)} %copy-done.3), channel_id=1, source_target_pairs={{0,16},{8,24},{16,0},{24,8},{1,17},{9,25},{17,1},{25,9},{2,18},{10... | collective-permute-start | bytes 2949128 | tf_op jit(solution)/shard_map/ppermute | solution.py:19
  37.6 23.9 %collective-permute-start.4 = (bf16[5,256,384]{2,1,0:T(8,128)(2,1)S(1)}, bf16[5,256,384]{2,1,0:T(8,128)(2,1)}, u32[]{:S(2)}, u32[]{:S(2)}) collective-permute-start(bf16[5,256,384]{2,1,0:T(8,128)(2,1)S(1)} %copy-done.3), channel_id=1, source_target_pairs={{0,8},{8,0},{16,24},{24,16},{1,9},{9,1},{17,25},{25,17},{2,10},{10... | collective-permute-start | bytes 2949128 | tf_op jit(solution)/shard_map/ppermute | solution.py:19
  59.8 3.6 %collective-permute-start.5 = (bf16[5,256,384]{2,1,0:T(8,128)(2,1)}, bf16[5,256,384]{2,1,0:T(8,128)(2,1)}, u32[]{:S(2)}, u32[]{:S(2)}) collective-permute-start(bf16[5,256,384]{2,1,0:T(8,128)(2,1)} %collective-permute-done.1.refs_7_), channel_id=1, source_target_pairs={{0,8},{8,0},{16,24},{24,16},{1,9},{9,1},{17,25},{25,17},{2,10},{10... | collective-permute-start | bytes 2949128 | tf_op jit(solution)/shard_map/ppermute | solution.py:19
  59.8 3.5 %collective-permute-start.6 = (s32[8]{0:T(128)S(1)}, s32[8]{0:T(128)S(1)}, u32[]{:S(2)}, u32[]{:S(2)}) collective-permute-start(s32[8]{0:T(128)S(1)} %copy-done.7), channel_id=1, source_target_pairs={{0,1},{1,0},{2,3},{3,2},{4,5},{5,4},{6,7},{7,6},{8,9},{9,8},{10,11... | collective-permute-start | bytes 104 | tf_op jit(solution)/shard_map/ppermute | solution.py:19
  63.3 0.6 copy-start.8
  74.8 4.5 %collective-permute-start.7 = (s32[16]{0:T(128)}, s32[16]{0:T(128)S(1)}, u32[]{:S(2)}, u32[]{:S(2)}) collective-permute-start(s32[16]{0:T(128)} %get-tuple-element.97.refs_0_), channel_id=1, source_target_pairs={{0,2},{1,3},{2,0},{3,1},{4,6},{5,7},{6,4},{7,5},{8,10},{9,11},{10,... | collective-permute-start | bytes 200 | tf_op jit(solution)/shard_map/ppermute | solution.py:19
  76.5 4.7 %collective-permute-start.8 = (s32[16]{0:T(128)}, s32[16]{0:T(128)S(1)}, u32[]{:S(2)}, u32[]{:S(2)}) collective-permute-start(s32[16]{0:T(128)} %get-tuple-element.97.refs_0_), channel_id=1, source_target_pairs={{0,4},{1,5},{2,6},{3,7},{4,0},{5,1},{6,2},{7,3},{8,12},{9,13},{10,... | collective-permute-start | bytes 200 | tf_op jit(solution)/shard_map/ppermute | solution.py:19
  78.9 5.5 %collective-permute-start.9 = (s32[16]{0:T(128)}, s32[16]{0:T(128)S(1)}, u32[]{:S(2)}, u32[]{:S(2)}) collective-permute-start(s32[16]{0:T(128)} %get-tuple-element.97.refs_0_), channel_id=1, source_target_pairs={{0,6},{1,7},{2,4},{3,5},{4,2},{5,3},{6,0},{7,1},{8,14},{9,15},{10,... | collective-permute-start | bytes 200 | tf_op jit(solution)/shard_map/ppermute | solution.py:19
  79.2 16.0 %copy-start.9 = (s32[16]{0:T(128)}, s32[16]{0:T(128)S(1)}, u32[]{:S(2)}) copy-start(s32[16]{0:T(128)S(1)} %collective-permute-done.7.refs_1_) | copy-start | bytes 196
  81.2 3.3 %copy-start.10 = (s32[16]{0:T(128)}, s32[16]{0:T(128)S(1)}, u32[]{:S(2)}) copy-start(s32[16]{0:T(128)S(1)} %collective-permute-done.8.refs_2_) | copy-start | bytes 196
  84.5 0.6 copy-start.11
  84.5 1.2 copy-start
  85.7 60.1 %all-to-all-start.3 = ((bf16[8,2,48,1408]{3,2,1,0:T(8,128)(2,1)}), bf16[8,2,48,1408]{3,2,1,0:T(8,128)(2,1)S(1)}, u32[]{:S(2)}, u32[]{:S(2)}) async-start(bf16[8,2,48,1408]{3,2,1,0:T(8,128)(2,1)} %get-tuple-element.95), calls=%async_computation.3 | async-start | bytes 4325376 | tf_op jit(solution)/shard_map/all_to_all | solution.py:527
  104.2 17.7 %collective-permute-start.10 = (bf16[4,2,48,512]{3,2,1,0:T(8,128)(2,1)S(1)}, bf16[4,2,48,512]{3,2,1,0:T(8,128)(2,1)}, u32[]{:S(2)}, u32[]{:S(2)}) collective-permute-start(bf16[4,2,48,512]{3,2,1,0:T(8,128)(2,1)S(1)} %dynamic-slice_bitcast_fusion), channel_id=1, source_target_pairs={{0,1},{1,0},{2,3},{3,2},{4,5},{5,4},{6,7},{7,6},{8,9},{9,8},{10,11... | collective-permute-start | bytes 1179656 | tf_op jit(solution)/shard_map/ppermute | solution.py:19
  123.8 10.7 %collective-permute-start.11 = (bf16[2,48,512]{2,1,0:T(8,128)(2,1)}, bf16[2,48,512]{2,1,0:T(8,128)(2,1)S(1)}, u32[]{:S(2)}, u32[]{:S(2)}) collective-permute-start(bf16[2,48,512]{2,1,0:T(8,128)(2,1)} %get-tuple-element.107), channel_id=1, source_target_pairs={{0,2},{1,3},{2,0},{3,1},{4,6},{5,7},{6,4},{7,5},{8,10},{9,11},{10,... | collective-permute-start | bytes 294920 | tf_op jit(solution)/shard_map/ppermute | solution.py:19
  123.8 20.5 %collective-permute-start.12 = (bf16[2,48,512]{2,1,0:T(8,128)(2,1)}, bf16[2,48,512]{2,1,0:T(8,128)(2,1)S(1)}, u32[]{:S(2)}, u32[]{:S(2)}) collective-permute-start(bf16[2,48,512]{2,1,0:T(8,128)(2,1)} %get-tuple-element.109), channel_id=1, source_target_pairs={{0,4},{1,5},{2,6},{3,7},{4,0},{5,1},{6,2},{7,3},{8,12},{9,13},{10,... | collective-permute-start | bytes 294920 | tf_op jit(solution)/shard_map/ppermute | solution.py:19
  131.1 13.2 %collective-permute-start.13 = (bf16[2,48,512]{2,1,0:T(8,128)(2,1)}, bf16[2,48,512]{2,1,0:T(8,128)(2,1)}, u32[]{:S(2)}, u32[]{:S(2)}) collective-permute-start(bf16[2,48,512]{2,1,0:T(8,128)(2,1)} %get-tuple-element.108), channel_id=1, source_target_pairs={{0,6},{1,7},{2,4},{3,5},{4,2},{5,3},{6,0},{7,1},{8,14},{9,15},{10,... | collective-permute-start | bytes 294920 | tf_op jit(solution)/shard_map/ppermute | solution.py:19

commit v5 on v3

--- a/solution.py
+++ b/solution.py
@@ -98,14 +98,15 @@
 
 def tables_kernel(cut, nblock, widths, me_ref, *refs):
     *group_refs, counts_ref, order_ref, offsets_ref, branch_ref, joined_ref = refs
-    group = group_refs[0].shape[0]
+    group, inner = group_refs[0].shape[0], len(group_refs)
     for place, group_ref in enumerate(group_refs):
         for k in range(group):
             joined_ref[place * group + k] = group_ref[k]
 
     def step(source, need):
         base = source * nblock
-        theirs = (source ^ me_ref[0]) * nblock
+        offset = source ^ me_ref[0]
+        theirs = (offset % inner) * group + (offset // inner) * nblock
         counts = [joined_ref[theirs + j] for j in range(nblock)]
         ranks, offsets = rank_blocks(counts, cut)
         used = jnp.int32(0)
@@ -244,14 +245,14 @@
     if packed:
         tile_ref, main_ref, over_ref, pack_ref = refs[5 + nshard :]
     else:
-        *near_refs, tile_ref, joined_ref = refs[5 + nshard :]
+        *far_refs, tile_ref, joined_ref = refs[5 + nshard :]
 
         @pl.when(j == 0)
         def _():
             nblock = source_counts_ref.shape[0]
-            for place, near_ref in enumerate([source_counts_ref] + near_refs):
+            for place, far_ref in enumerate([source_counts_ref] + far_refs):
                 for k in range(nblock):
-                    joined_ref[place * nblock + k] = near_ref[k]
+                    joined_ref[place * nblock + k] = far_ref[k]
 
     ntest, _, kmax, _ = left_ref.shape
     ndest, _, _, rows, width = tile_ref.shape
@@ -310,7 +311,7 @@
             over_ref[...] = pack_ref[:, :, :, main : main + over_ref.shape[3]]
 
 
-def tiles(ndest, first, tables, test_counts, left, shards, main, near=()):
+def tiles(ndest, first, tables, test_counts, left, shards, main, far=()):
     ntest, nsource, kmax, nq = left.shape
     nshard = len(shards)
     part, width = shards[0].shape[1:]
@@ -326,7 +327,7 @@
             specs.append(pl.BlockSpec(shape, lambda j, *_: (0, 0, 0, 0)))
         scratch.append(pltpu.VMEM((ndest, ntest, rows, nsource * width + LANES), jnp.bfloat16))
     else:
-        shapes.append(jax.ShapeDtypeStruct(((1 + len(near)) * tables[1].shape[0],), jnp.int32))
+        shapes.append(jax.ShapeDtypeStruct(((1 + len(far)) * tables[1].shape[0],), jnp.int32))
         specs.append(pl.BlockSpec(memory_space=pltpu.SMEM))
     return pl.pallas_call(
         functools.partial(tile_kernel, nshard, first, packed),
@@ -335,7 +336,7 @@
             grid=(nsource,),
             in_specs=[pl.BlockSpec((ntest, 1, kmax, nq), lambda j, *_: (0, j, 0, 0))]
             + [pl.BlockSpec((1, part, width), lambda j, *_: (j, 0, 0))] * nshard
-            + [pl.BlockSpec(memory_space=pltpu.SMEM)] * len(near),
+            + [pl.BlockSpec(memory_space=pltpu.SMEM)] * len(far),
             out_specs=specs,
             scratch_shapes=scratch,
         ),
@@ -346,7 +347,7 @@
             bytes_accessed=2 * ntest * nsource * kmax * (nq + width),
             transcendentals=0,
         ),
-    )(*tables, test_counts, left, *shards, *near)
+    )(*tables, test_counts, left, *shards, *far)
 
 
 def project_kernel(order_ref, tile_ref, coeff_ref, *refs):
@@ -401,7 +402,7 @@
             scratch_shapes=[pltpu.VMEM((ntest * ndest * rows, ncol), jnp.float32)],
         ),
         out_shape=sum_shape,
-        compiler_params=pltpu.CompilerParams(vmem_limit_bytes=SMALL_VMEM_LIMIT),
+        compiler_params=pltpu.CompilerParams(vmem_limit_bytes=VMEM_LIMIT),
         cost_estimate=pl.CostEstimate(
             flops=2 * ndest * ntest * rows * width * ncol * nsource,
             bytes_accessed=2 * ndest * ntest * rows * width * nsource,
@@ -505,16 +506,15 @@
 
     order, offsets, basis_a, basis_b = pick(cut, source_counts, source_basis)
     tables = (order, source_counts, offsets)
+    inner = max(1, nsrc // 4)
+    far = [exchange(source_counts, "src", flip) for flip in range(inner, nsrc, inner)]
+    basis_a, *far = lax.optimization_barrier((basis_a, *far))
     me = jnp.reshape(me_test, (1,))
     test_points, source_points = test_points.transpose(1, 0, 2), source_points.transpose(1, 0, 2)
 
     left_a = left_products(ntest_axis, me, order, test_points, source_points, test_basis, 0, cut)
     shards_a, left_a = gather("a", basis_a, left_a)
-    inner = max(1, nsrc // 4)
-    near = [exchange(source_counts, "src", flip) for flip in range(1, inner)]
-    *near, left_a = lax.optimization_barrier((*near, left_a))
-    tiles_a, joined = tiles(nsrc, 0, tables, test_counts, left_a, shards_a, None, near)
-    groups = [joined] + [exchange(joined, "src", flip) for flip in range(inner, nsrc, inner)]
+    tiles_a, joined = tiles(nsrc, 0, tables, test_counts, left_a, shards_a, None, far)
     moved_a = lax.all_to_all(tiles_a, "src", split_axis=0, concat_axis=0, tiled=True)
 
     rest, _ = lax.optimization_barrier((basis_b, held["a"]))
@@ -522,11 +522,12 @@
     left_b = left_products(ntest_axis, me, order, test_points, later, test_basis, cut, nsource)
     shards_b, left_b = gather("b", rest, left_b)
     tiles_b, packed, beyond = tiles(nsrc, cut, tables, test_counts, left_b, shards_b, main)
-    sums_a = project(order, 0, tiles_a, coefficients, None)
-    packed, sums_a, *groups = lax.optimization_barrier((packed, sums_a, *groups))
     moved_b = lax.all_to_all(packed, "src", split_axis=0, concat_axis=0, tiled=True)
 
-    sums = project(order, cut, tiles_b, coefficients, sums_a)
+    joined, _ = lax.optimization_barrier((joined, packed))
+    groups = [joined] + [exchange(joined, "src", flip) for flip in range(1, inner)]
+    sums = project(order, 0, tiles_a, coefficients, None)
+    sums = project(order, cut, tiles_b, coefficients, sums)
     projected = sum_rows(sums, "src")
     me_src, _ = lax.optimization_barrier((jnp.reshape(lax.axis_index("src"), (1,)), packed))
     all_counts, all_order, all_offsets, branch = all_tables(cut, nsource, widths, me_src, groups)

time: 153 us -> 155 us (1.013)
  Pallas kernels: 71.5 us -> 78 us
  starting transfers between devices: 31.4 us -> 25.2 us
  waiting for transfers between devices: 38 us -> 43.2 us
  local copies, waits for them, and re-layouts: 7.84 us -> 3.82 us
    pallas_call x2, Pallas kernels: 7.61 us -> 13.7 us  [project(): pl.pallas_call(project_kernel, grid_spec=pltpu.PrefetchScalarGridSpec(num...]
    unnamed x36 -> x20, local copies, waits for them, and re-layouts: 7.79 us -> 2.07 us
    all_to_all x1, waiting for transfers between devices: 0.01 us -> 4.12 us  [body(): lax.all_to_all(tiles_a, 'src', split_axis=0, concat_axis=0, tiled=True)]
    ppermute x14, starting transfers between devices: 19.9 us -> 17.7 us  [exchange(): return lax.ppermute(x, axis, [(a, a ^ flip) for a in range(size)])]
    all_to_all x1, starting transfers between devices: 5.8 us -> 3.72 us  [body(): lax.all_to_all(tiles_a, 'src', split_axis=0, concat_axis=0, tiled=True)]
    all_to_all x1, starting transfers between devices: 5.71 us -> 3.79 us  [body(): lax.all_to_all(packed, 'src', split_axis=0, concat_axis=0, tiled=True)]
  transfers between devices with their start and end apart: 16 -> 16, of which waited for: 4 -> 9; matrix products, arithmetic and copies ran while one was open for 1% -> 3% of each run, Pallas kernels for 36% -> 41%
where the time goes in v5:
time: 155 us; the launch traced here: 154 us
  Pallas kernels  78 us (50%)
  waiting for transfers between devices  43.2 us (28%)
  starting transfers between devices  25.2 us (16%)
  local copies, waits for them, and re-layouts  3.82 us (2%)
  other arithmetic  2.8 us (2%)
    ppermute x14, waiting for transfers between devices, exchange(): return lax.ppermute(x, axis, [(a, a ^ flip) for a in range(size)])  39 us
    pallas_call x2, Pallas kernels, left_products(): pl.pallas_call(functools.partial(left_kernel, nshard, first), grid_spec=p...  33.4 us
    pallas_call x2, Pallas kernels, tiles(): pl.pallas_call(functools.partial(tile_kernel, nshard, first, packed), gri...  17.7 us
    ppermute x14, starting transfers between devices, exchange(): return lax.ppermute(x, axis, [(a, a ^ flip) for a in range(size)])  17.7 us
    pallas_call x2, Pallas kernels, project(): pl.pallas_call(project_kernel, grid_spec=pltpu.PrefetchScalarGridSpec(num...  13.7 us
    pallas_call x1, Pallas kernels, unpack(): pl.pallas_call(functools.partial(unpack_kernel, cut), grid_spec=pltpu.Pre...  7.58 us
    all_to_all x1, waiting for transfers between devices, body(): lax.all_to_all(tiles_a, 'src', split_axis=0, concat_axis=0, tiled=True)  4.12 us
    all_to_all x1, starting transfers between devices, body(): lax.all_to_all(packed, 'src', split_axis=0, concat_axis=0, tiled=True)  3.79 us
  transfers between devices with their start and end apart: 16, of which 9 were waited for; matrix products, arithmetic and copies ran while one was open for 3% of the time, Pallas kernels for 41%

profile of v5, /device:TPU:0, one launch (start us, length us, event | category | flops | bytes accessed | tf_op | source)
XLA Modules:
  0.0 154.4 jit_solution(3703811263179845012)
XLA Ops:
  0.6 3.1 %collective-permute-start = (s32[8]{0:T(128)}, s32[8]{0:T(128)S(1)}, u32[]{:S(2)}, u32[]{:S(2)}) collective-permute-start(s32[8]{0:T(128)} %refs_1_.3), channel_id=1, source_target_pairs={{0,2},{1,3},{2,0},{3,1},{4,6},{5,7},{6,4},{7,5},{8,10},{9,11},{10,... | collective-permute-start | bytes 104 | tf_op jit(solution)/shard_map/ppermute | solution.py:19
  3.7 2.6 %collective-permute-start.1 = (s32[8]{0:T(128)}, s32[8]{0:T(128)S(1)}, u32[]{:S(2)}, u32[]{:S(2)}) collective-permute-start(s32[8]{0:T(128)} %refs_1_.3), channel_id=1, source_target_pairs={{0,4},{1,5},{2,6},{3,7},{4,0},{5,1},{6,2},{7,3},{8,12},{9,13},{10,... | collective-permute-start | bytes 104 | tf_op jit(solution)/shard_map/ppermute | solution.py:19
  6.3 0.0 collective-permute-start.2
  6.3 2.9 %shard_map.86 = (s32[8]{0:T(128)}, s32[8]{0:T(128)}, bf16[3,256,384]{2,1,0:T(8,128)(2,1)}, bf16[5,256,384]{2,1,0:T(8,128)(2,1)}) custom-call(s32[8]{0:T(128)} %refs_1_.3, bf16[8,256,384]{2,1,0:T(8,128)(2,1)} %basis_ref.3), custom_call_target="tpu_custom_call" | custom-call | tf_op jit(solution)/shard_map/pallas_call | solution.py:85
  9.2 0.0 collective-permute-done.refs_9_
  9.2 0.0 collective-permute-done.1.refs_10_
  9.2 2.5 %collective-permute-done.2.refs_11_ = s32[8]{0:T(128)S(1)} collective-permute-done((s32[8]{0:T(128)}, s32[8]{0:T(128)S(1)}, u32[]{:S(2)}, u32[]{:S(2)}) %collective-permute-start.2) | collective-permute-done | bytes 64 | tf_op jit(solution)/shard_map/ppermute | solution.py:19
  11.8 1.5 collective-permute-start.3
  13.3 13.6 %shard_map.87.refs_4_ = bf16[2,3,384,1024]{3,2,1,0:T(8,128)(2,1)} custom-call(s32[1]{0:T(128)} %bitcast.1.me_ref, s32[8]{0:T(128)} %get-tuple-element.82.order_ref.refs_0_, f32[3,2,1024]{2,1,0:T(2,128)} %bitcast.26, f32[3,8,1024]{2,1,0:T(8,128)} %bitcast.24, bf16[2,1024,384]{2,1,0:T(8,128)(2,1)} %basis_ref.5), custom_call_target="tpu_custom_call" | custom-call | flops 4831838208 | bytes 4718592 | tf_op jit(solution)/shard_map/pallas_call | solution.py:213
  26.9 0.1 collective-permute-start.5
  27.0 0.0 collective-permute-done.3.refs_7_
  27.0 0.5 collective-permute-start.6
  27.5 1.5 collective-permute-done.5.refs_6_
  29.0 0.8 collective-permute-done.6.refs_8_
  29.8 0.0 copy-done.6
  29.9 0.8 copy-done.7
  30.6 7.0 %shard_map.88 = (bf16[8,2,3,48,384]{4,3,2,1,0:T(8,128)(2,1)}, s32[32]{0:T(128)}) custom-call(s32[8]{0:T(128)} %get-tuple-element.82.order_ref.refs_0_, s32[8]{0:T(128)} %refs_1_.3, s32[8]{0:T(128)} %get-tuple-element.83.refs_2_, s32[2]{0:T(128)} %refs_3_.3, bf16[2,3,384,1024]{3,2,1,0:T(8,128)(2,1)} %shard_map.87.refs_4_, ...), custom_call_target="tpu_custom_call" | custom-call | flops 1811939328 | bytes 6488064 | tf_op jit(solution)/shard_map/pallas_call | solution.py:332
  37.6 3.7 %all-to-all-start.2 = ((bf16[8,2,3,48,384]{4,3,2,1,0:T(8,128)(2,1)}), bf16[8,2,3,48,384]{4,3,2,1,0:T(8,128)(2,1)S(1)}, u32[]{:S(2)}, u32[]{:S(2)}) async-start(bf16[8,2,3,48,384]{4,3,2,1,0:T(8,128)(2,1)} %get-tuple-element.93.tile_ref), calls=%async_computation.2 | async-start | bytes 3538944 | tf_op jit(solution)/shard_map/all_to_all | solution.py:518
  41.3 0.6 collective-permute-start.4
  41.9 0.0 collective-permute-start.7
  41.9 19.8 %shard_map.89.refs_4_ = bf16[2,5,384,1024]{3,2,1,0:T(8,128)(2,1)} custom-call(s32[1]{0:T(128)} %bitcast.1.me_ref, s32[8]{0:T(128)} %get-tuple-element.82.order_ref.refs_0_, f32[3,2,1024]{2,1,0:T(2,128)} %bitcast.27, f32[3,8,1024]{2,1,0:T(8,128)} %bitcast.25, bf16[2,1024,384]{2,1,0:T(8,128)(2,1)} %basis_ref.5), custom_call_target="tpu_custom_call" | custom-call | flops 8053063680 | bytes 7864320 | tf_op jit(solution)/shard_map/pallas_call | solution.py:213
  61.7 3.6 %collective-permute-done.4.refs_7_ = bf16[5,256,384]{2,1,0:T(8,128)(2,1)} collective-permute-done((bf16[5,256,384]{2,1,0:T(8,128)(2,1)S(1)}, bf16[5,256,384]{2,1,0:T(8,128)(2,1)}, u32[]{:S(2)}, u32[]{:S(2)}) %collective-permute-start.4) | collective-permute-done | bytes 983072 | tf_op jit(solution)/shard_map/ppermute | solution.py:19
  65.3 0.0 collective-permute-start.8
  65.3 0.0 collective-permute-done.7.refs_6_
  65.3 2.9 %collective-permute-done.8.refs_8_ = bf16[5,256,384]{2,1,0:T(8,128)(2,1)} collective-permute-done((bf16[5,256,384]{2,1,0:T(8,128)(2,1)}, bf16[5,256,384]{2,1,0:T(8,128)(2,1)}, u32[]{:S(2)}, u32[]{:S(2)}) %collective-permute-start.8) | collective-permute-done | bytes 983072 | tf_op jit(solution)/shard_map/ppermute | solution.py:19
  68.2 10.7 %shard_map.90 = (bf16[8,2,5,48,384]{4,3,2,1,0:T(8,128)(2,1)}, bf16[8,2,48,1408]{3,2,1,0:T(8,128)(2,1)}, bf16[8,2,48,512]{3,2,1,0:T(8,128)(2,1)S(1)}) custom-call(s32[8]{0:T(128)} %get-tuple-element.82.order_ref.refs_0_, s32[8]{0:T(128)} %refs_1_.3, s32[8]{0:T(128)} %get-tuple-element.83.refs_2_, s32[2]{0:T(128)} %refs_3_.3, ...), custom_call_target="tpu_custom_call" | custom-call | flops 3019898880 | bytes 10813440 | tf_op jit(solution)/shard_map/pallas_call | solution.py:332
  78.9 4.1 %all-to-all-done.2 = bf16[8,2,3,48,384]{4,3,2,1,0:T(8,128)(2,1)S(1)} async-done(((bf16[8,2,3,48,384]{4,3,2,1,0:T(8,128)(2,1)}), bf16[8,2,3,48,384]{4,3,2,1,0:T(8,128)(2,1)S(1)}, u32[]{:S(2)}, u32[]{:S(2)}) %all-to-all-start.2) | async-done | bytes 1769504 | tf_op jit(solution)/shard_map/all_to_all | solution.py:518
  83.1 1.2 copy-done
  84.3 3.8 %all-to-all-start.3 = ((bf16[8,2,48,1408]{3,2,1,0:T(8,128)(2,1)}), bf16[8,2,48,1408]{3,2,1,0:T(8,128)(2,1)S(1)}, u32[]{:S(2)}, u32[]{:S(2)}) async-start(bf16[8,2,48,1408]{3,2,1,0:T(8,128)(2,1)} %get-tuple-element.97), calls=%async_computation.3 | async-start | bytes 4325376 | tf_op jit(solution)/shard_map/all_to_all | solution.py:525
  88.1 5.7 %shard_map.92.refs_0_ = f32[768,512]{1,0:T(8,128)} custom-call(s32[8]{0:T(128)} %get-tuple-element.82.order_ref.refs_0_, bf16[8,2,3,48,384]{4,3,2,1,0:T(8,128)(2,1)} %get-tuple-element.93.tile_ref, bf16[8,384,512]{2,1,0:T(8,128)(2,1)} %coeff_ref.3), custom_call_target="tpu_custom_call" | custom-call | flops 905969664 | bytes 1769472 | tf_op jit(solution)/shard_map/pallas_call | solution.py:391
  93.8 8.1 %shard_map.93 = bf16[8,2,48,512]{3,2,1,0:T(8,128)(2,1)} custom-call(s32[8]{0:T(128)} %get-tuple-element.82.order_ref.refs_0_, bf16[8,2,5,48,384]{4,3,2,1,0:T(8,128)(2,1)} %get-tuple-element.106.tile_ref, bf16[8,384,512]{2,1,0:T(8,128)(2,1)} %coeff_ref.3, f32[768,512]{1,0:T(8,128)} %shard_map.92.refs_0_), custom_call_target="tpu_custom_call" | custom-call | flops 1509949440 | bytes 2949120 | tf_op jit(solution)/shard_map/pallas_call | solution.py:391
  101.8 1.0 dynamic-slice_bitcast_fusion
  102.9 1.9 %collective-permute-start.10 = (bf16[4,2,48,512]{3,2,1,0:T(8,128)(2,1)S(1)}, bf16[4,2,48,512]{3,2,1,0:T(8,128)(2,1)}, u32[]{:S(2)}, u32[]{:S(2)}) collective-permute-start(bf16[4,2,48,512]{3,2,1,0:T(8,128)(2,1)S(1)} %dynamic-slice_bitcast_fusion), channel_id=1, source_target_pairs={{0,1},{1,0},{2,3},{3,2},{4,5},{5,4},{6,7},{7,6},{8,9},{9,8},{10,11... | collective-permute-start | bytes 1179656 | tf_op jit(solution)/shard_map/ppermute | solution.py:19
  104.8 19.0 %collective-permute-done.10 = bf16[4,2,48,512]{3,2,1,0:T(8,128)(2,1)} collective-permute-done((bf16[4,2,48,512]{3,2,1,0:T(8,128)(2,1)S(1)}, bf16[4,2,48,512]{3,2,1,0:T(8,128)(2,1)}, u32[]{:S(2)}, u32[]{:S(2)}) %collective-permute-start.10) | collective-permute-done | bytes 393248 | tf_op jit(solution)/shard_map/ppermute | solution.py:19
  123.8 1.2 fusion
  125.0 0.7 dynamic-slice_bitcast_fusion.3
  125.8 0.0 collective-permute-start.11
  125.8 7.4 %collective-permute-start.12 = (bf16[2,48,512]{2,1,0:T(8,128)(2,1)}, bf16[2,48,512]{2,1,0:T(8,128)(2,1)S(1)}, u32[]{:S(2)}, u32[]{:S(2)}) collective-permute-start(bf16[2,48,512]{2,1,0:T(8,128)(2,1)} %get-tuple-element.109), channel_id=1, source_target_pairs={{0,4},{1,5},{2,6},{3,7},{4,0},{5,1},{6,2},{7,3},{8,12},{9,13},{10,... | collective-permute-start | bytes 294920 | tf_op jit(solution)/shard_map/ppermute | solution.py:19
  133.2 0.0 collective-permute-start.13
  133.2 3.5 %collective-permute-done.9.refs_1_ = s32[32]{0:T(128)} collective-permute-done((s32[32]{0:T(128)S(1)}, s32[32]{0:T(128)}, u32[]{:S(2)}, u32[]{:S(2)}) %collective-permute-start.9) | collective-permute-done | bytes 160 | tf_op jit(solution)/shard_map/ppermute | solution.py:19
  136.7 2.8 %shard_map.91 = (s32[64]{0:T(128)S(1)}, s32[64]{0:T(128)S(1)}, s32[64]{0:T(128)S(1)}, s32[1]{0:T(128)}) custom-call(s32[1]{0:T(128)} %bitcast.me_ref, s32[32]{0:T(128)} %get-tuple-element.100.refs_0_, s32[32]{0:T(128)} %collective-permute-done.9.refs_1_), custom_call_target="tpu_custom_call" | custom-call | tf_op jit(solution)/shard_map/pallas_call | solution.py:131
  140.1 0.0 collective-permute-done.11
  140.1 5.1 %collective-permute-done.12 = bf16[2,48,512]{2,1,0:T(8,128)(2,1)S(1)} collective-permute-done((bf16[2,48,512]{2,1,0:T(8,128)(2,1)}, bf16[2,48,512]{2,1,0:T(8,128)(2,1)S(1)}, u32[]{:S(2)}, u32[]{:S(2)}) %collective-permute-start.12) | collective-permute-done | bytes 98336 | tf_op jit(solution)/shard_map/ppermute | solution.py:19
  145.2 0.0 collective-permute-done.13
  145.2 1.6 %fusion.3 = bf16[2,48,512]{2,1,0:T(8,128)(2,1)} fusion(bf16[2,48,512]{2,1,0:T(8,128)(2,1)} %collective-permute-done.13, bf16[2,48,512]{2,1,0:T(8,128)(2,1)S(1)} %collective-permute-done.12, bf16[2,48,512]{2,1,0:T(8,128)(2,1)S(1)} %collective-permute-done.11, bf16[4,2,48,512]{3,2,1,0:T(8,128)(2,1)S(1)} %fusion, s32[]{:T(128)S(6)} %select_n.36), kind=kLoop, calls=%fused_computation.8 | loop fusion | flops 393216 | bytes 491524 | tf_op jit(solution)/shard_map/convert_element_type | solution.py:46
  146.8 0.0 all-to-all-done.3
  146.8 7.6 %conditional.1 = (bf16[2,48,64,384]{3,2,1,0:T(8,128)(2,1)}) conditional(s32[]{:T(128)} %bitcast.4, (s32[64]{0:T(128)S(1)}, s32[64]{0:T(128)S(1)}, s32[64]{0:T(128)S(1)}, bf16[8,2,3,48,384]{4,3,2,1,0:T(8,128)(2,1)}, bf16[8,2,48,1408]{3,2,1,0:T(8,128)(2,1)S(1)}) %tuple.39, (bf16[8,2,48,512]{3,2,1,0:T(8,128)(2,1)S(1)}, ...), branch_computations={%region_0.1_spmd, %region_1.2_spmd, %region_2.3_spmd} | conditional | flops 5898240 | bytes 14549028 | solution.py:544
  146.8 7.6 %branch_0_fun.1 = bf16[2,48,64,384]{3,2,1,0:T(8,128)(2,1)} custom-call(s32[64]{0:T(128)S(1)} %get-tuple-element.26.order_ref, s32[64]{0:T(128)S(1)} %get-tuple-element.27.counts_ref, s32[64]{0:T(128)S(1)} %get-tuple-element.40.offsets_ref, bf16[8,2,3,48,384]{4,3,2,1,0:T(8,128)(2,1)} %get-tuple-element.41.whole_ref, ...), custom_call_target="tpu_custom_call" | custom-call | tf_op jit(solution)/shard_map/cond/branch_0_fun/pallas_call | solution.py:459
  (18 shorter events, 0.0 us)
Async XLA Ops:
  0.6 8.6 %collective-permute-start = (s32[8]{0:T(128)}, s32[8]{0:T(128)S(1)}, u32[]{:S(2)}, u32[]{:S(2)}) collective-permute-start(s32[8]{0:T(128)} %refs_1_.3), channel_id=1, source_target_pairs={{0,2},{1,3},{2,0},{3,1},{4,6},{5,7},{6,4},{7,5},{8,10},{9,11},{10,... | collective-permute-start | bytes 104 | tf_op jit(solution)/shard_map/ppermute | solution.py:19
  3.7 5.5 %collective-permute-start.1 = (s32[8]{0:T(128)}, s32[8]{0:T(128)S(1)}, u32[]{:S(2)}, u32[]{:S(2)}) collective-permute-start(s32[8]{0:T(128)} %refs_1_.3), channel_id=1, source_target_pairs={{0,4},{1,5},{2,6},{3,7},{4,0},{5,1},{6,2},{7,3},{8,12},{9,13},{10,... | collective-permute-start | bytes 104 | tf_op jit(solution)/shard_map/ppermute | solution.py:19
  6.3 5.5 %collective-permute-start.2 = (s32[8]{0:T(128)}, s32[8]{0:T(128)S(1)}, u32[]{:S(2)}, u32[]{:S(2)}) collective-permute-start(s32[8]{0:T(128)} %refs_1_.3), channel_id=1, source_target_pairs={{0,6},{1,7},{2,4},{3,5},{4,2},{5,3},{6,0},{7,1},{8,14},{9,15},{10,... | collective-permute-start | bytes 104 | tf_op jit(solution)/shard_map/ppermute | solution.py:19
  9.2 17.7 %copy-start.8 = (s32[8]{0:T(128)}, s32[8]{0:T(128)S(1)}, u32[]{:S(2)}) copy-start(s32[8]{0:T(128)S(1)} %collective-permute-done.refs_9_) | copy-start | bytes 100
  9.2 17.7 %copy-start.9 = (s32[8]{0:T(128)}, s32[8]{0:T(128)S(1)}, u32[]{:S(2)}) copy-start(s32[8]{0:T(128)S(1)} %collective-permute-done.1.refs_10_) | copy-start | bytes 100
  11.8 15.1 %copy-start.10 = (s32[8]{0:T(128)}, s32[8]{0:T(128)S(1)}, u32[]{:S(2)}) copy-start(s32[8]{0:T(128)S(1)} %collective-permute-done.2.refs_11_) | copy-start | bytes 100
  11.8 15.2 %collective-permute-start.3 = (bf16[3,256,384]{2,1,0:T(8,128)(2,1)}, bf16[3,256,384]{2,1,0:T(8,128)(2,1)S(1)}, u32[]{:S(2)}, u32[]{:S(2)}) collective-permute-start(bf16[3,256,384]{2,1,0:T(8,128)(2,1)} %get-tuple-element.86.refs_5_), channel_id=1, source_target_pairs={{0,16},{8,24},{16,0},{24,8},{1,17},{9,25},{17,1},{25,9},{2,18},{10... | collective-permute-start | bytes 1769480 | tf_op jit(solution)/shard_map/ppermute | solution.py:19
  13.3 13.6 %copy-start.4 = (bf16[3,256,384]{2,1,0:T(8,128)(2,1)S(1)}, bf16[3,256,384]{2,1,0:T(8,128)(2,1)}, u32[]{:S(2)}) copy-start(bf16[3,256,384]{2,1,0:T(8,128)(2,1)} %get-tuple-element.86.refs_5_) | copy-start | bytes 1769476
  26.9 2.1 %collective-permute-start.5 = (bf16[3,256,384]{2,1,0:T(8,128)(2,1)S(1)}, bf16[3,256,384]{2,1,0:T(8,128)(2,1)S(1)}, u32[]{:S(2)}, u32[]{:S(2)}) collective-permute-start(bf16[3,256,384]{2,1,0:T(8,128)(2,1)S(1)} %copy-done.4), channel_id=1, source_target_pairs={{0,8},{8,0},{16,24},{24,16},{1,9},{9,1},{17,25},{25,17},{2,10},{10... | collective-permute-start | bytes 1769480 | tf_op jit(solution)/shard_map/ppermute | solution.py:19
  27.0 2.8 %copy-start.5 = (bf16[3,256,384]{2,1,0:T(8,128)(2,1)}, bf16[3,256,384]{2,1,0:T(8,128)(2,1)S(1)}, u32[]{:S(2)}) copy-start(bf16[3,256,384]{2,1,0:T(8,128)(2,1)S(1)} %collective-permute-done.3.refs_7_) | copy-start | bytes 1769476
  27.0 2.8 %collective-permute-start.6 = (bf16[3,256,384]{2,1,0:T(8,128)(2,1)S(1)}, bf16[3,256,384]{2,1,0:T(8,128)(2,1)S(1)}, u32[]{:S(2)}, u32[]{:S(2)}) collective-permute-start(bf16[3,256,384]{2,1,0:T(8,128)(2,1)S(1)} %collective-permute-done.3.refs_7_), channel_id=1, source_target_pairs={{0,8},{8,0},{16,24},{24,16},{1,9},{9,1},{17,25},{25,17},{2,10},{10... | collective-permute-start | bytes 1769480 | tf_op jit(solution)/shard_map/ppermute | solution.py:19
  29.0 0.9 copy-start.6
  29.8 0.8 copy-start.7
  37.6 3.7 %copy-start.3 = (bf16[5,256,384]{2,1,0:T(8,128)(2,1)S(1)}, bf16[5,256,384]{2,1,0:T(8,128)(2,1)}, u32[]{:S(2)}) copy-start(bf16[5,256,384]{2,1,0:T(8,128)(2,1)} %get-tuple-element.87.refs_5_) | copy-start | bytes 2949124
  37.6 45.4 %all-to-all-start.2 = ((bf16[8,2,3,48,384]{4,3,2,1,0:T(8,128)(2,1)}), bf16[8,2,3,48,384]{4,3,2,1,0:T(8,128)(2,1)S(1)}, u32[]{:S(2)}, u32[]{:S(2)}) async-start(bf16[8,2,3,48,384]{4,3,2,1,0:T(8,128)(2,1)} %get-tuple-element.93.tile_ref), calls=%async_computation.2 | async-start | bytes 3538944 | tf_op jit(solution)/shard_map/all_to_all | solution.py:518
  41.3 24.0 %collective-permute-start.4 = (bf16[5,256,384]{2,1,0:T(8,128)(2,1)S(1)}, bf16[5,256,384]{2,1,0:T(8,128)(2,1)}, u32[]{:S(2)}, u32[]{:S(2)}) collective-permute-start(bf16[5,256,384]{2,1,0:T(8,128)(2,1)S(1)} %copy-done.3), channel_id=1, source_target_pairs={{0,16},{8,24},{16,0},{24,8},{1,17},{9,25},{17,1},{25,9},{2,18},{10... | collective-permute-start | bytes 2949128 | tf_op jit(solution)/shard_map/ppermute | solution.py:19
  41.9 23.4 %collective-permute-start.7 = (bf16[5,256,384]{2,1,0:T(8,128)(2,1)S(1)}, bf16[5,256,384]{2,1,0:T(8,128)(2,1)}, u32[]{:S(2)}, u32[]{:S(2)}) collective-permute-start(bf16[5,256,384]{2,1,0:T(8,128)(2,1)S(1)} %copy-done.3), channel_id=1, source_target_pairs={{0,8},{8,0},{16,24},{24,16},{1,9},{9,1},{17,25},{25,17},{2,10},{10... | collective-permute-start | bytes 2949128 | tf_op jit(solution)/shard_map/ppermute | solution.py:19
  65.3 2.9 %collective-permute-start.8 = (bf16[5,256,384]{2,1,0:T(8,128)(2,1)}, bf16[5,256,384]{2,1,0:T(8,128)(2,1)}, u32[]{:S(2)}, u32[]{:S(2)}) collective-permute-start(bf16[5,256,384]{2,1,0:T(8,128)(2,1)} %collective-permute-done.4.refs_7_), channel_id=1, source_target_pairs={{0,8},{8,0},{16,24},{24,16},{1,9},{9,1},{17,25},{25,17},{2,10},{10... | collective-permute-start | bytes 2949128 | tf_op jit(solution)/shard_map/ppermute | solution.py:19
  83.1 1.2 copy-start
  84.3 62.5 %all-to-all-start.3 = ((bf16[8,2,48,1408]{3,2,1,0:T(8,128)(2,1)}), bf16[8,2,48,1408]{3,2,1,0:T(8,128)(2,1)S(1)}, u32[]{:S(2)}, u32[]{:S(2)}) async-start(bf16[8,2,48,1408]{3,2,1,0:T(8,128)(2,1)} %get-tuple-element.97), calls=%async_computation.3 | async-start | bytes 4325376 | tf_op jit(solution)/shard_map/all_to_all | solution.py:525
  93.8 39.4 %copy-start.11 = (s32[32]{0:T(128)S(1)}, s32[32]{0:T(128)}, u32[]{:S(2)}) copy-start(s32[32]{0:T(128)} %get-tuple-element.100.refs_0_) | copy-start | bytes 388
  102.9 20.9 %collective-permute-start.10 = (bf16[4,2,48,512]{3,2,1,0:T(8,128)(2,1)S(1)}, bf16[4,2,48,512]{3,2,1,0:T(8,128)(2,1)}, u32[]{:S(2)}, u32[]{:S(2)}) collective-permute-start(bf16[4,2,48,512]{3,2,1,0:T(8,128)(2,1)S(1)} %dynamic-slice_bitcast_fusion), channel_id=1, source_target_pairs={{0,1},{1,0},{2,3},{3,2},{4,5},{5,4},{6,7},{7,6},{8,9},{9,8},{10,11... | collective-permute-start | bytes 1179656 | tf_op jit(solution)/shard_map/ppermute | solution.py:19
  125.8 14.4 %collective-permute-start.11 = (bf16[2,48,512]{2,1,0:T(8,128)(2,1)}, bf16[2,48,512]{2,1,0:T(8,128)(2,1)S(1)}, u32[]{:S(2)}, u32[]{:S(2)}) collective-permute-start(bf16[2,48,512]{2,1,0:T(8,128)(2,1)} %get-tuple-element.107), channel_id=1, source_target_pairs={{0,2},{1,3},{2,0},{3,1},{4,6},{5,7},{6,4},{7,5},{8,10},{9,11},{10,... | collective-permute-start | bytes 294920 | tf_op jit(solution)/shard_map/ppermute | solution.py:19
  125.8 19.5 %collective-permute-start.12 = (bf16[2,48,512]{2,1,0:T(8,128)(2,1)}, bf16[2,48,512]{2,1,0:T(8,128)(2,1)S(1)}, u32[]{:S(2)}, u32[]{:S(2)}) collective-permute-start(bf16[2,48,512]{2,1,0:T(8,128)(2,1)} %get-tuple-element.109), channel_id=1, source_target_pairs={{0,4},{1,5},{2,6},{3,7},{4,0},{5,1},{6,2},{7,3},{8,12},{9,13},{10,... | collective-permute-start | bytes 294920 | tf_op jit(solution)/shard_map/ppermute | solution.py:19
  133.2 12.0 %collective-permute-start.13 = (bf16[2,48,512]{2,1,0:T(8,128)(2,1)}, bf16[2,48,512]{2,1,0:T(8,128)(2,1)}, u32[]{:S(2)}, u32[]{:S(2)}) collective-permute-start(bf16[2,48,512]{2,1,0:T(8,128)(2,1)} %get-tuple-element.108), channel_id=1, source_target_pairs={{0,6},{1,7},{2,4},{3,5},{4,2},{5,3},{6,0},{7,1},{8,14},{9,15},{10,... | collective-permute-start | bytes 294920 | tf_op jit(solution)/shard_map/ppermute | solution.py:19
  133.2 3.5 %collective-permute-start.9 = (s32[32]{0:T(128)S(1)}, s32[32]{0:T(128)}, u32[]{:S(2)}, u32[]{:S(2)}) collective-permute-start(s32[32]{0:T(128)S(1)} %copy-done.11), channel_id=1, source_target_pairs={{0,1},{1,0},{2,3},{3,2},{4,5},{5,4},{6,7},{7,6},{8,9},{9,8},{10,11... | collective-permute-start | bytes 392 | tf_op jit(solution)/shard_map/ppermute | solution.py:19

commit v6 on v5

--- a/solution.py
+++ b/solution.py
@@ -242,10 +242,10 @@
     order_ref, source_counts_ref, offsets_ref, test_counts_ref, left_ref = refs[:5]
     shard_refs = refs[5 : 5 + nshard]
     j = pl.program_id(0)
-    if packed:
-        tile_ref, main_ref, over_ref, pack_ref = refs[5 + nshard :]
+    if not packed:
+        (tile_ref,) = refs[5 + nshard :]
     else:
-        *far_refs, tile_ref, joined_ref = refs[5 + nshard :]
+        *far_refs, tile_ref, main_ref, over_ref, joined_ref, pack_ref = refs[5 + nshard :]
 
         @pl.when(j == 0)
         def _():
@@ -326,7 +326,6 @@
             shapes.append(jax.ShapeDtypeStruct(shape, jnp.bfloat16))
             specs.append(pl.BlockSpec(shape, lambda j, *_: (0, 0, 0, 0)))
         scratch.append(pltpu.VMEM((ndest, ntest, rows, nsource * width + LANES), jnp.bfloat16))
-    else:
         shapes.append(jax.ShapeDtypeStruct(((1 + len(far)) * tables[1].shape[0],), jnp.int32))
         specs.append(pl.BlockSpec(memory_space=pltpu.SMEM))
     return pl.pallas_call(
@@ -506,22 +505,24 @@
 
     order, offsets, basis_a, basis_b = pick(cut, source_counts, source_basis)
     tables = (order, source_counts, offsets)
-    inner = max(1, nsrc // 4)
-    far = [exchange(source_counts, "src", flip) for flip in range(inner, nsrc, inner)]
-    basis_a, *far = lax.optimization_barrier((basis_a, *far))
     me = jnp.reshape(me_test, (1,))
     test_points, source_points = test_points.transpose(1, 0, 2), source_points.transpose(1, 0, 2)
 
     left_a = left_products(ntest_axis, me, order, test_points, source_points, test_basis, 0, cut)
     shards_a, left_a = gather("a", basis_a, left_a)
-    tiles_a, joined = tiles(nsrc, 0, tables, test_counts, left_a, shards_a, None, far)
+    (tiles_a,) = tiles(nsrc, 0, tables, test_counts, left_a, shards_a, None)
     moved_a = lax.all_to_all(tiles_a, "src", split_axis=0, concat_axis=0, tiled=True)
 
     rest, _ = lax.optimization_barrier((basis_b, held["a"]))
     later, _ = lax.optimization_barrier((source_points, tiles_a))
     left_b = left_products(ntest_axis, me, order, test_points, later, test_basis, cut, nsource)
     shards_b, left_b = gather("b", rest, left_b)
-    tiles_b, packed, beyond = tiles(nsrc, cut, tables, test_counts, left_b, shards_b, main)
+    inner = max(1, nsrc // 4)
+    counts, _ = lax.optimization_barrier((source_counts, left_b))
+    far = [exchange(counts, "src", flip) for flip in range(inner, nsrc, inner)]
+    tiles_b, packed, beyond, joined = tiles(
+        nsrc, cut, tables, test_counts, left_b, shards_b, main, far
+    )
     moved_b = lax.all_to_all(packed, "src", split_axis=0, concat_axis=0, tiled=True)
 
     joined, _ = lax.optimization_barrier((joined, packed))

time: 155 us -> 161 us (1.039)
  starting transfers between devices: 25.2 us -> 29.8 us
  waiting for transfers between devices: 43.2 us -> 45.2 us
    ppermute x14, waiting for transfers between devices: 39 us -> 45.2 us  [exchange(): return lax.ppermute(x, axis, [(a, a ^ flip) for a in range(size)])]
    all_to_all x1, waiting for transfers between devices: 4.12 us -> 0.01 us  [body(): lax.all_to_all(tiles_a, 'src', split_axis=0, concat_axis=0, tiled=True)]
    all_to_all x1, starting transfers between devices: 3.72 us -> 6.48 us  [body(): lax.all_to_all(tiles_a, 'src', split_axis=0, concat_axis=0, tiled=True)]
  transfers between devices with their start and end apart: 16 -> 16, of which waited for: 9 -> 8; matrix products, arithmetic and copies ran while one was open for 3% -> 3% of each run, Pallas kernels for 41% -> 37%
where the time goes in v6:
time: 161 us
  Pallas kernels  77.1 us (48%)
  waiting for transfers between devices  45.2 us (28%)
  starting transfers between devices  29.8 us (19%)
  local copies, waits for them, and re-layouts  4.33 us (3%)
  other arithmetic  2.8 us (2%)
    ppermute x14, waiting for transfers between devices, exchange(): return lax.ppermute(x, axis, [(a, a ^ flip) for a in range(size)])  45.2 us
    pallas_call x2, Pallas kernels, left_products(): pl.pallas_call(functools.partial(left_kernel, nshard, first), grid_spec=p...  33.2 us
    ppermute x14, starting transfers between devices, exchange(): return lax.ppermute(x, axis, [(a, a ^ flip) for a in range(size)])  18.9 us
    pallas_call x2, Pallas kernels, tiles(): pl.pallas_call(functools.partial(tile_kernel, nshard, first, packed), gri...  16.9 us
    pallas_call x2, Pallas kernels, project(): pl.pallas_call(project_kernel, grid_spec=pltpu.PrefetchScalarGridSpec(num...  13.7 us
    pallas_call x1, Pallas kernels, unpack(): pl.pallas_call(functools.partial(unpack_kernel, cut), grid_spec=pltpu.Pre...  7.58 us
    all_to_all x1, starting transfers between devices, body(): lax.all_to_all(tiles_a, 'src', split_axis=0, concat_axis=0, tiled=True)  6.48 us
    all_to_all x1, starting transfers between devices, body(): lax.all_to_all(packed, 'src', split_axis=0, concat_axis=0, tiled=True)  4.38 us
  transfers between devices with their start and end apart: 16, of which 8 were waited for; matrix products, arithmetic and copies ran while one was open for 3% of the time, Pallas kernels for 37%

profile of v6, /device:TPU:0, one launch (start us, length us, event | category | flops | bytes accessed | tf_op | source)
XLA Modules:
  0.0 160.6 jit_solution(5252013052081808414)
XLA Ops:
  0.6 2.9 %shard_map.86 = (s32[8]{0:T(128)}, s32[8]{0:T(128)}, bf16[3,256,384]{2,1,0:T(8,128)(2,1)}, bf16[5,256,384]{2,1,0:T(8,128)(2,1)}) custom-call(s32[8]{0:T(128)} %refs_1_.3, bf16[8,256,384]{2,1,0:T(8,128)(2,1)} %basis_ref.3), custom_call_target="tpu_custom_call" | custom-call | tf_op jit(solution)/shard_map/pallas_call | solution.py:85
  3.5 3.0 %collective-permute-start = (bf16[3,256,384]{2,1,0:T(8,128)(2,1)}, bf16[3,256,384]{2,1,0:T(8,128)(2,1)S(1)}, u32[]{:S(2)}, u32[]{:S(2)}) collective-permute-start(bf16[3,256,384]{2,1,0:T(8,128)(2,1)} %get-tuple-element.81.refs_5_), channel_id=1, source_target_pairs={{0,16},{8,24},{16,0},{24,8},{1,17},{9,25},{17,1},{25,9},{2,18},{10... | collective-permute-start | bytes 1769480 | tf_op jit(solution)/shard_map/ppermute | solution.py:19
  6.5 0.0 collective-permute-start.2
  6.5 13.5 %shard_map.87.refs_4_ = bf16[2,3,384,1024]{3,2,1,0:T(8,128)(2,1)} custom-call(s32[1]{0:T(128)} %bitcast.1.me_ref, s32[8]{0:T(128)} %get-tuple-element.78.order_ref.refs_0_, f32[3,2,1024]{2,1,0:T(2,128)} %bitcast.26, f32[3,8,1024]{2,1,0:T(8,128)} %bitcast.24, bf16[2,1024,384]{2,1,0:T(8,128)(2,1)} %basis_ref.5), custom_call_target="tpu_custom_call" | custom-call | flops 4831838208 | bytes 4718592 | tf_op jit(solution)/shard_map/pallas_call | solution.py:213
  20.0 0.1 collective-permute-done.refs_7_
  20.1 0.4 collective-permute-start.3
  20.5 0.0 collective-permute-done.2.refs_6_
  20.5 1.6 %collective-permute-done.3.refs_8_ = bf16[3,256,384]{2,1,0:T(8,128)(2,1)S(1)} collective-permute-done((bf16[3,256,384]{2,1,0:T(8,128)(2,1)S(1)}, bf16[3,256,384]{2,1,0:T(8,128)(2,1)S(1)}, u32[]{:S(2)}, u32[]{:S(2)}) %collective-permute-start.3) | collective-permute-done | bytes 589856 | tf_op jit(solution)/shard_map/ppermute | solution.py:19
  22.2 0.8 copy-done.6
  23.0 6.5 %shard_map.88.tile_ref = bf16[8,2,3,48,384]{4,3,2,1,0:T(8,128)(2,1)} custom-call(s32[8]{0:T(128)} %get-tuple-element.78.order_ref.refs_0_, s32[8]{0:T(128)} %refs_1_.3, s32[8]{0:T(128)} %get-tuple-element.79.refs_2_, s32[2]{0:T(128)} %refs_3_.3, bf16[2,3,384,1024]{3,2,1,0:T(8,128)(2,1)} %shard_map.87.refs_4_, ...), custom_call_target="tpu_custom_call" | custom-call | flops 1811939328 | bytes 6488064 | tf_op jit(solution)/shard_map/pallas_call | solution.py:331
  29.5 6.5 %all-to-all-start.2 = ((bf16[8,2,3,48,384]{4,3,2,1,0:T(8,128)(2,1)}), bf16[8,2,3,48,384]{4,3,2,1,0:T(8,128)(2,1)S(1)}, u32[]{:S(2)}, u32[]{:S(2)}) async-start(bf16[8,2,3,48,384]{4,3,2,1,0:T(8,128)(2,1)} %shard_map.88.tile_ref), calls=%async_computation.2 | async-start | bytes 3538944 | tf_op jit(solution)/shard_map/all_to_all | solution.py:514
  36.0 0.0 copy-start.7
  36.0 1.6 collective-permute-start.1
  37.6 0.0 collective-permute-start.4
  37.6 19.7 %shard_map.89.refs_4_ = bf16[2,5,384,1024]{3,2,1,0:T(8,128)(2,1)} custom-call(s32[1]{0:T(128)} %bitcast.1.me_ref, s32[8]{0:T(128)} %get-tuple-element.78.order_ref.refs_0_, f32[3,2,1024]{2,1,0:T(2,128)} %bitcast.27, f32[3,8,1024]{2,1,0:T(8,128)} %bitcast.25, bf16[2,1024,384]{2,1,0:T(8,128)(2,1)} %basis_ref.5), custom_call_target="tpu_custom_call" | custom-call | flops 8053063680 | bytes 7864320 | tf_op jit(solution)/shard_map/pallas_call | solution.py:213
  57.3 2.5 %collective-permute-done.1.refs_7_ = bf16[5,256,384]{2,1,0:T(8,128)(2,1)} collective-permute-done((bf16[5,256,384]{2,1,0:T(8,128)(2,1)S(1)}, bf16[5,256,384]{2,1,0:T(8,128)(2,1)}, u32[]{:S(2)}, u32[]{:S(2)}) %collective-permute-start.1) | collective-permute-done | bytes 983072 | tf_op jit(solution)/shard_map/ppermute | solution.py:19
  59.8 0.0 collective-permute-start.5
  59.8 1.7 %collective-permute-start.6 = (s32[8]{0:T(128)S(1)}, s32[8]{0:T(128)S(1)}, u32[]{:S(2)}, u32[]{:S(2)}) collective-permute-start(s32[8]{0:T(128)S(1)} %copy-done.7), channel_id=1, source_target_pairs={{0,2},{1,3},{2,0},{3,1},{4,6},{5,7},{6,4},{7,5},{8,10},{9,11},{10,... | collective-permute-start | bytes 104 | tf_op jit(solution)/shard_map/ppermute | solution.py:19
  61.5 2.4 %collective-permute-start.7 = (s32[8]{0:T(128)S(1)}, s32[8]{0:T(128)S(1)}, u32[]{:S(2)}, u32[]{:S(2)}) collective-permute-start(s32[8]{0:T(128)S(1)} %copy-done.7), channel_id=1, source_target_pairs={{0,4},{1,5},{2,6},{3,7},{4,0},{5,1},{6,2},{7,3},{8,12},{9,13},{10,... | collective-permute-start | bytes 104 | tf_op jit(solution)/shard_map/ppermute | solution.py:19
  63.8 0.3 collective-permute-start.8
  64.1 0.0 collective-permute-done.4.refs_6_
  64.2 2.2 %collective-permute-done.6.refs_9_ = s32[8]{0:T(128)S(1)} collective-permute-done((s32[8]{0:T(128)S(1)}, s32[8]{0:T(128)S(1)}, u32[]{:S(2)}, u32[]{:S(2)}) %collective-permute-start.6) | collective-permute-done | bytes 64 | tf_op jit(solution)/shard_map/ppermute | solution.py:19
  66.4 11.3 %collective-permute-done.7.refs_10_ = s32[8]{0:T(128)S(1)} collective-permute-done((s32[8]{0:T(128)S(1)}, s32[8]{0:T(128)S(1)}, u32[]{:S(2)}, u32[]{:S(2)}) %collective-permute-start.7) | collective-permute-done | bytes 64 | tf_op jit(solution)/shard_map/ppermute | solution.py:19
  77.7 0.0 collective-permute-done.8.refs_11_
  77.7 0.0 collective-permute-done.5.refs_8_
  77.7 0.5 copy-done.9
  78.2 10.4 %shard_map.90 = (bf16[8,2,5,48,384]{4,3,2,1,0:T(8,128)(2,1)}, bf16[8,2,48,1408]{3,2,1,0:T(8,128)(2,1)}, bf16[8,2,48,512]{3,2,1,0:T(8,128)(2,1)S(1)}, s32[32]{0:T(128)}) custom-call(s32[8]{0:T(128)} %get-tuple-element.78.order_ref.refs_0_, s32[8]{0:T(128)} %refs_1_.3, s32[8]{0:T(128)} %get-tuple-element.79.refs_2_, s32[2]{0:T(128)} %refs_3_.3, ...), custom_call_target="tpu_custom_call" | custom-call | flops 3019898880 | bytes 10813440 | tf_op jit(solution)/shard_map/pallas_call | solution.py:331
  88.6 0.0 all-to-all-done.2
  88.7 1.2 copy-done
  89.9 4.4 %all-to-all-start.3 = ((bf16[8,2,48,1408]{3,2,1,0:T(8,128)(2,1)}), bf16[8,2,48,1408]{3,2,1,0:T(8,128)(2,1)S(1)}, u32[]{:S(2)}, u32[]{:S(2)}) async-start(bf16[8,2,48,1408]{3,2,1,0:T(8,128)(2,1)} %get-tuple-element.89), calls=%async_computation.3 | async-start | bytes 4325376 | tf_op jit(solution)/shard_map/all_to_all | solution.py:526
  94.3 5.7 %shard_map.92.refs_0_ = f32[768,512]{1,0:T(8,128)} custom-call(s32[8]{0:T(128)} %get-tuple-element.78.order_ref.refs_0_, bf16[8,2,3,48,384]{4,3,2,1,0:T(8,128)(2,1)} %shard_map.88.tile_ref, bf16[8,384,512]{2,1,0:T(8,128)(2,1)} %coeff_ref.3), custom_call_target="tpu_custom_call" | custom-call | flops 905969664 | bytes 1769472 | tf_op jit(solution)/shard_map/pallas_call | solution.py:390
  99.9 8.1 %shard_map.93 = bf16[8,2,48,512]{3,2,1,0:T(8,128)(2,1)} custom-call(s32[8]{0:T(128)} %get-tuple-element.78.order_ref.refs_0_, bf16[8,2,5,48,384]{4,3,2,1,0:T(8,128)(2,1)} %get-tuple-element.98.tile_ref, bf16[8,384,512]{2,1,0:T(8,128)(2,1)} %coeff_ref.3, f32[768,512]{1,0:T(8,128)} %shard_map.92.refs_0_), custom_call_target="tpu_custom_call" | custom-call | flops 1509949440 | bytes 2949120 | tf_op jit(solution)/shard_map/pallas_call | solution.py:390
  108.0 1.0 dynamic-slice_bitcast_fusion
  109.0 2.1 %collective-permute-start.10 = (bf16[4,2,48,512]{3,2,1,0:T(8,128)(2,1)S(1)}, bf16[4,2,48,512]{3,2,1,0:T(8,128)(2,1)}, u32[]{:S(2)}, u32[]{:S(2)}) collective-permute-start(bf16[4,2,48,512]{3,2,1,0:T(8,128)(2,1)S(1)} %dynamic-slice_bitcast_fusion), channel_id=1, source_target_pairs={{0,1},{1,0},{2,3},{3,2},{4,5},{5,4},{6,7},{7,6},{8,9},{9,8},{10,11... | collective-permute-start | bytes 1179656 | tf_op jit(solution)/shard_map/ppermute | solution.py:19
  111.1 19.0 %collective-permute-done.10 = bf16[4,2,48,512]{3,2,1,0:T(8,128)(2,1)} collective-permute-done((bf16[4,2,48,512]{3,2,1,0:T(8,128)(2,1)S(1)}, bf16[4,2,48,512]{3,2,1,0:T(8,128)(2,1)}, u32[]{:S(2)}, u32[]{:S(2)}) %collective-permute-start.10) | collective-permute-done | bytes 393248 | tf_op jit(solution)/shard_map/ppermute | solution.py:19
  130.1 1.2 fusion
  131.4 0.7 dynamic-slice_bitcast_fusion.3
  132.1 0.0 collective-permute-start.11
  132.1 7.4 %collective-permute-start.12 = (bf16[2,48,512]{2,1,0:T(8,128)(2,1)}, bf16[2,48,512]{2,1,0:T(8,128)(2,1)S(1)}, u32[]{:S(2)}, u32[]{:S(2)}) collective-permute-start(bf16[2,48,512]{2,1,0:T(8,128)(2,1)} %get-tuple-element.101), channel_id=1, source_target_pairs={{0,4},{1,5},{2,6},{3,7},{4,0},{5,1},{6,2},{7,3},{8,12},{9,13},{10,... | collective-permute-start | bytes 294920 | tf_op jit(solution)/shard_map/ppermute | solution.py:19
  139.4 0.0 collective-permute-start.13
  139.4 3.6 %collective-permute-done.9.refs_1_ = s32[32]{0:T(128)} collective-permute-done((s32[32]{0:T(128)S(1)}, s32[32]{0:T(128)}, u32[]{:S(2)}, u32[]{:S(2)}) %collective-permute-start.9) | collective-permute-done | bytes 160 | tf_op jit(solution)/shard_map/ppermute | solution.py:19
  143.1 2.8 %shard_map.91 = (s32[64]{0:T(128)S(1)}, s32[64]{0:T(128)S(1)}, s32[64]{0:T(128)S(1)}, s32[1]{0:T(128)}) custom-call(s32[1]{0:T(128)} %bitcast.me_ref, s32[32]{0:T(128)} %get-tuple-element.92.refs_0_, s32[32]{0:T(128)} %collective-permute-done.9.refs_1_), custom_call_target="tpu_custom_call" | custom-call | tf_op jit(solution)/shard_map/pallas_call | solution.py:131
  146.6 0.0 collective-permute-done.11
  146.6 4.9 %collective-permute-done.12 = bf16[2,48,512]{2,1,0:T(8,128)(2,1)S(1)} collective-permute-done((bf16[2,48,512]{2,1,0:T(8,128)(2,1)}, bf16[2,48,512]{2,1,0:T(8,128)(2,1)S(1)}, u32[]{:S(2)}, u32[]{:S(2)}) %collective-permute-start.12) | collective-permute-done | bytes 98336 | tf_op jit(solution)/shard_map/ppermute | solution.py:19
  151.5 1.6 fusion.3
  153.0 0.0 all-to-all-done.3
  153.0 7.6 %conditional.1 = (bf16[2,48,64,384]{3,2,1,0:T(8,128)(2,1)}) conditional(s32[]{:T(128)} %bitcast.4, (s32[64]{0:T(128)S(1)}, s32[64]{0:T(128)S(1)}, s32[64]{0:T(128)S(1)}, bf16[8,2,3,48,384]{4,3,2,1,0:T(8,128)(2,1)}, bf16[8,2,48,1408]{3,2,1,0:T(8,128)(2,1)S(1)}) %tuple.39, (bf16[8,2,48,512]{3,2,1,0:T(8,128)(2,1)S(1)}, ...), branch_computations={%region_0.1_spmd, %region_1.2_spmd, %region_2.3_spmd} | conditional | flops 5898240 | bytes 14549028 | solution.py:545
  153.0 7.6 %branch_0_fun.1 = bf16[2,48,64,384]{3,2,1,0:T(8,128)(2,1)} custom-call(s32[64]{0:T(128)S(1)} %get-tuple-element.26.order_ref, s32[64]{0:T(128)S(1)} %get-tuple-element.27.counts_ref, s32[64]{0:T(128)S(1)} %get-tuple-element.40.offsets_ref, bf16[8,2,3,48,384]{4,3,2,1,0:T(8,128)(2,1)} %get-tuple-element.41.whole_ref, ...), custom_call_target="tpu_custom_call" | custom-call | tf_op jit(solution)/shard_map/cond/branch_0_fun/pallas_call | solution.py:458
  (18 shorter events, 0.0 us)
Async XLA Ops:
  3.5 16.6 %collective-permute-start = (bf16[3,256,384]{2,1,0:T(8,128)(2,1)}, bf16[3,256,384]{2,1,0:T(8,128)(2,1)S(1)}, u32[]{:S(2)}, u32[]{:S(2)}) collective-permute-start(bf16[3,256,384]{2,1,0:T(8,128)(2,1)} %get-tuple-element.81.refs_5_), channel_id=1, source_target_pairs={{0,16},{8,24},{16,0},{24,8},{1,17},{9,25},{17,1},{25,9},{2,18},{10... | collective-permute-start | bytes 1769480 | tf_op jit(solution)/shard_map/ppermute | solution.py:19
  6.5 14.0 %collective-permute-start.2 = (bf16[3,256,384]{2,1,0:T(8,128)(2,1)}, bf16[3,256,384]{2,1,0:T(8,128)(2,1)S(1)}, u32[]{:S(2)}, u32[]{:S(2)}) collective-permute-start(bf16[3,256,384]{2,1,0:T(8,128)(2,1)} %get-tuple-element.81.refs_5_), channel_id=1, source_target_pairs={{0,8},{8,0},{16,24},{24,16},{1,9},{9,1},{17,25},{25,17},{2,10},{10... | collective-permute-start | bytes 1769480 | tf_op jit(solution)/shard_map/ppermute | solution.py:19
  20.1 2.1 %copy-start.4 = (bf16[3,256,384]{2,1,0:T(8,128)(2,1)}, bf16[3,256,384]{2,1,0:T(8,128)(2,1)S(1)}, u32[]{:S(2)}) copy-start(bf16[3,256,384]{2,1,0:T(8,128)(2,1)S(1)} %collective-permute-done.refs_7_) | copy-start | bytes 1769476
  20.1 2.1 %collective-permute-start.3 = (bf16[3,256,384]{2,1,0:T(8,128)(2,1)S(1)}, bf16[3,256,384]{2,1,0:T(8,128)(2,1)S(1)}, u32[]{:S(2)}, u32[]{:S(2)}) collective-permute-start(bf16[3,256,384]{2,1,0:T(8,128)(2,1)S(1)} %collective-permute-done.refs_7_), channel_id=1, source_target_pairs={{0,8},{8,0},{16,24},{24,16},{1,9},{9,1},{17,25},{25,17},{2,10},{10... | collective-permute-start | bytes 1769480 | tf_op jit(solution)/shard_map/ppermute | solution.py:19
  20.5 1.6 %copy-start.5 = (bf16[3,256,384]{2,1,0:T(8,128)(2,1)}, bf16[3,256,384]{2,1,0:T(8,128)(2,1)S(1)}, u32[]{:S(2)}) copy-start(bf16[3,256,384]{2,1,0:T(8,128)(2,1)S(1)} %collective-permute-done.2.refs_6_) | copy-start | bytes 1769476
  22.2 0.8 copy-start.6
  29.5 6.5 %copy-start.3 = (bf16[5,256,384]{2,1,0:T(8,128)(2,1)S(1)}, bf16[5,256,384]{2,1,0:T(8,128)(2,1)}, u32[]{:S(2)}) copy-start(bf16[5,256,384]{2,1,0:T(8,128)(2,1)} %get-tuple-element.82.refs_5_) | copy-start | bytes 2949124
  29.5 59.2 %all-to-all-start.2 = ((bf16[8,2,3,48,384]{4,3,2,1,0:T(8,128)(2,1)}), bf16[8,2,3,48,384]{4,3,2,1,0:T(8,128)(2,1)S(1)}, u32[]{:S(2)}, u32[]{:S(2)}) async-start(bf16[8,2,3,48,384]{4,3,2,1,0:T(8,128)(2,1)} %shard_map.88.tile_ref), calls=%async_computation.2 | async-start | bytes 3538944 | tf_op jit(solution)/shard_map/all_to_all | solution.py:514
  36.0 23.8 %copy-start.7 = (s32[8]{0:T(128)S(1)}, s32[8]{0:T(128)}, u32[]{:S(2)}) copy-start(s32[8]{0:T(128)} %refs_1_.3) | copy-start | bytes 100
  36.0 23.8 %collective-permute-start.1 = (bf16[5,256,384]{2,1,0:T(8,128)(2,1)S(1)}, bf16[5,256,384]{2,1,0:T(8,128)(2,1)}, u32[]{:S(2)}, u32[]{:S(2)}) collective-permute-start(bf16[5,256,384]{2,1,0:T(8,128)(2,1)S(1)} %copy-done.3), channel_id=1, source_target_pairs={{0,16},{8,24},{16,0},{24,8},{1,17},{9,25},{17,1},{25,9},{2,18},{10... | collective-permute-start | bytes 2949128 | tf_op jit(solution)/shard_map/ppermute | solution.py:19
  37.6 26.6 %collective-permute-start.4 = (bf16[5,256,384]{2,1,0:T(8,128)(2,1)S(1)}, bf16[5,256,384]{2,1,0:T(8,128)(2,1)}, u32[]{:S(2)}, u32[]{:S(2)}) collective-permute-start(bf16[5,256,384]{2,1,0:T(8,128)(2,1)S(1)} %copy-done.3), channel_id=1, source_target_pairs={{0,8},{8,0},{16,24},{24,16},{1,9},{9,1},{17,25},{25,17},{2,10},{10... | collective-permute-start | bytes 2949128 | tf_op jit(solution)/shard_map/ppermute | solution.py:19
  59.8 17.9 %collective-permute-start.5 = (bf16[5,256,384]{2,1,0:T(8,128)(2,1)}, bf16[5,256,384]{2,1,0:T(8,128)(2,1)}, u32[]{:S(2)}, u32[]{:S(2)}) collective-permute-start(bf16[5,256,384]{2,1,0:T(8,128)(2,1)} %collective-permute-done.1.refs_7_), channel_id=1, source_target_pairs={{0,8},{8,0},{16,24},{24,16},{1,9},{9,1},{17,25},{25,17},{2,10},{10... | collective-permute-start | bytes 2949128 | tf_op jit(solution)/shard_map/ppermute | solution.py:19
  59.8 6.6 %collective-permute-start.6 = (s32[8]{0:T(128)S(1)}, s32[8]{0:T(128)S(1)}, u32[]{:S(2)}, u32[]{:S(2)}) collective-permute-start(s32[8]{0:T(128)S(1)} %copy-done.7), channel_id=1, source_target_pairs={{0,2},{1,3},{2,0},{3,1},{4,6},{5,7},{6,4},{7,5},{8,10},{9,11},{10,... | collective-permute-start | bytes 104 | tf_op jit(solution)/shard_map/ppermute | solution.py:19
  61.5 16.2 %collective-permute-start.7 = (s32[8]{0:T(128)S(1)}, s32[8]{0:T(128)S(1)}, u32[]{:S(2)}, u32[]{:S(2)}) collective-permute-start(s32[8]{0:T(128)S(1)} %copy-done.7), channel_id=1, source_target_pairs={{0,4},{1,5},{2,6},{3,7},{4,0},{5,1},{6,2},{7,3},{8,12},{9,13},{10,... | collective-permute-start | bytes 104 | tf_op jit(solution)/shard_map/ppermute | solution.py:19
  63.8 13.8 %collective-permute-start.8 = (s32[8]{0:T(128)S(1)}, s32[8]{0:T(128)S(1)}, u32[]{:S(2)}, u32[]{:S(2)}) collective-permute-start(s32[8]{0:T(128)S(1)} %copy-done.7), channel_id=1, source_target_pairs={{0,6},{1,7},{2,4},{3,5},{4,2},{5,3},{6,0},{7,1},{8,14},{9,15},{10,... | collective-permute-start | bytes 104 | tf_op jit(solution)/shard_map/ppermute | solution.py:19
  66.4 11.3 %copy-start.8 = (s32[8]{0:T(128)}, s32[8]{0:T(128)S(1)}, u32[]{:S(2)}) copy-start(s32[8]{0:T(128)S(1)} %collective-permute-done.6.refs_9_) | copy-start | bytes 100
  77.7 0.5 copy-start.9
  77.7 0.5 copy-start.10
  88.7 1.2 copy-start
  89.9 63.1 %all-to-all-start.3 = ((bf16[8,2,48,1408]{3,2,1,0:T(8,128)(2,1)}), bf16[8,2,48,1408]{3,2,1,0:T(8,128)(2,1)S(1)}, u32[]{:S(2)}, u32[]{:S(2)}) async-start(bf16[8,2,48,1408]{3,2,1,0:T(8,128)(2,1)} %get-tuple-element.89), calls=%async_computation.3 | async-start | bytes 4325376 | tf_op jit(solution)/shard_map/all_to_all | solution.py:526
  99.9 39.5 %copy-start.11 = (s32[32]{0:T(128)S(1)}, s32[32]{0:T(128)}, u32[]{:S(2)}) copy-start(s32[32]{0:T(128)} %get-tuple-element.92.refs_0_) | copy-start | bytes 388
  109.0 21.1 %collective-permute-start.10 = (bf16[4,2,48,512]{3,2,1,0:T(8,128)(2,1)S(1)}, bf16[4,2,48,512]{3,2,1,0:T(8,128)(2,1)}, u32[]{:S(2)}, u32[]{:S(2)}) collective-permute-start(bf16[4,2,48,512]{3,2,1,0:T(8,128)(2,1)S(1)} %dynamic-slice_bitcast_fusion), channel_id=1, source_target_pairs={{0,1},{1,0},{2,3},{3,2},{4,5},{5,4},{6,7},{7,6},{8,9},{9,8},{10,11... | collective-permute-start | bytes 1179656 | tf_op jit(solution)/shard_map/ppermute | solution.py:19
  132.1 14.5 %collective-permute-start.11 = (bf16[2,48,512]{2,1,0:T(8,128)(2,1)}, bf16[2,48,512]{2,1,0:T(8,128)(2,1)S(1)}, u32[]{:S(2)}, u32[]{:S(2)}) collective-permute-start(bf16[2,48,512]{2,1,0:T(8,128)(2,1)} %get-tuple-element.99), channel_id=1, source_target_pairs={{0,2},{1,3},{2,0},{3,1},{4,6},{5,7},{6,4},{7,5},{8,10},{9,11},{10,... | collective-permute-start | bytes 294920 | tf_op jit(solution)/shard_map/ppermute | solution.py:19
  132.1 19.4 %collective-permute-start.12 = (bf16[2,48,512]{2,1,0:T(8,128)(2,1)}, bf16[2,48,512]{2,1,0:T(8,128)(2,1)S(1)}, u32[]{:S(2)}, u32[]{:S(2)}) collective-permute-start(bf16[2,48,512]{2,1,0:T(8,128)(2,1)} %get-tuple-element.101), channel_id=1, source_target_pairs={{0,4},{1,5},{2,6},{3,7},{4,0},{5,1},{6,2},{7,3},{8,12},{9,13},{10,... | collective-permute-start | bytes 294920 | tf_op jit(solution)/shard_map/ppermute | solution.py:19
  139.4 12.0 %collective-permute-start.13 = (bf16[2,48,512]{2,1,0:T(8,128)(2,1)}, bf16[2,48,512]{2,1,0:T(8,128)(2,1)}, u32[]{:S(2)}, u32[]{:S(2)}) collective-permute-start(bf16[2,48,512]{2,1,0:T(8,128)(2,1)} %get-tuple-element.100), channel_id=1, source_target_pairs={{0,6},{1,7},{2,4},{3,5},{4,2},{5,3},{6,0},{7,1},{8,14},{9,15},{10,... | collective-permute-start | bytes 294920 | tf_op jit(solution)/shard_map/ppermute | solution.py:19
  139.4 3.6 %collective-permute-start.9 = (s32[32]{0:T(128)S(1)}, s32[32]{0:T(128)}, u32[]{:S(2)}, u32[]{:S(2)}) collective-permute-start(s32[32]{0:T(128)S(1)} %copy-done.11), channel_id=1, source_target_pairs={{0,1},{1,0},{2,3},{3,2},{4,5},{5,4},{6,7},{7,6},{8,9},{9,8},{10,11... | collective-permute-start | bytes 392 | tf_op jit(solution)/shard_map/ppermute | solution.py:19

commit v7 on v6

--- a/solution.py
+++ b/solution.py
@@ -242,18 +242,10 @@
     order_ref, source_counts_ref, offsets_ref, test_counts_ref, left_ref = refs[:5]
     shard_refs = refs[5 : 5 + nshard]
     j = pl.program_id(0)
-    if not packed:
+    if packed:
+        tile_ref, main_ref, over_ref, pack_ref = refs[5 + nshard :]
+    else:
         (tile_ref,) = refs[5 + nshard :]
-    else:
-        *far_refs, tile_ref, main_ref, over_ref, joined_ref, pack_ref = refs[5 + nshard :]
-
-        @pl.when(j == 0)
-        def _():
-            nblock = source_counts_ref.shape[0]
-            for place, far_ref in enumerate([source_counts_ref] + far_refs):
-                for k in range(nblock):
-                    joined_ref[place * nblock + k] = far_ref[k]
-
     ntest, _, kmax, _ = left_ref.shape
     ndest, _, _, rows, width = tile_ref.shape
     count = source_counts_ref[order_ref[first + j]]
@@ -311,7 +303,7 @@
             over_ref[...] = pack_ref[:, :, :, main : main + over_ref.shape[3]]
 
 
-def tiles(ndest, first, tables, test_counts, left, shards, main, far=()):
+def tiles(ndest, first, tables, test_counts, left, shards, main):
     ntest, nsource, kmax, nq = left.shape
     nshard = len(shards)
     part, width = shards[0].shape[1:]
@@ -326,16 +318,13 @@
             shapes.append(jax.ShapeDtypeStruct(shape, jnp.bfloat16))
             specs.append(pl.BlockSpec(shape, lambda j, *_: (0, 0, 0, 0)))
         scratch.append(pltpu.VMEM((ndest, ntest, rows, nsource * width + LANES), jnp.bfloat16))
-        shapes.append(jax.ShapeDtypeStruct(((1 + len(far)) * tables[1].shape[0],), jnp.int32))
-        specs.append(pl.BlockSpec(memory_space=pltpu.SMEM))
     return pl.pallas_call(
         functools.partial(tile_kernel, nshard, first, packed),
         grid_spec=pltpu.PrefetchScalarGridSpec(
             num_scalar_prefetch=4,
             grid=(nsource,),
             in_specs=[pl.BlockSpec((ntest, 1, kmax, nq), lambda j, *_: (0, j, 0, 0))]
-            + [pl.BlockSpec((1, part, width), lambda j, *_: (j, 0, 0))] * nshard
-            + [pl.BlockSpec(memory_space=pltpu.SMEM)] * len(far),
+            + [pl.BlockSpec((1, part, width), lambda j, *_: (j, 0, 0))] * nshard,
             out_specs=specs,
             scratch_shapes=scratch,
         ),
@@ -346,11 +335,14 @@
             bytes_accessed=2 * ntest * nsource * kmax * (nq + width),
             transcendentals=0,
         ),
-    )(*tables, test_counts, left, *shards, *far)
-
-
-def project_kernel(order_ref, tile_ref, coeff_ref, *refs):
-    *start_refs, sum_ref, total_ref = refs
+    )(*tables, test_counts, left, *shards)
+
+
+def project_kernel(started, order_ref, tile_ref, coeff_ref, *refs):
+    if started:
+        start_ref, sum_ref, total_ref = refs
+    else:
+        *counts_refs, sum_ref, joined_ref, total_ref = refs
     j = pl.program_id(0)
     ndest, ntest, _, rows, _ = tile_ref.shape
     whole = [tile_ref[dest, i, 0] for i in range(ntest) for dest in range(ndest)]
@@ -358,7 +350,7 @@
 
     @pl.when(j == 0)
     def _():
-        total_ref[...] = term + start_refs[0][...] if start_refs else term
+        total_ref[...] = term + start_ref[...] if started else term
 
     @pl.when(j > 0)
     def _():
@@ -366,8 +358,12 @@
 
     @pl.when(j == pl.num_programs(0) - 1)
     def _():
-        if not start_refs:
+        if not started:
             sum_ref[...] = total_ref[...]
+            nblock = counts_refs[0].shape[0]
+            for place, counts_ref in enumerate(counts_refs):
+                for k in range(nblock):
+                    joined_ref[place * nblock + k] = counts_ref[k]
             return
         for i in range(ntest):
             for dest in range(ndest):
@@ -375,20 +371,25 @@
                 sum_ref[dest, i] = total_ref[top : top + rows, :].astype(sum_ref.dtype)
 
 
-def project(order, first, tiles, coefficients, start):
+def project(order, first, tiles, coefficients, start=None, counts=()):
     ndest, ntest, nsource, rows, width = tiles.shape
     ncol = coefficients.shape[2]
+    smem = pl.BlockSpec(memory_space=pltpu.SMEM)
     total_spec = pl.BlockSpec((ntest * ndest * rows, ncol), lambda j, order: (0, 0))
-    if start is None:
-        started = []
-        sum_spec = total_spec
-        sum_shape = jax.ShapeDtypeStruct((ntest * ndest * rows, ncol), jnp.float32)
+    started = start is not None
+    if started:
+        more, more_specs = [start], [total_spec]
+        out_specs = pl.BlockSpec((ndest, ntest, rows, ncol), lambda j, order: (0, 0, 0, 0))
+        out_shape = jax.ShapeDtypeStruct((ndest, ntest, rows, ncol), jnp.bfloat16)
     else:
-        started = [start]
-        sum_spec = pl.BlockSpec((ndest, ntest, rows, ncol), lambda j, order: (0, 0, 0, 0))
-        sum_shape = jax.ShapeDtypeStruct((ndest, ntest, rows, ncol), jnp.bfloat16)
+        more, more_specs = list(counts), [smem] * len(counts)
+        out_specs = (total_spec, smem)
+        out_shape = (
+            jax.ShapeDtypeStruct((ntest * ndest * rows, ncol), jnp.float32),
+            jax.ShapeDtypeStruct((sum(part.shape[0] for part in counts),), jnp.int32),
+        )
     return pl.pallas_call(
-        project_kernel,
+        functools.partial(project_kernel, started),
         grid_spec=pltpu.PrefetchScalarGridSpec(
             num_scalar_prefetch=1,
             grid=(nsource,),
@@ -396,18 +397,18 @@
                 pl.BlockSpec((ndest, ntest, 1, rows, width), lambda j, order: (0, 0, j, 0, 0)),
                 pl.BlockSpec((1, width, ncol), lambda j, order: (order[first + j], 0, 0)),
             ]
-            + [total_spec] * len(started),
-            out_specs=sum_spec,
+            + more_specs,
+            out_specs=out_specs,
             scratch_shapes=[pltpu.VMEM((ntest * ndest * rows, ncol), jnp.float32)],
         ),
-        out_shape=sum_shape,
+        out_shape=out_shape,
         compiler_params=pltpu.CompilerParams(vmem_limit_bytes=VMEM_LIMIT),
         cost_estimate=pl.CostEstimate(
             flops=2 * ndest * ntest * rows * width * ncol * nsource,
             bytes_accessed=2 * ndest * ntest * rows * width * nsource,
             transcendentals=0,
         ),
-    )(order, tiles, coefficients, *started)
+    )(order, tiles, coefficients, *more)
 
 
 def unpack_kernel(cut, order_ref, counts_ref, offsets_ref, whole_ref, packed_ref, out_ref, rows_ref):
@@ -520,14 +521,12 @@
     inner = max(1, nsrc // 4)
     counts, _ = lax.optimization_barrier((source_counts, left_b))
     far = [exchange(counts, "src", flip) for flip in range(inner, nsrc, inner)]
-    tiles_b, packed, beyond, joined = tiles(
-        nsrc, cut, tables, test_counts, left_b, shards_b, main, far
-    )
+    tiles_b, packed, beyond = tiles(nsrc, cut, tables, test_counts, left_b, shards_b, main)
+    packed, *far = lax.optimization_barrier((packed, *far))
     moved_b = lax.all_to_all(packed, "src", split_axis=0, concat_axis=0, tiled=True)
 
-    joined, _ = lax.optimization_barrier((joined, packed))
+    sums, joined = project(order, 0, tiles_a, coefficients, counts=[source_counts] + far)
     groups = [joined] + [exchange(joined, "src", flip) for flip in range(1, inner)]
-    sums = project(order, 0, tiles_a, coefficients, None)
     sums = project(order, cut, tiles_b, coefficients, sums)
     projected = sum_rows(sums, "src")
     me_src, _ = lax.optimization_barrier((jnp.reshape(lax.axis_index("src"), (1,)), packed))

time: 161 us -> 150 us (0.932)
  waiting for transfers between devices: 45.2 us -> 34.5 us
    ppermute x14, waiting for transfers between devices: 45.2 us -> 34.5 us  [exchange(): return lax.ppermute(x, axis, [(a, a ^ flip) for a in range(size)])]
  transfers between devices with their start and end apart: 16 -> 16, of which waited for: 8 -> 7; matrix products, arithmetic and copies ran while one was open for 3% -> 3% of each run, Pallas kernels for 37% -> 41%
where the time goes in v7:
time: 150 us; the launch traced here: 149 us
  Pallas kernels  77.8 us (52%)
  waiting for transfers between devices  34.5 us (23%)
  starting transfers between devices  28.6 us (19%)
  local copies, waits for them, and re-layouts  3.81 us (3%)
  other arithmetic  2.8 us (2%)
    ppermute x14, waiting for transfers between devices, exchange(): return lax.ppermute(x, axis, [(a, a ^ flip) for a in range(size)])  34.5 us
    pallas_call x2, Pallas kernels, left_products(): pl.pallas_call(functools.partial(left_kernel, nshard, first), grid_spec=p...  33.2 us
    ppermute x14, starting transfers between devices, exchange(): return lax.ppermute(x, axis, [(a, a ^ flip) for a in range(size)])  18.7 us
    pallas_call x2, Pallas kernels, tiles(): pl.pallas_call(functools.partial(tile_kernel, nshard, first, packed), gri...  17.6 us
    pallas_call x2, Pallas kernels, project(): pl.pallas_call(functools.partial(project_kernel, started), grid_spec=pltp...  13.7 us
    pallas_call x1, Pallas kernels, unpack(): pl.pallas_call(functools.partial(unpack_kernel, cut), grid_spec=pltpu.Pre...  7.58 us
    all_to_all x1, starting transfers between devices, body(): lax.all_to_all(tiles_a, 'src', split_axis=0, concat_axis=0, tiled=True)  6.09 us
    all_to_all x1, starting transfers between devices, body(): lax.all_to_all(packed, 'src', split_axis=0, concat_axis=0, tiled=True)  3.79 us
  transfers between devices with their start and end apart: 16, of which 7 were waited for; matrix products, arithmetic and copies ran while one was open for 3% of the time, Pallas kernels for 41%

profile of v7, /device:TPU:0, one launch (start us, length us, event | category | flops | bytes accessed | tf_op | source)
XLA Modules:
  0.0 148.9 jit_solution(12917812907242114331)
XLA Ops:
  0.6 2.9 %shard_map.86 = (s32[8]{0:T(128)}, s32[8]{0:T(128)}, bf16[3,256,384]{2,1,0:T(8,128)(2,1)}, bf16[5,256,384]{2,1,0:T(8,128)(2,1)}) custom-call(s32[8]{0:T(128)} %refs_0_.1, bf16[8,256,384]{2,1,0:T(8,128)(2,1)} %basis_ref.3), custom_call_target="tpu_custom_call" | custom-call | tf_op jit(solution)/shard_map/pallas_call | solution.py:85
  3.5 3.0 %collective-permute-start = (bf16[3,256,384]{2,1,0:T(8,128)(2,1)}, bf16[3,256,384]{2,1,0:T(8,128)(2,1)S(1)}, u32[]{:S(2)}, u32[]{:S(2)}) collective-permute-start(bf16[3,256,384]{2,1,0:T(8,128)(2,1)} %get-tuple-element.85.refs_5_), channel_id=1, source_target_pairs={{0,16},{8,24},{16,0},{24,8},{1,17},{9,25},{17,1},{25,9},{2,18},{10... | collective-permute-start | bytes 1769480 | tf_op jit(solution)/shard_map/ppermute | solution.py:19
  6.6 0.0 collective-permute-start.2
  6.6 13.5 %shard_map.87.refs_4_ = bf16[2,3,384,1024]{3,2,1,0:T(8,128)(2,1)} custom-call(s32[1]{0:T(128)} %bitcast.1.me_ref, s32[8]{0:T(128)} %get-tuple-element.82.order_ref.refs_0_, f32[3,2,1024]{2,1,0:T(2,128)} %bitcast.26, f32[3,8,1024]{2,1,0:T(8,128)} %bitcast.24, bf16[2,1024,384]{2,1,0:T(8,128)(2,1)} %basis_ref.5), custom_call_target="tpu_custom_call" | custom-call | flops 4831838208 | bytes 4718592 | tf_op jit(solution)/shard_map/pallas_call | solution.py:213
  20.0 0.1 collective-permute-done.refs_7_
  20.1 0.4 collective-permute-start.3
  20.5 0.0 collective-permute-done.2.refs_6_
  20.5 1.6 %collective-permute-done.3.refs_8_ = bf16[3,256,384]{2,1,0:T(8,128)(2,1)S(1)} collective-permute-done((bf16[3,256,384]{2,1,0:T(8,128)(2,1)S(1)}, bf16[3,256,384]{2,1,0:T(8,128)(2,1)S(1)}, u32[]{:S(2)}, u32[]{:S(2)}) %collective-permute-start.3) | collective-permute-done | bytes 589856 | tf_op jit(solution)/shard_map/ppermute | solution.py:19
  22.2 0.8 copy-done.6
  23.0 6.9 %shard_map.88.tile_ref = bf16[8,2,3,48,384]{4,3,2,1,0:T(8,128)(2,1)} custom-call(s32[8]{0:T(128)} %get-tuple-element.82.order_ref.refs_0_, s32[8]{0:T(128)} %refs_0_.1, s32[8]{0:T(128)} %get-tuple-element.83.refs_2_, s32[2]{0:T(128)} %refs_3_.3, bf16[2,3,384,1024]{3,2,1,0:T(8,128)(2,1)} %shard_map.87.refs_4_, ...), custom_call_target="tpu_custom_call" | custom-call | flops 1811939328 | bytes 6488064 | tf_op jit(solution)/shard_map/pallas_call | solution.py:321
  29.9 6.1 %all-to-all-start.2 = ((bf16[8,2,3,48,384]{4,3,2,1,0:T(8,128)(2,1)}), bf16[8,2,3,48,384]{4,3,2,1,0:T(8,128)(2,1)S(1)}, u32[]{:S(2)}, u32[]{:S(2)}) async-start(bf16[8,2,3,48,384]{4,3,2,1,0:T(8,128)(2,1)} %shard_map.88.tile_ref), calls=%async_computation.2 | async-start | bytes 3538944 | tf_op jit(solution)/shard_map/all_to_all | solution.py:515
  36.0 0.0 copy-start.7
  36.0 1.6 %collective-permute-start.1 = (bf16[5,256,384]{2,1,0:T(8,128)(2,1)S(1)}, bf16[5,256,384]{2,1,0:T(8,128)(2,1)}, u32[]{:S(2)}, u32[]{:S(2)}) collective-permute-start(bf16[5,256,384]{2,1,0:T(8,128)(2,1)S(1)} %copy-done.3), channel_id=1, source_target_pairs={{0,16},{8,24},{16,0},{24,8},{1,17},{9,25},{17,1},{25,9},{2,18},{10... | collective-permute-start | bytes 2949128 | tf_op jit(solution)/shard_map/ppermute | solution.py:19
  37.6 0.0 collective-permute-start.4
  37.6 19.7 %shard_map.89.refs_4_ = bf16[2,5,384,1024]{3,2,1,0:T(8,128)(2,1)} custom-call(s32[1]{0:T(128)} %bitcast.1.me_ref, s32[8]{0:T(128)} %get-tuple-element.82.order_ref.refs_0_, f32[3,2,1024]{2,1,0:T(2,128)} %bitcast.27, f32[3,8,1024]{2,1,0:T(8,128)} %bitcast.25, bf16[2,1024,384]{2,1,0:T(8,128)(2,1)} %basis_ref.5), custom_call_target="tpu_custom_call" | custom-call | flops 8053063680 | bytes 7864320 | tf_op jit(solution)/shard_map/pallas_call | solution.py:213
  57.3 2.4 %collective-permute-done.1.refs_7_ = bf16[5,256,384]{2,1,0:T(8,128)(2,1)} collective-permute-done((bf16[5,256,384]{2,1,0:T(8,128)(2,1)S(1)}, bf16[5,256,384]{2,1,0:T(8,128)(2,1)}, u32[]{:S(2)}, u32[]{:S(2)}) %collective-permute-start.1) | collective-permute-done | bytes 983072 | tf_op jit(solution)/shard_map/ppermute | solution.py:19
  59.7 0.0 collective-permute-start.5
  59.7 1.7 %collective-permute-start.6 = (s32[8]{0:T(128)S(1)}, s32[8]{0:T(128)S(1)}, u32[]{:S(2)}, u32[]{:S(2)}) collective-permute-start(s32[8]{0:T(128)S(1)} %copy-done.7), channel_id=1, source_target_pairs={{0,2},{1,3},{2,0},{3,1},{4,6},{5,7},{6,4},{7,5},{8,10},{9,11},{10,... | collective-permute-start | bytes 104 | tf_op jit(solution)/shard_map/ppermute | solution.py:19
  61.5 2.4 %collective-permute-start.7 = (s32[8]{0:T(128)S(1)}, s32[8]{0:T(128)S(1)}, u32[]{:S(2)}, u32[]{:S(2)}) collective-permute-start(s32[8]{0:T(128)S(1)} %copy-done.7), channel_id=1, source_target_pairs={{0,4},{1,5},{2,6},{3,7},{4,0},{5,1},{6,2},{7,3},{8,12},{9,13},{10,... | collective-permute-start | bytes 104 | tf_op jit(solution)/shard_map/ppermute | solution.py:19
  63.8 0.3 collective-permute-start.8
  64.1 0.0 collective-permute-done.4.refs_6_
  64.1 10.8 %shard_map.90 = (bf16[8,2,5,48,384]{4,3,2,1,0:T(8,128)(2,1)}, bf16[8,2,48,1408]{3,2,1,0:T(8,128)(2,1)}, bf16[8,2,48,512]{3,2,1,0:T(8,128)(2,1)S(1)}) custom-call(s32[8]{0:T(128)} %get-tuple-element.82.order_ref.refs_0_, s32[8]{0:T(128)} %refs_0_.1, s32[8]{0:T(128)} %get-tuple-element.83.refs_2_, s32[2]{0:T(128)} %refs_3_.3, ...), custom_call_target="tpu_custom_call" | custom-call | flops 3019898880 | bytes 10813440 | tf_op jit(solution)/shard_map/pallas_call | solution.py:321
  74.9 0.0 collective-permute-done.6.refs_1_
  74.9 2.7 %collective-permute-done.7.refs_2_ = s32[8]{0:T(128)S(1)} collective-permute-done((s32[8]{0:T(128)S(1)}, s32[8]{0:T(128)S(1)}, u32[]{:S(2)}, u32[]{:S(2)}) %collective-permute-start.7) | collective-permute-done | bytes 64 | tf_op jit(solution)/shard_map/ppermute | solution.py:19
  77.6 0.0 collective-permute-done.8.refs_3_
  77.6 0.0 all-to-all-done.2
  77.7 1.2 copy-done
  78.9 3.8 %all-to-all-start.3 = ((bf16[8,2,48,1408]{3,2,1,0:T(8,128)(2,1)}), bf16[8,2,48,1408]{3,2,1,0:T(8,128)(2,1)S(1)}, u32[]{:S(2)}, u32[]{:S(2)}) async-start(bf16[8,2,48,1408]{3,2,1,0:T(8,128)(2,1)} %get-tuple-element.94), calls=%async_computation.3 | async-start | bytes 4325376 | tf_op jit(solution)/shard_map/all_to_all | solution.py:526
  82.7 5.7 %shard_map.91 = (f32[768,512]{1,0:T(8,128)}, s32[32]{0:T(128)}) custom-call(s32[8]{0:T(128)} %get-tuple-element.82.order_ref.refs_0_, bf16[8,2,3,48,384]{4,3,2,1,0:T(8,128)(2,1)} %shard_map.88.tile_ref, bf16[8,384,512]{2,1,0:T(8,128)(2,1)} %coeff_ref.3, s32[8]{0:T(128)} %refs_0_.1, s32[8]{0:T(128)} %copy-done.8, s32[8]{0:T(128)} %copy-done.9, s32[8]{0:T(128)} %copy-done.10), custom_call_target="tpu_custom_call" | custom-call | flops 905969664 | bytes 1769472 | tf_op jit(solution)/shard_map/pallas_call | solution.py:391
  88.5 8.0 %shard_map.93 = bf16[8,2,48,512]{3,2,1,0:T(8,128)(2,1)} custom-call(s32[8]{0:T(128)} %get-tuple-element.82.order_ref.refs_0_, bf16[8,2,5,48,384]{4,3,2,1,0:T(8,128)(2,1)} %get-tuple-element.105.tile_ref, bf16[8,384,512]{2,1,0:T(8,128)(2,1)} %coeff_ref.3, f32[768,512]{1,0:T(8,128)} %get-tuple-element.106.refs_0_), custom_call_target="tpu_custom_call" | custom-call | flops 1509949440 | bytes 2949120 | tf_op jit(solution)/shard_map/pallas_call | solution.py:391
  96.4 1.0 dynamic-slice_bitcast_fusion
  97.5 1.9 %collective-permute-start.10 = (bf16[4,2,48,512]{3,2,1,0:T(8,128)(2,1)S(1)}, bf16[4,2,48,512]{3,2,1,0:T(8,128)(2,1)}, u32[]{:S(2)}, u32[]{:S(2)}) collective-permute-start(bf16[4,2,48,512]{3,2,1,0:T(8,128)(2,1)S(1)} %dynamic-slice_bitcast_fusion), channel_id=1, source_target_pairs={{0,1},{1,0},{2,3},{3,2},{4,5},{5,4},{6,7},{7,6},{8,9},{9,8},{10,11... | collective-permute-start | bytes 1179656 | tf_op jit(solution)/shard_map/ppermute | solution.py:19
  99.4 19.0 %collective-permute-done.10 = bf16[4,2,48,512]{3,2,1,0:T(8,128)(2,1)} collective-permute-done((bf16[4,2,48,512]{3,2,1,0:T(8,128)(2,1)S(1)}, bf16[4,2,48,512]{3,2,1,0:T(8,128)(2,1)}, u32[]{:S(2)}, u32[]{:S(2)}) %collective-permute-start.10) | collective-permute-done | bytes 393248 | tf_op jit(solution)/shard_map/ppermute | solution.py:19
  118.4 1.2 fusion
  119.6 0.7 dynamic-slice_bitcast_fusion.3
  120.3 0.0 collective-permute-start.11
  120.3 7.3 %collective-permute-start.12 = (bf16[2,48,512]{2,1,0:T(8,128)(2,1)}, bf16[2,48,512]{2,1,0:T(8,128)(2,1)S(1)}, u32[]{:S(2)}, u32[]{:S(2)}) collective-permute-start(bf16[2,48,512]{2,1,0:T(8,128)(2,1)} %get-tuple-element.109), channel_id=1, source_target_pairs={{0,4},{1,5},{2,6},{3,7},{4,0},{5,1},{6,2},{7,3},{8,12},{9,13},{10,... | collective-permute-start | bytes 294920 | tf_op jit(solution)/shard_map/ppermute | solution.py:19
  127.7 0.0 collective-permute-start.13
  127.7 0.0 collective-permute-start.9
  127.7 3.5 %collective-permute-done.9.refs_1_ = s32[32]{0:T(128)} collective-permute-done((s32[32]{0:T(128)S(1)}, s32[32]{0:T(128)}, u32[]{:S(2)}, u32[]{:S(2)}) %collective-permute-start.9) | collective-permute-done | bytes 160 | tf_op jit(solution)/shard_map/ppermute | solution.py:19
  131.2 2.8 %shard_map.92 = (s32[64]{0:T(128)S(1)}, s32[64]{0:T(128)S(1)}, s32[64]{0:T(128)S(1)}, s32[1]{0:T(128)}) custom-call(s32[1]{0:T(128)} %bitcast.me_ref, s32[32]{0:T(128)} %get-tuple-element.99.refs_0_, s32[32]{0:T(128)} %collective-permute-done.9.refs_1_), custom_call_target="tpu_custom_call" | custom-call | tf_op jit(solution)/shard_map/pallas_call | solution.py:131
  134.6 0.0 collective-permute-done.11
  134.6 5.1 %collective-permute-done.12 = bf16[2,48,512]{2,1,0:T(8,128)(2,1)S(1)} collective-permute-done((bf16[2,48,512]{2,1,0:T(8,128)(2,1)}, bf16[2,48,512]{2,1,0:T(8,128)(2,1)S(1)}, u32[]{:S(2)}, u32[]{:S(2)}) %collective-permute-start.12) | collective-permute-done | bytes 98336 | tf_op jit(solution)/shard_map/ppermute | solution.py:19
  139.7 0.0 collective-permute-done.13
  139.7 1.6 %fusion.3 = bf16[2,48,512]{2,1,0:T(8,128)(2,1)} fusion(bf16[2,48,512]{2,1,0:T(8,128)(2,1)} %collective-permute-done.13, bf16[2,48,512]{2,1,0:T(8,128)(2,1)S(1)} %collective-permute-done.12, bf16[2,48,512]{2,1,0:T(8,128)(2,1)S(1)} %collective-permute-done.11, bf16[4,2,48,512]{3,2,1,0:T(8,128)(2,1)S(1)} %fusion, s32[]{:T(128)S(6)} %select_n.36), kind=kLoop, calls=%fused_computation.8 | loop fusion | flops 393216 | bytes 491524 | tf_op jit(solution)/shard_map/convert_element_type | solution.py:46
  141.3 0.0 all-to-all-done.3
  141.3 7.6 %conditional.1 = (bf16[2,48,64,384]{3,2,1,0:T(8,128)(2,1)}) conditional(s32[]{:T(128)} %bitcast.4, (s32[64]{0:T(128)S(1)}, s32[64]{0:T(128)S(1)}, s32[64]{0:T(128)S(1)}, bf16[8,2,3,48,384]{4,3,2,1,0:T(8,128)(2,1)}, bf16[8,2,48,1408]{3,2,1,0:T(8,128)(2,1)S(1)}) %tuple.39, (bf16[8,2,48,512]{3,2,1,0:T(8,128)(2,1)S(1)}, ...), branch_computations={%region_0.1_spmd, %region_1.2_spmd, %region_2.3_spmd} | conditional | flops 5898240 | bytes 14549028 | solution.py:544
  141.3 7.6 %branch_0_fun.1 = bf16[2,48,64,384]{3,2,1,0:T(8,128)(2,1)} custom-call(s32[64]{0:T(128)S(1)} %get-tuple-element.26.order_ref, s32[64]{0:T(128)S(1)} %get-tuple-element.27.counts_ref, s32[64]{0:T(128)S(1)} %get-tuple-element.40.offsets_ref, bf16[8,2,3,48,384]{4,3,2,1,0:T(8,128)(2,1)} %get-tuple-element.41.whole_ref, ...), custom_call_target="tpu_custom_call" | custom-call | tf_op jit(solution)/shard_map/cond/branch_0_fun/pallas_call | solution.py:459
  (18 shorter events, 0.0 us)
Async XLA Ops:
  3.5 16.6 %collective-permute-start = (bf16[3,256,384]{2,1,0:T(8,128)(2,1)}, bf16[3,256,384]{2,1,0:T(8,128)(2,1)S(1)}, u32[]{:S(2)}, u32[]{:S(2)}) collective-permute-start(bf16[3,256,384]{2,1,0:T(8,128)(2,1)} %get-tuple-element.85.refs_5_), channel_id=1, source_target_pairs={{0,16},{8,24},{16,0},{24,8},{1,17},{9,25},{17,1},{25,9},{2,18},{10... | collective-permute-start | bytes 1769480 | tf_op jit(solution)/shard_map/ppermute | solution.py:19
  6.6 14.0 %collective-permute-start.2 = (bf16[3,256,384]{2,1,0:T(8,128)(2,1)}, bf16[3,256,384]{2,1,0:T(8,128)(2,1)S(1)}, u32[]{:S(2)}, u32[]{:S(2)}) collective-permute-start(bf16[3,256,384]{2,1,0:T(8,128)(2,1)} %get-tuple-element.85.refs_5_), channel_id=1, source_target_pairs={{0,8},{8,0},{16,24},{24,16},{1,9},{9,1},{17,25},{25,17},{2,10},{10... | collective-permute-start | bytes 1769480 | tf_op jit(solution)/shard_map/ppermute | solution.py:19
  20.1 2.1 %copy-start.4 = (bf16[3,256,384]{2,1,0:T(8,128)(2,1)}, bf16[3,256,384]{2,1,0:T(8,128)(2,1)S(1)}, u32[]{:S(2)}) copy-start(bf16[3,256,384]{2,1,0:T(8,128)(2,1)S(1)} %collective-permute-done.refs_7_) | copy-start | bytes 1769476
  20.1 2.1 %collective-permute-start.3 = (bf16[3,256,384]{2,1,0:T(8,128)(2,1)S(1)}, bf16[3,256,384]{2,1,0:T(8,128)(2,1)S(1)}, u32[]{:S(2)}, u32[]{:S(2)}) collective-permute-start(bf16[3,256,384]{2,1,0:T(8,128)(2,1)S(1)} %collective-permute-done.refs_7_), channel_id=1, source_target_pairs={{0,8},{8,0},{16,24},{24,16},{1,9},{9,1},{17,25},{25,17},{2,10},{10... | collective-permute-start | bytes 1769480 | tf_op jit(solution)/shard_map/ppermute | solution.py:19
  20.5 1.6 %copy-start.5 = (bf16[3,256,384]{2,1,0:T(8,128)(2,1)}, bf16[3,256,384]{2,1,0:T(8,128)(2,1)S(1)}, u32[]{:S(2)}) copy-start(bf16[3,256,384]{2,1,0:T(8,128)(2,1)S(1)} %collective-permute-done.2.refs_6_) | copy-start | bytes 1769476
  22.2 0.8 copy-start.6
  29.9 6.1 %copy-start.3 = (bf16[5,256,384]{2,1,0:T(8,128)(2,1)S(1)}, bf16[5,256,384]{2,1,0:T(8,128)(2,1)}, u32[]{:S(2)}) copy-start(bf16[5,256,384]{2,1,0:T(8,128)(2,1)} %get-tuple-element.86.refs_5_) | copy-start | bytes 2949124
  29.9 47.8 %all-to-all-start.2 = ((bf16[8,2,3,48,384]{4,3,2,1,0:T(8,128)(2,1)}), bf16[8,2,3,48,384]{4,3,2,1,0:T(8,128)(2,1)S(1)}, u32[]{:S(2)}, u32[]{:S(2)}) async-start(bf16[8,2,3,48,384]{4,3,2,1,0:T(8,128)(2,1)} %shard_map.88.tile_ref), calls=%async_computation.2 | async-start | bytes 3538944 | tf_op jit(solution)/shard_map/all_to_all | solution.py:515
  36.0 23.8 %copy-start.7 = (s32[8]{0:T(128)S(1)}, s32[8]{0:T(128)}, u32[]{:S(2)}) copy-start(s32[8]{0:T(128)} %refs_0_.1) | copy-start | bytes 100
  36.0 23.8 %collective-permute-start.1 = (bf16[5,256,384]{2,1,0:T(8,128)(2,1)S(1)}, bf16[5,256,384]{2,1,0:T(8,128)(2,1)}, u32[]{:S(2)}, u32[]{:S(2)}) collective-permute-start(bf16[5,256,384]{2,1,0:T(8,128)(2,1)S(1)} %copy-done.3), channel_id=1, source_target_pairs={{0,16},{8,24},{16,0},{24,8},{1,17},{9,25},{17,1},{25,9},{2,18},{10... | collective-permute-start | bytes 2949128 | tf_op jit(solution)/shard_map/ppermute | solution.py:19
  37.6 26.6 %collective-permute-start.4 = (bf16[5,256,384]{2,1,0:T(8,128)(2,1)S(1)}, bf16[5,256,384]{2,1,0:T(8,128)(2,1)}, u32[]{:S(2)}, u32[]{:S(2)}) collective-permute-start(bf16[5,256,384]{2,1,0:T(8,128)(2,1)S(1)} %copy-done.3), channel_id=1, source_target_pairs={{0,8},{8,0},{16,24},{24,16},{1,9},{9,1},{17,25},{25,17},{2,10},{10... | collective-permute-start | bytes 2949128 | tf_op jit(solution)/shard_map/ppermute | solution.py:19
  59.7 4.4 %collective-permute-start.5 = (bf16[5,256,384]{2,1,0:T(8,128)(2,1)}, bf16[5,256,384]{2,1,0:T(8,128)(2,1)}, u32[]{:S(2)}, u32[]{:S(2)}) collective-permute-start(bf16[5,256,384]{2,1,0:T(8,128)(2,1)} %collective-permute-done.1.refs_7_), channel_id=1, source_target_pairs={{0,8},{8,0},{16,24},{24,16},{1,9},{9,1},{17,25},{25,17},{2,10},{10... | collective-permute-start | bytes 2949128 | tf_op jit(solution)/shard_map/ppermute | solution.py:19
  59.7 15.1 %collective-permute-start.6 = (s32[8]{0:T(128)S(1)}, s32[8]{0:T(128)S(1)}, u32[]{:S(2)}, u32[]{:S(2)}) collective-permute-start(s32[8]{0:T(128)S(1)} %copy-done.7), channel_id=1, source_target_pairs={{0,2},{1,3},{2,0},{3,1},{4,6},{5,7},{6,4},{7,5},{8,10},{9,11},{10,... | collective-permute-start | bytes 104 | tf_op jit(solution)/shard_map/ppermute | solution.py:19
  61.5 16.2 %collective-permute-start.7 = (s32[8]{0:T(128)S(1)}, s32[8]{0:T(128)S(1)}, u32[]{:S(2)}, u32[]{:S(2)}) collective-permute-start(s32[8]{0:T(128)S(1)} %copy-done.7), channel_id=1, source_target_pairs={{0,4},{1,5},{2,6},{3,7},{4,0},{5,1},{6,2},{7,3},{8,12},{9,13},{10,... | collective-permute-start | bytes 104 | tf_op jit(solution)/shard_map/ppermute | solution.py:19
  63.8 13.8 %collective-permute-start.8 = (s32[8]{0:T(128)S(1)}, s32[8]{0:T(128)S(1)}, u32[]{:S(2)}, u32[]{:S(2)}) collective-permute-start(s32[8]{0:T(128)S(1)} %copy-done.7), channel_id=1, source_target_pairs={{0,6},{1,7},{2,4},{3,5},{4,2},{5,3},{6,0},{7,1},{8,14},{9,15},{10,... | collective-permute-start | bytes 104 | tf_op jit(solution)/shard_map/ppermute | solution.py:19
  74.9 7.8 %copy-start.8 = (s32[8]{0:T(128)}, s32[8]{0:T(128)S(1)}, u32[]{:S(2)}) copy-start(s32[8]{0:T(128)S(1)} %collective-permute-done.6.refs_1_) | copy-start | bytes 100
  77.6 5.1 %copy-start.9 = (s32[8]{0:T(128)}, s32[8]{0:T(128)S(1)}, u32[]{:S(2)}) copy-start(s32[8]{0:T(128)S(1)} %collective-permute-done.7.refs_2_) | copy-start | bytes 100
  77.6 5.1 %copy-start.10 = (s32[8]{0:T(128)}, s32[8]{0:T(128)S(1)}, u32[]{:S(2)}) copy-start(s32[8]{0:T(128)S(1)} %collective-permute-done.8.refs_3_) | copy-start | bytes 100
  77.7 1.2 copy-start
  78.9 62.4 %all-to-all-start.3 = ((bf16[8,2,48,1408]{3,2,1,0:T(8,128)(2,1)}), bf16[8,2,48,1408]{3,2,1,0:T(8,128)(2,1)S(1)}, u32[]{:S(2)}, u32[]{:S(2)}) async-start(bf16[8,2,48,1408]{3,2,1,0:T(8,128)(2,1)} %get-tuple-element.94), calls=%async_computation.3 | async-start | bytes 4325376 | tf_op jit(solution)/shard_map/all_to_all | solution.py:526
  88.5 39.2 %copy-start.11 = (s32[32]{0:T(128)S(1)}, s32[32]{0:T(128)}, u32[]{:S(2)}) copy-start(s32[32]{0:T(128)} %get-tuple-element.99.refs_0_) | copy-start | bytes 388
  97.5 20.9 %collective-permute-start.10 = (bf16[4,2,48,512]{3,2,1,0:T(8,128)(2,1)S(1)}, bf16[4,2,48,512]{3,2,1,0:T(8,128)(2,1)}, u32[]{:S(2)}, u32[]{:S(2)}) collective-permute-start(bf16[4,2,48,512]{3,2,1,0:T(8,128)(2,1)S(1)} %dynamic-slice_bitcast_fusion), channel_id=1, source_target_pairs={{0,1},{1,0},{2,3},{3,2},{4,5},{5,4},{6,7},{7,6},{8,9},{9,8},{10,11... | collective-permute-start | bytes 1179656 | tf_op jit(solution)/shard_map/ppermute | solution.py:19
  120.3 14.3 %collective-permute-start.11 = (bf16[2,48,512]{2,1,0:T(8,128)(2,1)}, bf16[2,48,512]{2,1,0:T(8,128)(2,1)S(1)}, u32[]{:S(2)}, u32[]{:S(2)}) collective-permute-start(bf16[2,48,512]{2,1,0:T(8,128)(2,1)} %get-tuple-element.107), channel_id=1, source_target_pairs={{0,2},{1,3},{2,0},{3,1},{4,6},{5,7},{6,4},{7,5},{8,10},{9,11},{10,... | collective-permute-start | bytes 294920 | tf_op jit(solution)/shard_map/ppermute | solution.py:19
  120.3 19.4 %collective-permute-start.12 = (bf16[2,48,512]{2,1,0:T(8,128)(2,1)}, bf16[2,48,512]{2,1,0:T(8,128)(2,1)S(1)}, u32[]{:S(2)}, u32[]{:S(2)}) collective-permute-start(bf16[2,48,512]{2,1,0:T(8,128)(2,1)} %get-tuple-element.109), channel_id=1, source_target_pairs={{0,4},{1,5},{2,6},{3,7},{4,0},{5,1},{6,2},{7,3},{8,12},{9,13},{10,... | collective-permute-start | bytes 294920 | tf_op jit(solution)/shard_map/ppermute | solution.py:19
  127.7 12.1 %collective-permute-start.13 = (bf16[2,48,512]{2,1,0:T(8,128)(2,1)}, bf16[2,48,512]{2,1,0:T(8,128)(2,1)}, u32[]{:S(2)}, u32[]{:S(2)}) collective-permute-start(bf16[2,48,512]{2,1,0:T(8,128)(2,1)} %get-tuple-element.108), channel_id=1, source_target_pairs={{0,6},{1,7},{2,4},{3,5},{4,2},{5,3},{6,0},{7,1},{8,14},{9,15},{10,... | collective-permute-start | bytes 294920 | tf_op jit(solution)/shard_map/ppermute | solution.py:19
  127.7 3.5 %collective-permute-start.9 = (s32[32]{0:T(128)S(1)}, s32[32]{0:T(128)}, u32[]{:S(2)}, u32[]{:S(2)}) collective-permute-start(s32[32]{0:T(128)S(1)} %copy-done.11), channel_id=1, source_target_pairs={{0,1},{1,0},{2,3},{3,2},{4,5},{5,4},{6,7},{7,6},{8,9},{9,8},{10,11... | collective-permute-start | bytes 392 | tf_op jit(solution)/shard_map/ppermute | solution.py:19
